TPU v7x, 128 devices: a whole 4x4x4 slice. The times are simulated.
128 devices in a mesh: inst: 8 (over z, x_lo), space: 16 (over x_hi, y, core).
Axes of the slice: x: 4 (x_hi: 2, x_lo: 2; x = x_hi * 2 + x_lo), y: 4, z: 4, core: 2. Of those that a mesh axis runs over, the one named last changes fastest.
Arguments:
- basis: float32 [8, 8, 7, 131072], P(None, 'inst', None, 'space'), may hold values from -13 to 13
- flux_adjoint: bfloat16 [8, 7, 7, 7, 131072], P('inst', None, None, None, 'space'), may hold values from -0.875 to 0.875
- recon_adjoint: bfloat16 [8, 7, 7, 7, 131072], P('inst', None, None, None, 'space'), may hold values from -0.875 to 0.875
- pseudo_time: float32 [131072], P('space'), may hold values from 0.5 to 2
- vol_omega: float32 [131072], P('space'), may hold values from 0.25 to 1
- block_ids: int32 [32], replicated, may hold values from 0 to 31, each once
- neighbour: int32 [32, 6], replicated, may hold values from -1 to 191, as said below
- orient: int32 [32, 6], replicated, may hold values from 0 to 7, as said below
Outputs:
- next_vector: float32 [8, 7, 131072], P('inst', None, 'space')
- hessenberg: float32 [9], replicated
Inputs may be any that keep to these rules, and one draw needn't show every extreme that they name: `block_ids`: a permutation of the block numbers. `neighbour`: exactly 32 faces are walls; every other face touches one different face, the pairing is mutual. `orient`: walls have 0; the codes of the two sides of a connection undo each other.
All inputs are finite; a program needn't handle non-finite values.
Results may differ from a plain program's by a relative error of at most 0.0003.
Values sent between devices are 32-bit elements; how exact they have to be, the bound alone decides.
No kernel may reach another device: no remote copies, remote signals or barrier semaphores. Data moves between devices by JAX's collectives and lax.ppermute only.
A program may use at most 128 MiB of HBM per device.

v0:
```python
import jax
import jax.numpy as jnp
from jax import lax
from jax.sharding import PartitionSpec as P

BLOCK_EDGE = 16


def spectral_weight(offsets, count):
    angle = jnp.pi * offsets.astype(jnp.float32) / count
    parity = (offsets % 2).astype(jnp.float32)
    on_diagonal = offsets % count == 0
    sine = jnp.where(on_diagonal, 1.0, jnp.sin(angle))
    signed = 1.0 - 2.0 * parity
    first = 0.5 * signed * jnp.cos(angle) / sine
    second = -0.5 * signed / (sine * sine)
    centre = -0.25 * (count * count + 2) / 12.0
    return jnp.where(on_diagonal, centre, first + 0.25 * second)


def table_lookup(table, index):
    numbers = jnp.arange(table.shape[0], dtype=jnp.int32)
    matches = index[:, None] == numbers[None, :]
    return jnp.sum(jnp.where(matches, table[None, :], 0), axis=1)


def row_lookup(table, index):
    numbers = jnp.arange(table.shape[0], dtype=jnp.int32)
    matches = index[:, None, None] == numbers[None, :, None]
    return jnp.sum(jnp.where(matches, table[None, :, :], 0), axis=1)


def face_sources(block_ids, neighbour, orient, slots):
    numbers = jnp.arange(block_ids.shape[0], dtype=jnp.int32)
    position = jnp.sum(
        jnp.where(block_ids[None, :] == numbers[:, None], numbers[None, :], 0), axis=1
    )
    owners = table_lookup(block_ids, slots)
    partner = row_lookup(neighbour, owners).reshape(-1)
    codes = row_lookup(orient, owners).reshape(-1)
    is_wall = partner < 0
    target = jnp.maximum(partner, 0)
    source_row = table_lookup(position, target // 6) * 6 + target % 6
    return (source_row, is_wall, codes)


def block_faces(blocks, edge):
    variables, count = (blocks.shape[0], blocks.shape[1])
    square = edge * edge
    parts = [
        blocks[:, :, 0, :],
        blocks[:, :, edge - 1, :],
        blocks[..., :edge].reshape(variables, count, square),
        blocks[..., square - edge :].reshape(variables, count, square),
        blocks[..., 0::edge].reshape(variables, count, square),
        blocks[..., edge - 1 :: edge].reshape(variables, count, square),
    ]
    stacked = jnp.stack(parts, axis=2)
    return jnp.moveaxis(stacked, 0, 2).reshape(count * 6, variables, square)


def turn_faces(faces, codes, edge):
    grid = faces.reshape(faces.shape[0], faces.shape[1], edge, edge)
    grid = jnp.where((codes & 1 == 1)[:, None, None, None], jnp.swapaxes(grid, 2, 3), grid)
    grid = jnp.where((codes & 2 == 2)[:, None, None, None], jnp.flip(grid, 2), grid)
    grid = jnp.where((codes & 4 == 4)[:, None, None, None], jnp.flip(grid, 3), grid)
    return grid.reshape(faces.shape)


def section_halos(all_faces, source_row, is_wall, codes, edge, count, variables):
    picked = jnp.take(all_faces, source_row, axis=0)
    turned = turn_faces(picked, codes, edge)
    turned = jnp.where(is_wall[:, None, None], 0.0, turned)
    grouped = turned.reshape(count, 6, variables, edge * edge)
    return [jnp.moveaxis(grouped[:, facing], 1, 0) for facing in range(6)]


def neighbour_fields(blocks, halos, edge):
    variables, count = (blocks.shape[0], blocks.shape[1])
    grid_shape = (variables, count, edge, edge)
    lower_x = jnp.concatenate([halos[0][:, :, None, :], blocks[:, :, :-1, :]], axis=2)
    upper_x = jnp.concatenate([blocks[:, :, 1:, :], halos[1][:, :, None, :]], axis=2)
    lower_y = jnp.concatenate([halos[2].reshape(grid_shape), blocks[..., :-edge]], axis=3)
    upper_y = jnp.concatenate([blocks[..., edge:], halos[3].reshape(grid_shape)], axis=3)
    column = jnp.arange(edge * edge, dtype=jnp.int32) % edge
    lower_z = jnp.where(
        column == 0,
        jnp.repeat(halos[4].reshape(grid_shape), edge, axis=3),
        jnp.roll(blocks, 1, axis=3),
    )
    upper_z = jnp.where(
        column == edge - 1,
        jnp.repeat(halos[5].reshape(grid_shape), edge, axis=3),
        jnp.roll(blocks, -1, axis=3),
    )
    return [blocks, lower_x, upper_x, lower_y, upper_y, lower_z, upper_z]


def apply_section(coeffs, blocks, halos, edge):
    result = jnp.zeros(blocks.shape, jnp.float32)
    for stencil_pos, values in enumerate(neighbour_fields(blocks, halos, edge)):
        result = result + jnp.sum(coeffs[stencil_pos].astype(jnp.float32) * values[None], axis=1)
    return result


def local(basis, flux_adjoint, recon_adjoint, pseudo_time, vol_omega, block_ids, neighbour, orient):
    edge = BLOCK_EDGE
    square = edge * edge
    variables = basis.shape[2]
    cells = basis.shape[3]
    block_count = cells // (edge * square)
    space_size = lax.axis_size("space")
    space_rank = lax.axis_index("space")
    inst_size = lax.axis_size("inst")
    inst_rank = lax.axis_index("inst")
    slots = space_rank * block_count + jnp.arange(block_count, dtype=jnp.int32)
    source_row, is_wall, codes = face_sources(block_ids, neighbour, orient, slots)
    vector = basis[basis.shape[0] - 1]

    def section(coeffs, blocks):
        faces = block_faces(blocks, edge)
        all_faces = lax.all_gather(faces, "space", axis=0, tiled=True)
        halos = section_halos(all_faces, source_row, is_wall, codes, edge, block_count, variables)
        return apply_section(
            coeffs.reshape(7, variables, variables, block_count, edge, square), blocks, halos, edge
        )

    piece = lax.all_gather(vector, "inst", axis=0, tiled=True)
    offsets = jnp.arange(piece.shape[0], dtype=jnp.int32) - inst_rank
    weights = spectral_weight(offsets, inst_size)
    spectral = jnp.sum(weights[:, None, None] * piece, axis=0, keepdims=True)
    blocks = vector[0].reshape(variables, block_count, edge, square)
    first = section(flux_adjoint[0], blocks)
    second = section(recon_adjoint[0], first)
    image = pseudo_time * vector + second.reshape(1, variables, cells) + vol_omega * spectral
    entries = float(inst_size * variables * cells * space_size)
    flat_basis = basis.reshape(basis.shape[0], -1)
    partial_dots = jnp.dot(flat_basis, image.reshape(-1), precision=lax.Precision.HIGHEST)
    coeffs = lax.psum(partial_dots, ("inst", "space")) / entries
    ortho = image - jnp.einsum("k,knvc->nvc", coeffs, basis, precision=lax.Precision.HIGHEST)
    squares = lax.psum(jnp.sum(ortho * ortho), ("inst", "space")) / entries
    norm = jnp.sqrt(squares + 1e-06)
    return (ortho / norm, jnp.concatenate([coeffs, norm[None]]))


def solution(mesh):
    placed = (
        P(None, "inst", None, "space"),
        P("inst", None, None, None, "space"),
        P("inst", None, None, None, "space"),
        P("space"),
        P("space"),
        P(),
        P(),
        P(),
    )
    return jax.shard_map(
        local,
        mesh=mesh,
        in_specs=placed,
        out_specs=(P("inst", None, "space"), P()),
        check_vma=False,
    )
```

profile of v0, /device:TPU:1, one launch (start us, length us, event | category | flops | bytes accessed | tf_op | source)
XLA Modules:
  0.0 325.2 jit_solution(13811059401169535473)
XLA Ops:
  7.2 1.9 fusion.24
  9.4 1.0 slice.191
  10.4 1.1 slice.192
  14.6 0.8 fusion.30
  18.1 44.7 %all-gather.5.cloned.1.call-done = f32[192,7,256]{2,1,0:T(8,128)} async-done(((f32[12,7,256]{2,1,0:T(8,128)}), f32[192,7,256]{2,1,0:T(8,128)}) %all-gather.5.cloned.1.call-update) | async-done | bytes 1376272 | tf_op jit(solution)/shard_map/all_gather | solution.py:122
  62.8 2.0 gather_fusion
  68.0 1.1 reshape.550
  69.7 1.8 reshape.552
  71.6 1.2 broadcast_select_fusion.5
  73.8 6.2 %multiply_reduce_fusion.12 = (f32[7,8192]{1,0:T(8,128)S(1)}, f32[7,8192]{1,0:T(8,128)S(1)}, f32[7,8192]{1,0:T(8,128)S(1)}, f32[7,8192]{1,0:T(8,128)S(1)}, f32[7,...) fusion(f32[7,8192]{1,0:T(8,128)S(1)} %bitcast.200, bf16[1,7,7,7,8192]{4,3,2,1,0:T(8,128)(2,1)} %param.11, ...), kind=kLoop, calls=%fused_computation.20 | loop fusion | flops 8028160 | bytes 8830976 | tf_op jit(solution)/shard_map/reduce_sum | solution.py:102
  80.2 1.0 slice.217
  81.3 1.1 slice.218
  84.5 0.8 fusion.25
  85.3 0.8 fusion.26
  86.2 24.5 %all-gather.9.cloned.1.call-done = f32[8,1,7,8192]{3,1,2,0:T(1,128)} async-done(((f32[1,1,7,8192]{3,1,2,0:T(1,128)}), f32[8,1,7,8192]{3,1,2,0:T(1,128)}) %all-gather.9.cloned.1.call-update) | async-done | bytes 1835024 | tf_op jit(solution)/shard_map/all_gather | solution.py:128
  110.7 2.9 fusion.4
  113.6 0.8 reduce_sum.223
  114.5 44.6 %all-gather.7.cloned.1.call-done = f32[192,7,256]{2,1,0:T(8,128)} async-done(((f32[12,7,256]{2,1,0:T(8,128)}), f32[192,7,256]{2,1,0:T(8,128)}) %all-gather.7.cloned.1.call-update) | async-done | bytes 1376272 | tf_op jit(solution)/shard_map/all_gather | solution.py:122
  159.1 2.0 gather_fusion.1
  162.2 0.8 rev.17
  164.3 1.8 reshape.559
  166.7 1.8 reshape.561
  168.5 1.0 pad_maximum_fusion.7
  169.8 1.1 pad_maximum_fusion.8
  171.9 6.2 %multiply_reduce_fusion.5 = (f32[7,8192]{1,0:T(8,128)S(1)}, f32[7,8192]{1,0:T(8,128)S(1)}, f32[7,8192]{1,0:T(8,128)S(1)}, f32[7,8192]{1,0:T(8,128)S(1)}, f32[7,8...) fusion(f32[7,8192]{1,0:T(8,128)S(1)} %bitcast.199, bf16[1,7,7,7,8192]{4,3,2,1,0:T(8,128)(2,1)} %param.12, ...), kind=kLoop, calls=%fused_computation.13 | loop fusion | flops 8028160 | bytes 8830976 | tf_op jit(solution)/shard_map/reduce_sum | solution.py:102
  178.2 1.4 copy-done.1
  179.6 4.8 %fusion.7 = f32[8]{0:T(128)S(1)} fusion(f32[8,1,7,8192]{3,1,2,0:T(1,128)S(1)} %copy-done.1, f32[1,1,7,8192]{3,2,1,0:T(8,128)S(1)} %bitcast.203, f32[1,1,7,8192]{3,1,2,0:T(1,128)S(1)} %copy-done.10, f32[8192]{0:T(1024)S(1)} %copy-done.11, f32[8192]{0:T(1024)S(1)} %copy-done.12), kind=kOutput, calls=%fused_computation.24 | convolution fusion | flops 5734400 | bytes 2621472 | tf_op jit(solution)/shard_map/dot_general | solution.py:138
  184.3 64.8 %psum.14 = f32[8]{0:T(128)S(1)} all-reduce(f32[8]{0:T(128)S(1)} %fusion.7), channel_id=1, replica_groups=mesh['inst'=8,'space'=16] {'inst','space'}, use_global_device_ids=true, to_apply=%region_20.22 | all-reduce | flops 8 | bytes 64 | tf_op jit(solution)/shard_map/psum | solution.py:139
  249.1 2.5 fusion
  251.6 0.9 multiply_reduce_fusion.14
  252.5 63.9 %psum.15 = f32[]{:T(128)} all-reduce(f32[]{:T(128)} %get-tuple-element.25), channel_id=1, replica_groups=mesh['inst'=8,'space'=16] {'inst','space'}, use_global_device_ids=true, to_apply=%region_22.24 | all-reduce | flops 1 | bytes 8 | tf_op jit(solution)/shard_map/psum | solution.py:141
  317.2 0.9 copy.199
  (156 shorter events, 17.7 us)
Async XLA Ops:
  7.2 6.5 %copy-start.15 = (s32[32]{0:T(128)S(1)}, s32[32]{0:T(128)}, u32[]{:S(2)}) copy-start(s32[32]{0:T(128)} %param.15) | copy-start | bytes 388
  7.2 6.7 %copy-start.14 = (s32[32,6]{0,1:T(8,128)S(1)}, s32[32,6]{0,1:T(8,128)}, u32[]{:S(2)}) copy-start(s32[32,6]{0,1:T(8,128)} %param.16) | copy-start | bytes 2308
  7.2 6.7 %copy-start.13 = (s32[32,6]{0,1:T(8,128)S(1)}, s32[32,6]{0,1:T(8,128)}, u32[]{:S(2)}) copy-start(s32[32,6]{0,1:T(8,128)} %param.17) | copy-start | bytes 2308
  7.2 55.6 %all-gather.5.cloned.1.call-start = ((), (), s32[]{:S(2)}) async-start(), calls=%async_computation | async-start | bytes 1671168 | tf_op jit(solution)/shard_map/all_gather | solution.py:122
  12.8 3.5 %copy-start = (f32[1,1,7,8192]{3,1,2,0:T(1,128)S(1)}, f32[1,1,7,8192]{3,1,2,0:T(1,128)}, u32[]{:S(2)}) copy-start(f32[1,1,7,8192]{3,1,2,0:T(1,128)} %get-tuple-element.29) | copy-start | bytes 688132
  12.8 97.9 %all-gather.9.cloned.1.call-start = ((), (), s32[]{:S(2)}) async-start(), calls=%async_computation.2 | async-start | bytes 2064384 | tf_op jit(solution)/shard_map/all_gather | solution.py:128
  13.6 145.5 %all-gather.7.cloned.1.call-start = ((), (), s32[]{:S(2)}) async-start(), calls=%async_computation.1 | async-start | bytes 1671168 | tf_op jit(solution)/shard_map/all_gather | solution.py:122
  71.5 1.5 copy-start.8
  71.5 1.5 copy-start.9
  71.5 2.0 copy-start.6
  71.5 2.0 copy-start.7
  166.7 4.4 %copy-start.4 = (f32[7,2,16,240]{3,2,1,0:T(8,128)S(1)}, f32[7,2,16,240]{3,2,1,0:T(8,128)}, u32[]{:S(2)}) copy-start(f32[7,2,16,240]{3,2,1,0:T(8,128)} %get-tuple-element.38) | copy-start | bytes 645124
  168.5 2.9 copy-start.5
  169.5 2.1 copy-start.2
  170.8 1.0 copy-start.3
  171.9 6.4 %copy-start.12 = (f32[8192]{0:T(1024)S(1)}, f32[8192]{0:T(1024)}, u32[]{:S(2)}) copy-start(f32[8192]{0:T(1024)} %param.13) | copy-start | bytes 98308
  178.1 1.5 copy-start.1
  178.1 1.5 copy-start.10
  178.1 1.5 copy-start.11
Sparse Core Ops, SparseCore 0:
  12.9 49.8 all-gather.4
  65.0 45.6 all-gather.8
  113.2 45.8 all-gather.6
where the time goes:
time: 326 us; the launch traced here: 325 us
  blocking collectives  129 us (40%)
  waiting for transfers between devices  114 us (35%)
  local copies, waits for them, and re-layouts  36 us (11%)
  other arithmetic  23.3 us (7%)
  between operations  15.4 us (5%)
  matrix products  7.25 us (2%)
    all_gather x2, waiting for transfers between devices, section(): all_faces = lax.all_gather(faces, 'space', axis=0, tiled=True)  89.2 us
    psum x1, blocking collectives, local(): coeffs = lax.psum(partial_dots, ('inst', 'space')) / entries  64.8 us
    psum x1, blocking collectives, local(): squares = lax.psum(jnp.sum(ortho * ortho), ('inst', 'space')) / entries  63.9 us
    all_gather x1, waiting for transfers between devices, local(): piece = lax.all_gather(vector, 'inst', axis=0, tiled=True)  24.5 us
    reduce_sum x2, other arithmetic, apply_section(): jnp.sum(coeffs[stencil_pos].astype(jnp.float32) * values[None], axis=1)  12.4 us
  transfers between devices with their start and end apart: 3, of which 3 were waited for; matrix products, arithmetic and copies ran while one was open for 10% of the time, Pallas kernels for 0%

commit v1 on v0

v1 whole, which is shorter than its diff:
```python
import functools
import math

import jax
import jax.numpy as jnp
import numpy as np
from jax import lax
from jax.experimental import pallas as pl
from jax.experimental.pallas import tpu as pltpu
from jax.sharding import Mesh, PartitionSpec as P

EDGE = 16
SQUARE = EDGE * EDGE
CUBE = EDGE * SQUARE
VARS = 7
KRYLOV = 8
INST = 8
BLOCKS = 32
SPACE = 16
CELLS = 8192
PER = CELLS // CUBE
FACES = 6 * PER
SLABS = CELLS // SQUARE
ENTRIES = float(INST * VARS * CELLS * SPACE)
ALL = ("z", "xl", "xh", "y", "core")
CHIPS = ("xh", "y")
HALF = 128
VMEM = pltpu.VMEM
SMEM = pltpu.SMEM
GUARD = 0.02


def mixing_weights():
    k = np.arange(INST)
    parity = np.where(k % 2 == 0, 1.0, -1.0)
    weight = np.empty(INST)
    weight[0] = -0.25 * (INST * INST + 2) / 12.0
    angle = np.pi * k[1:] / INST
    weight[1:] = 0.5 * parity[1:] / np.tan(angle) - 0.125 * parity[1:] / np.sin(angle) ** 2
    return weight.astype(np.float32)


def lanes(shape):
    return lax.broadcasted_iota(jnp.int32, shape, len(shape) - 1)


def pick(values, index):
    return jnp.take_along_axis(values, index, axis=1)


def collect_faces(slab, block, x, faces):
    lane = lanes((8, HALF))
    low, high = (slab[:, :HALF], slab[:, HALF:])
    within = lane % 8
    own = lane // EDGE == x % 8
    upper_half = lane % EDGE >= 8
    strips = (
        pick(low, lane % EDGE),
        pick(high, lane % EDGE + (HALF - EDGE)),
        jnp.where(upper_half, pick(high, within * EDGE), pick(low, within * EDGE)),
        jnp.where(upper_half, pick(high, within * EDGE + 15), pick(low, within * EDGE + 15)),
    )
    start = pl.multiple_of((x // 8) * HALF, HALF)
    for number, strip in enumerate(strips):
        spot = (block * 6 + 2 + number, slice(None), pl.ds(start, HALF))
        faces[spot] = jnp.where(own, strip, faces[spot])

    @pl.when(x == 0)
    def _():
        faces[block * 6] = slab

    @pl.when(x == EDGE - 1)
    def _():
        faces[block * 6 + 1] = slab


def copy_out(faces, sent_ref):
    for number in range(FACES):
        face = faces[number]
        for chip in range(sent_ref.shape[0]):
            sent_ref[chip, number] = face


def first_faces_kernel(which_ref, vector_ref, sent_ref, mine_ref, other_ref, faces):
    faces[...] = jnp.zeros_like(faces)

    def step(k, carry):
        start = pl.multiple_of(k * SQUARE, SQUARE)
        slab = vector_ref[0, 0, :, pl.ds(start, SQUARE)]
        slab = jnp.concatenate([slab, jnp.zeros((1, SQUARE), jnp.float32)], axis=0)
        collect_faces(slab, k // EDGE, k % EDGE, faces)
        return carry

    lax.fori_loop(0, SLABS, step, 0)
    copy_out(faces, sent_ref)
    mine = pl.multiple_of(which_ref[0] * CUBE, CUBE)
    other = pl.multiple_of((1 - which_ref[0]) * CUBE, CUBE)
    mine_ref[...] = vector_ref[0, 0, :, pl.ds(mine, CUBE)]
    other_ref[...] = vector_ref[0, 0, :, pl.ds(other, CUBE)]


def fetch_halos(tables_ref, own_ref, swapped_ref, position, halos):
    rank = tables_ref[BLOCKS * 13]

    def place(slot, carry):
        position[tables_ref[slot]] = slot
        return carry

    lax.fori_loop(0, BLOCKS, place, 0)
    lane = lanes((8, HALF))

    def face(number, carry):
        owner = tables_ref[rank * PER + number // 6]
        entry = owner * 6 + number % 6
        partner = tables_ref[BLOCKS + entry]
        code = tables_ref[BLOCKS * 7 + entry]
        target = jnp.maximum(partner, 0)
        slot = position[target // 6]
        device = slot // PER
        row = (slot % PER) * 6 + target % 6
        own = own_ref[device // 2, row]
        swapped = swapped_ref[device // 2, row]
        source = jnp.where(device % 2 == rank % 2, own, swapped)
        source = jnp.where(partner < 0, 0.0, source)
        low, high = (source[:, :HALF], source[:, HALF:])
        transposed = code % 2 == 1
        flip_a = (code // 2) % 2 * (EDGE - 1)
        flip_b = (code // 4) * (EDGE - 1)
        for half in range(2):
            a = lane // EDGE + half * 8
            b = lane % EDGE
            a = jnp.abs(a - flip_a)
            b = jnp.abs(b - flip_b)
            index = jnp.where(transposed, b * EDGE + a, a * EDGE + b)
            inside = index % HALF
            halos[number, :, half * HALF : (half + 1) * HALF] = jnp.where(
                index < HALF, pick(low, inside), pick(high, inside)
            )
        return carry

    lax.fori_loop(0, FACES, face, 0)


def slab_neighbours(load, halos, k):
    block, x = (k // EDGE, k % EDGE)
    centre = load(k)
    below = jnp.where(x == 0, halos[block * 6, :VARS], load(jnp.maximum(k - 1, 0)))
    above = jnp.where(x == EDGE - 1, halos[block * 6 + 1, :VARS], load(jnp.minimum(k + 1, SLABS - 1)))
    lane = lanes((8, HALF))
    start = pl.multiple_of((x // 8) * HALF, HALF)
    offset = (x % 8) * EDGE

    def strip(face):
        return halos[block * 6 + face, :, pl.ds(start, HALF)]

    def spread_y(face):
        piece = pick(strip(face), lane % EDGE + offset)
        return jnp.concatenate([piece, piece], axis=1)[:VARS]

    def spread_z(face):
        source = strip(face)
        return jnp.concatenate(
            [pick(source, lane // EDGE + offset), pick(source, lane // EDGE + (offset + 8))], axis=1
        )[:VARS]

    column = lanes((VARS, SQUARE))
    z = column % EDGE
    y_low = jnp.where(column < EDGE, spread_y(2), pltpu.roll(centre, EDGE, 1))
    y_high = jnp.where(column >= SQUARE - EDGE, spread_y(3), pltpu.roll(centre, SQUARE - EDGE, 1))
    z_low = jnp.where(z == 0, spread_z(4), pltpu.roll(centre, 1, 1))
    z_high = jnp.where(z == EDGE - 1, spread_z(5), pltpu.roll(centre, SQUARE - 1, 1))
    return [centre, below, above, y_low, y_high, z_low, z_high]


def section_slab(coeff_ref, operands, start):
    totals = [None] * VARS
    for s, operand in enumerate(operands):
        for o in range(VARS):
            term = coeff_ref[0, s, o, :, pl.ds(start, SQUARE)].astype(jnp.float32) * operand
            totals[o] = term if totals[o] is None else totals[o] + term
    empty = jnp.zeros((1, SQUARE), jnp.float32)
    padded = [jnp.concatenate([total, empty], axis=0) for total in totals]
    padded.append(jnp.zeros((8, SQUARE), jnp.float32))
    row = lax.broadcasted_iota(jnp.int32, (8, SQUARE), 0)

    quarter = [fold4(padded[i], padded[i + 4], row) for i in range(4)]
    pair = [fold2(quarter[i], quarter[i + 2], row) for i in range(2)]
    return fold1(pair[0], pair[1], row)


def fold4(a, b, row):
    first = row < 4
    return jnp.where(first, a, b) + pltpu.roll(jnp.where(first, b, a), 4, 0)


def fold2(a, b, row):
    first = row % 4 < 2
    other = jnp.where(first, b, a)
    moved = jnp.where(first, pltpu.roll(other, 6, 0), pltpu.roll(other, 2, 0))
    return jnp.where(first, a, b) + moved


def fold1(a, b, row):
    first = row % 2 == 0
    other = jnp.where(first, b, a)
    moved = jnp.where(first, pltpu.roll(other, 7, 0), pltpu.roll(other, 1, 0))
    return jnp.where(first, a, b) + moved


def flux_kernel(tables_ref, own_ref, swapped_ref, vector_ref, coeff_ref, first_ref, sent_ref, halos, faces, position):
    fetch_halos(tables_ref, own_ref, swapped_ref, position, halos)
    faces[...] = jnp.zeros_like(faces)

    def load(k):
        return vector_ref[0, 0, :, pl.ds(pl.multiple_of(k * SQUARE, SQUARE), SQUARE)]

    def step(k, carry):
        start = pl.multiple_of(k * SQUARE, SQUARE)
        slab = section_slab(coeff_ref, slab_neighbours(load, halos, k), start)
        first_ref[:, pl.ds(start, SQUARE)] = slab[:VARS]
        collect_faces(slab, k // EDGE, k % EDGE, faces)
        return carry

    lax.fori_loop(0, SLABS, step, 0)
    copy_out(faces, sent_ref)


def gram_kernel(basis_ref, gram_ref):
    rows = []

    def step(k, totals):
        start = pl.multiple_of(k * SQUARE, SQUARE)
        fields = [basis_ref[j, 0, :, pl.ds(start, SQUARE)] for j in range(KRYLOV)]
        out = []
        number = 0
        for i in range(KRYLOV):
            for j in range(i, KRYLOV):
                term = fields[i] * fields[j]
                out.append(totals[number] + term[:, :HALF] + term[:, HALF:])
                number += 1
        return tuple(out)

    zero = jnp.zeros((VARS, HALF), jnp.float32)
    totals = lax.fori_loop(0, SLABS, step, (zero,) * (KRYLOV * (KRYLOV + 1) // 2))
    number = 0
    for i in range(KRYLOV):
        for j in range(i, KRYLOV):
            line = jnp.sum(totals[number], axis=0, keepdims=True)
            gram_ref[i * KRYLOV + j : i * KRYLOV + j + 1] = line
            if i != j:
                gram_ref[j * KRYLOV + i : j * KRYLOV + i + 1] = line
            number += 1


def image_kernel(
    tables_ref, own_ref, swapped_ref, first_ref, coeff_ref, basis_ref, pseudo_ref, omega_ref,
    mixed_ref, returned_ref, gram_ref, image_ref, sums_ref, halos, position, lines
):
    fetch_halos(tables_ref, own_ref, swapped_ref, position, halos)
    which = tables_ref[BLOCKS * 13 + 1]

    def load(k):
        return first_ref[:, pl.ds(pl.multiple_of(k * SQUARE, SQUARE), SQUARE)]

    def step(k, totals):
        start = pl.multiple_of(k * SQUARE, SQUARE)
        inner = pl.multiple_of((k % EDGE) * SQUARE, SQUARE)
        slab = section_slab(coeff_ref, slab_neighbours(load, halos, k), start)[:VARS]
        spectral = jnp.where(
            k // EDGE == which, mixed_ref[:, pl.ds(inner, SQUARE)], returned_ref[:, pl.ds(inner, SQUARE)]
        )
        vector = basis_ref[KRYLOV - 1, 0, :, pl.ds(start, SQUARE)]
        image = pseudo_ref[:, pl.ds(start, SQUARE)] * vector + slab + omega_ref[:, pl.ds(start, SQUARE)] * spectral
        image_ref[:, pl.ds(start, SQUARE)] = image
        out = []
        for j in range(KRYLOV + 1):
            field = image if j == KRYLOV else basis_ref[j, 0, :, pl.ds(start, SQUARE)]
            term = field * image
            out.append(totals[j] + term[:, :HALF] + term[:, HALF:])
        return tuple(out)

    zero = jnp.zeros((VARS, HALF), jnp.float32)
    totals = lax.fori_loop(0, SLABS, step, (zero,) * (KRYLOV + 1))
    lines[...] = jnp.zeros_like(lines)
    for j in range(KRYLOV + 1):
        lines[j : j + 1] = jnp.sum(totals[j], axis=0, keepdims=True)
    lines[64:] = gram_ref[...]
    ones = jnp.ones((8, HALF), jnp.float32)
    sums = lax.dot_general(
        ones, lines[...], (((1,), (1,)), ((), ())),
        precision=lax.Precision.HIGHEST, preferred_element_type=jnp.float32,
    )
    for group in range(16):
        sums_ref[group * 8 : group * 8 + 8] = sums


def finish_kernel(received_ref, image_ref, basis_ref, next_ref, column_ref):
    sums = jnp.sum(received_ref[...], axis=0, keepdims=True)
    sums = jnp.broadcast_to(sums, (8, HALF)) / ENTRIES
    lane = lanes((8, HALF))
    left = pick(sums, jnp.maximum(lane - 64, 0) // 8)
    right = pick(sums, lane % 8)
    quadratic = jnp.sum(jnp.where(lane >= 64, sums * left * right, 0.0), axis=1, keepdims=True)
    linear = jnp.sum(jnp.where(lane < KRYLOV, sums * sums, 0.0), axis=1, keepdims=True)
    whole = sums[:, KRYLOV : KRYLOV + 1]
    squares = whole - 2.0 * linear + quadratic
    size = whole + 2.0 * linear + jnp.abs(quadratic)
    norm = jnp.sqrt(jnp.maximum(squares, 0.0) + 1e-06)
    inverse = 1.0 / norm
    column = jnp.where(lane < KRYLOV, sums, jnp.where(lane == KRYLOV, norm, 0.0))
    column_ref[...] = jnp.where(lane == KRYLOV + 1, jnp.where(squares < GUARD * size, 1.0, 0.0), column)
    coeffs = [jnp.broadcast_to(sums[:VARS, j : j + 1], (VARS, SQUARE)) for j in range(KRYLOV)]
    scale = jnp.broadcast_to(inverse[:VARS], (VARS, SQUARE))

    def step(k, carry):
        start = pl.multiple_of(k * SQUARE, SQUARE)
        ortho = image_ref[:, pl.ds(start, SQUARE)]
        for j in range(KRYLOV):
            ortho = ortho - coeffs[j] * basis_ref[j, 0, :, pl.ds(start, SQUARE)]
        next_ref[0, :, pl.ds(start, SQUARE)] = ortho * scale
        return carry

    lax.fori_loop(0, SLABS, step, 0)


def whole(memory=VMEM):
    return pl.BlockSpec(memory_space=memory)


def last_vector():
    return pl.BlockSpec((1, 1, VARS, CELLS), lambda i: (KRYLOV - 1, 0, 0, 0))


def whole_in_grid(shape):
    return pl.BlockSpec(shape, lambda i: (0,) * len(shape))


def f32(*shape):
    return jax.ShapeDtypeStruct(shape, jnp.float32)


PARAMS = pltpu.CompilerParams(vmem_limit_bytes=24 * 2**20)


def swap(size, bit):
    return [(i, i ^ bit) for i in range(size)]


def exchange(sent):
    own = lax.all_to_all(sent, CHIPS, 0, 0)
    return own, lax.ppermute(own, "core", swap(2, 1))


def mix(mine, other, z):
    received = lax.ppermute(other, "xl", swap(2, 1))
    xl = lax.axis_index("xl")
    even = jnp.where(xl == 0, mine, received)
    odd = jnp.where(xl == 0, received, mine)
    pair = jnp.stack([even, odd])
    parts = [pair] + [lax.ppermute(pair, "z", swap(4, k)) for k in (1, 2, 3)]
    weights = jnp.asarray(mixing_weights())
    results = []
    for target in (xl, 1 - xl):
        total = 0.0
        for k, part in enumerate(parts):
            source = (z ^ k) * 2
            for offset in range(2):
                weight = weights[(source + offset - (2 * z + target)) % INST]
                total = total + weight * part[offset]
        results.append(total)
    return results[0], lax.ppermute(results[1], "xl", swap(2, 1))


def local(basis, flux, recon, pseudo_time, vol_omega, block_ids, neighbour, orient):
    z = lax.axis_index("z")
    xl = lax.axis_index("xl").astype(jnp.int32)
    rank = lax.axis_index(("xh", "y", "core")).astype(jnp.int32)
    tables = jnp.concatenate(
        [block_ids, neighbour.reshape(-1), orient.reshape(-1), rank[None], xl[None]]
    )
    sent, mine, other = pl.pallas_call(
        first_faces_kernel,
        grid=(1,),
        in_specs=[whole(SMEM), last_vector()],
        out_specs=[whole_in_grid((8, FACES, 8, SQUARE)), whole_in_grid((VARS, CUBE)), whole_in_grid((VARS, CUBE))],
        out_shape=[f32(8, FACES, 8, SQUARE), f32(VARS, CUBE), f32(VARS, CUBE)],
        scratch_shapes=[VMEM((FACES, 8, SQUARE), jnp.float32)],
        compiler_params=PARAMS,
        name="first_faces",
    )(xl[None], basis)
    own, swapped = exchange(sent)
    mixed, returned = mix(mine, other, z)
    gram = pl.pallas_call(
        gram_kernel,
        in_specs=[whole()],
        out_specs=whole(),
        out_shape=f32(KRYLOV * KRYLOV, HALF),
        compiler_params=PARAMS,
        cost_estimate=pl.CostEstimate(flops=2 * 36 * 7 * 8192, bytes_accessed=2 * 2**20, transcendentals=0),
        name="gram",
    )(basis)
    first, sent = pl.pallas_call(
        flux_kernel,
        grid=(1,),
        in_specs=[
            whole(SMEM), whole(), whole(), last_vector(), whole(),
        ],
        out_specs=[whole_in_grid((VARS, CELLS)), whole_in_grid((8, FACES, 8, SQUARE))],
        out_shape=[f32(VARS, CELLS), f32(8, FACES, 8, SQUARE)],
        scratch_shapes=[
            VMEM((FACES, 8, SQUARE), jnp.float32),
            VMEM((FACES, 8, SQUARE), jnp.float32),
            SMEM((BLOCKS,), jnp.int32),
        ],
        compiler_params=PARAMS,
        name="flux_section",
    )(tables, own, swapped, basis, flux)
    own, swapped = exchange(sent)
    image, sums = pl.pallas_call(
        image_kernel,
        in_specs=[whole(SMEM)] + [whole()] * 10,
        out_specs=[whole(), whole()],
        out_shape=[f32(VARS, CELLS), f32(HALF, HALF)],
        scratch_shapes=[
            VMEM((FACES, 8, SQUARE), jnp.float32),
            SMEM((BLOCKS,), jnp.int32),
            VMEM((HALF, HALF), jnp.float32),
        ],
        compiler_params=PARAMS,
        name="image",
    )(
        tables, own, swapped, first, recon, basis, pseudo_time[None], vol_omega[None],
        mixed, returned, gram,
    )
    received = lax.all_to_all(sums, ALL, 0, 0)
    following, column = pl.pallas_call(
        finish_kernel,
        in_specs=[whole()] * 3,
        out_specs=[whole(), whole()],
        out_shape=[f32(1, VARS, CELLS), f32(8, HALF)],
        compiler_params=PARAMS,
        name="finish",
    )(received, image, basis)
    coeffs = column[0, :KRYLOV]
    hessenberg = column[0, : KRYLOV + 1]

    def direct(state):
        ortho = image - jnp.einsum("k,kvc->vc", coeffs, basis[:, 0], precision=lax.Precision.HIGHEST)
        squares = lax.psum(jnp.sum(ortho * ortho), ALL) / ENTRIES
        norm = jnp.sqrt(squares + 1e-06)
        return ((ortho / norm)[None], jnp.concatenate([coeffs, norm[None]]), 0.0 * norm)

    following, hessenberg, _ = lax.while_loop(
        lambda state: state[2] > 0.5, direct, (following, hessenberg, column[0, KRYLOV + 1])
    )
    return following, hessenberg


def solution(mesh):
    fine = Mesh(mesh.devices.reshape(4, 2, 2, 4, 2), ALL)
    inst, space = (("z", "xl"), ("xh", "y", "core"))
    placed = (
        P(None, inst, None, space),
        P(inst, None, None, None, space),
        P(inst, None, None, None, space),
        P(space),
        P(space),
        P(),
        P(),
        P(),
    )
    return jax.shard_map(
        local,
        mesh=fine,
        in_specs=placed,
        out_specs=(P(inst, None, space), P()),
        check_vma=False,
    )
```

time: 326 us -> 174 us (0.53)
  waiting for transfers between devices: 114 us -> 13.7 us
  blocking collectives: 129 us -> 78.4 us
  starting transfers between devices: 0.12 us -> 25.2 us
  local copies, waits for them, and re-layouts: 36 us -> 14.9 us
  Pallas kernels: 0 us -> 20.8 us
  between operations: 15.4 us -> 1.61 us
  other arithmetic: 23.3 us -> 15.8 us
  matrix products: 7.25 us -> 2.5 us
    all_gather x3 -> x0, waiting for transfers between devices: 114 us -> none  [the longest x2 89.2 us: section(): all_faces = lax.all_gather(faces, 'space', axis=0, tiled=True)]
    psum x2 -> x1, blocking collectives: 129 us -> 62.7 us  [direct(): squares = lax.psum(jnp.sum(ortho * ortho), ALL) / ENTRIES]
    pallas_call x0 -> x5, Pallas kernels: none -> 20.8 us  [the longest x1 9.08 us: local(): pl.pallas_call(flux_kernel, grid=(1,), in_specs=[whole(SMEM), whole(), wh...]
    reduce_sum x8 -> x1, other arithmetic: 17 us -> 0.77 us  [direct(): squares = lax.psum(jnp.sum(ortho * ortho), ALL) / ENTRIES]
    all_to_all x0 -> x1, blocking collectives: none -> 15.8 us  [local(): received = lax.all_to_all(sums, ALL, 0, 0)]
    all_to_all x0 -> x2, waiting for transfers between devices: none -> 13.7 us  [exchange(): own = lax.all_to_all(sent, CHIPS, 0, 0)]
    ppermute x0 -> x7, starting transfers between devices: none -> 13.6 us  [the longest x2 8.03 us: exchange(): return (own, lax.ppermute(own, 'core', swap(2, 1)))]
    add x3 -> x2, other arithmetic: 0.2 us -> 13.2 us  [mix(): total = total + weight * part[offset]]
  transfers between devices with their start and end apart: 3 -> 9, of which waited for: 3 -> 2; matrix products, arithmetic and copies ran while one was open for 10% -> 9% of each run, Pallas kernels for 0% -> 6%
where the time goes in v1:
time: 174 us
  blocking collectives  78.4 us (45%)
  starting transfers between devices  25.2 us (14%)
  Pallas kernels  20.8 us (12%)
  other arithmetic  15.8 us (9%)
  local copies, waits for them, and re-layouts  14.9 us (9%)
  waiting for transfers between devices  13.7 us (8%)
  matrix products  2.5 us (1%)
    psum x1, blocking collectives, direct(): squares = lax.psum(jnp.sum(ortho * ortho), ALL) / ENTRIES  62.7 us
    all_to_all x1, blocking collectives, local(): received = lax.all_to_all(sums, ALL, 0, 0)  15.8 us
    all_to_all x2, waiting for transfers between devices, exchange(): own = lax.all_to_all(sent, CHIPS, 0, 0)  13.7 us
    add x2, other arithmetic, mix(): total = total + weight * part[offset]  13.2 us
    unnamed x30, local copies, waits for them, and re-layouts  12.7 us
    all_to_all x2, starting transfers between devices, exchange(): own = lax.all_to_all(sent, CHIPS, 0, 0)  11.6 us
    pallas_call x1, Pallas kernels, local(): pl.pallas_call(flux_kernel, grid=(1,), in_specs=[whole(SMEM), whole(), wh...  9.08 us
    ppermute x2, starting transfers between devices, exchange(): return (own, lax.ppermute(own, 'core', swap(2, 1)))  8.03 us
  transfers between devices with their start and end apart: 9, of which 2 were waited for; matrix products, arithmetic and copies ran while one was open for 9% of the time, Pallas kernels for 6%

profile of v1, /device:TPU:1, one launch (start us, length us, event | category | flops | bytes accessed | tf_op | source)
XLA Modules:
  0.0 173.6 jit_solution(4398892898974836991)
XLA Ops:
  0.6 2.6 %copy.28.vector_ref.basis_ref = f32[8,1,7,8192]{3,2,1,0:T(8,128)S(1)} copy(f32[8,1,7,8192]{3,1,2,0:T(1,128)} %param.11) | data formatting | bytes 3670016 | tf_op args[0]
  3.2 2.8 %first_faces.1 = (f32[8,12,8,256]{3,2,1,0:T(8,128)S(1)}, f32[7,4096]{1,0:T(8,128)S(1)}, f32[7,4096]{1,0:T(8,128)S(1)}) custom-call(s32[1]{0:T(128)} %bitcast.2.which_ref, f32[8,1,7,8192]{3,2,1,0:T(8,128)S(1)} %copy.28.vector_ref.basis_ref), custom_call_target="tpu_custom_call" | custom-call | tf_op jit(solution)/shard_map/first_faces/pallas_call | solution.py:381
  6.0 0.9 copy-done.3
  6.9 7.6 %all-to-all-start = ((f32[8,12,8,256]{3,2,1,0:T(8,128)}), f32[8,12,8,256]{3,2,1,0:T(8,128)S(1)}, u32[]{:S(2)}, u32[]{:S(2)}) async-start(f32[8,12,8,256]{3,2,1,0:T(8,128)} %copy-done.3), calls=%async_computation | async-start | bytes 1572864 | tf_op jit(solution)/shard_map/all_to_all | solution.py:350
  14.8 11.1 %all-to-all-done.own_ref = f32[8,12,8,256]{3,2,1,0:T(8,128)S(1)} async-done(((f32[8,12,8,256]{3,2,1,0:T(8,128)}), f32[8,12,8,256]{3,2,1,0:T(8,128)S(1)}, u32[]{:S(2)}, u32[]{:S(2)}) %all-to-all-start) | async-done | bytes 786464 | tf_op jit(solution)/shard_map/all_to_all | solution.py:350
  25.9 3.3 %collective-permute-start = (f32[8,12,8,256]{3,2,1,0:T(8,128)S(1)}, f32[8,12,8,256]{3,2,1,0:T(8,128)}, u32[]{:S(2)}, u32[]{:S(2)}) collective-permute-start(f32[8,12,8,256]{3,2,1,0:T(8,128)S(1)} %all-to-all-done.own_ref), channel_id=1, source_target_pairs={{0,1},{1,0},{2,3},{3,2},{4,5},{5,4},{6,7},{7,6},{8,9},{9,8},{10,11... | collective-permute-start | bytes 2359304 | tf_op jit(solution)/shard_map/ppermute | solution.py:351
  29.2 0.7 copy-done.8
  29.8 0.9 broadcast_select_fusion.1
  30.8 0.8 pad_maximum_fusion
  31.5 1.6 collective-permute-start.3
  33.2 3.3 %collective-permute-start.4 = (f32[2,7,4096]{2,1,0:T(8,128)}, f32[2,7,4096]{2,1,0:T(8,128)}, u32[]{:S(2)}, u32[]{:S(2)}) collective-permute-start(f32[2,7,4096]{2,1,0:T(8,128)} %pad_maximum_fusion), channel_id=1, source_target_pairs={{0,64},{32,96},{64,0},{96,32},{1,65},{33,97},{65,1},{97,33},{2,66}... | collective-permute-start | bytes 688136 | tf_op jit(solution)/shard_map/ppermute | solution.py:360
  37.1 1.0 gram.1.gram_ref
  38.1 0.8 fusion.5
  38.9 2.8 %copy-done = bf16[1,7,7,7,8192]{4,3,2,1,0:T(8,128)(2,1)S(1)} copy-done((bf16[1,7,7,7,8192]{4,3,2,1,0:T(8,128)(2,1)S(1)}, bf16[1,7,7,7,8192]{4,3,2,1,0:T(8,128)(2,1)}, u32[]{:S(2)}) %copy-start) | copy-done | bytes 5619736
  41.7 9.1 %flux_section.1 = (f32[7,8192]{1,0:T(8,128)S(1)}, f32[8,12,8,256]{3,2,1,0:T(8,128)S(1)}) custom-call(s32[418]{0:T(512)S(1)} %concatenate.8.tables_ref, f32[8,12,8,256]{3,2,1,0:T(8,128)S(1)} %all-to-all-done.own_ref, f32[8,12,8,256]{3,2,1,0:T(8,128)} %collective-permute-done.swapped_ref, f32[8,1,7,8192]{3,2,1,0:T(8,128)S(1)} %copy.28.vector_ref.basis_ref, ...), custom_call_target="tpu_custom_call" | custom-call | tf_op jit(solution)/shard_map/flux_section/pallas_call | solution.py:402
  50.8 0.9 copy-done.2
  51.7 4.0 %all-to-all-start.1 = ((f32[8,12,8,256]{3,2,1,0:T(8,128)}), f32[8,12,8,256]{3,2,1,0:T(8,128)S(1)}, u32[]{:S(2)}, u32[]{:S(2)}) async-start(f32[8,12,8,256]{3,2,1,0:T(8,128)} %copy-done.2), calls=%async_computation.1 | async-start | bytes 1572864 | tf_op jit(solution)/shard_map/all_to_all | solution.py:350
  55.8 6.9 %bitcast_add_fusion = f32[7,4096]{1,0:T(8,128)} fusion(f32[7,4096]{1,0:T(8,128)S(1)} %get-tuple-element.124, f32[7,4096]{1,0:T(8,128)S(1)} %get-tuple-element.123, f32[2,7,4096]{2,1,0:T(8,128)} %collective-permute-done.5, f32[2,7,4096]{2,1,0:T(8,128)} %collective-permute-done.4, f32[2,7,4096]{2,1,0:T(8,128)} %collective-permute-done.3, f32[]{:T(128)} %bitcast.33, ...), kind=kLoop, calls=%fused_computation.7 | loop fusion | flops 430080 | bytes 1032224 | tf_op jit(solution)/shard_map/add | solution.py:369
  63.0 2.6 %all-to-all-done.1.own_ref = f32[8,12,8,256]{3,2,1,0:T(8,128)S(1)} async-done(((f32[8,12,8,256]{3,2,1,0:T(8,128)}), f32[8,12,8,256]{3,2,1,0:T(8,128)S(1)}, u32[]{:S(2)}, u32[]{:S(2)}) %all-to-all-start.1) | async-done | bytes 786464 | tf_op jit(solution)/shard_map/all_to_all | solution.py:350
  65.6 4.7 %collective-permute-start.1 = (f32[8,12,8,256]{3,2,1,0:T(8,128)S(1)}, f32[8,12,8,256]{3,2,1,0:T(8,128)S(1)}, u32[]{:S(2)}, u32[]{:S(2)}) collective-permute-start(f32[8,12,8,256]{3,2,1,0:T(8,128)S(1)} %all-to-all-done.1.own_ref), channel_id=1, source_target_pairs={{0,1},{1,0},{2,3},{3,2},{4,5},{5,4},{6,7},{7,6},{8,9},{9,8},{10,11... | collective-permute-start | bytes 2359304 | tf_op jit(solution)/shard_map/ppermute | solution.py:351
  70.3 6.3 %bitcast_add_fusion.6.mixed_ref = f32[7,4096]{1,0:T(8,128)S(1)} fusion(f32[7,4096]{1,0:T(8,128)} %copy-done.7, f32[7,4096]{1,0:T(8,128)S(1)} %get-tuple-element.123, f32[2,7,4096]{2,1,0:T(8,128)} %collective-permute-done.5, f32[2,7,4096]{2,1,0:T(8,128)} %collective-permute-done.4, f32[2,7,4096]{2,1,0:T(8,128)} %collective-permute-done.3, f32[]{:T(128)} %bitcast.19, ...), kind=kLoop, calls=%fused_computation.13 | loop fusion | flops 430080 | bytes 1032224 | tf_op jit(solution)/shard_map/add | solution.py:369
  76.7 2.8 %copy-done.1 = bf16[1,7,7,7,8192]{4,3,2,1,0:T(8,128)(2,1)S(1)} copy-done((bf16[1,7,7,7,8192]{4,3,2,1,0:T(8,128)(2,1)S(1)}, bf16[1,7,7,7,8192]{4,3,2,1,0:T(8,128)(2,1)}, u32[]{:S(2)}) %copy-start.1) | copy-done | bytes 5619736
  79.5 6.6 %image.1 = (f32[7,8192]{1,0:T(8,128)S(1)}, f32[128,128]{1,0:T(8,128)S(1)}) custom-call(s32[418]{0:T(512)S(1)} %concatenate.8.tables_ref, f32[8,12,8,256]{3,2,1,0:T(8,128)S(1)} %all-to-all-done.1.own_ref, f32[8,12,8,256]{3,2,1,0:T(8,128)S(1)} %collective-permute-done.1.swapped_ref, f32[7,8192]{1,0:T(8,128)S(1)} %get-tuple-element.92.first_ref, ...), custom_call_target="tpu_custom_call" | custom-call | tf_op jit(solution)/shard_map/image/pallas_call | solution.py:419
  86.1 15.8 %all_to_all.21 = f32[128,1,128]{2,1,0:T(1,128)S(1)} all-to-all(f32[128,1,128]{2,1,0:T(1,128)S(1)} %bitcast.89), channel_id=1, replica_groups=mesh['z'=4,'xl'=2,'xh'=2,'y'=4,'core'=2] {'z','xl','xh','y','core'}, dimensions={0} | all-to-all | bytes 131072 | tf_op jit(solution)/shard_map/all_to_all | solution.py:435
  101.9 1.4 finish.1
  103.2 2.5 %fusion = f32[1,7,8192]{2,0,1:T(1,128)S(1)} fusion(f32[8,1,7,8192]{3,1,2,0:T(1,128)S(1)} %copy-done.6, f32[8,128]{1,0:T(8,128)S(1)} %get-tuple-element.98), kind=kOutput, calls=%fused_computation.1 | convolution fusion | flops 5505024 | bytes 2064896 | tf_op jit(solution)/shard_map/while/body/k,kvc->vc/dot_general | solution.py:448
  105.8 0.6 slice.40
  106.3 0.5 slice_bitcast_fusion
  106.8 0.8 multiply_reduce_fusion
  107.6 62.7 %psum.9 = f32[]{:T(128)} all-reduce(f32[]{:T(128)} %get-tuple-element.121), channel_id=1, replica_groups=mesh['z'=4,'xl'=2,'xh'=2,'y'=4,'core'=2] {'z','xl','xh','y','core'}, use_global_device_ids=true, to_apply=%region_1.2 | all-reduce | flops 1 | bytes 8 | tf_op jit(solution)/shard_map/while/body/psum | solution.py:449
  171.0 0.7 while.13
  171.7 1.9 %copy.35 = f32[1,7,8192]{2,0,1:T(1,128)} copy(f32[1,7,8192]{2,1,0:T(8,128)} %get-tuple-element.105) | data formatting | bytes 458752
  (38 shorter events, 1.2 us)
Async XLA Ops:
  6.0 0.9 copy-start.3
  6.9 29.6 %copy-start.10 = (s32[32,6]{0,1:T(8,128)S(1)}, s32[32,6]{0,1:T(8,128)}, u32[]{:S(2)}) copy-start(s32[32,6]{0,1:T(8,128)} %param.17) | copy-start | bytes 2308
  6.9 29.8 %copy-start.11 = (s32[32,6]{0,1:T(8,128)S(1)}, s32[32,6]{0,1:T(8,128)}, u32[]{:S(2)}) copy-start(s32[32,6]{0,1:T(8,128)} %param.18) | copy-start | bytes 2308
  6.9 30.1 %copy-start.12 = (s32[32]{0:T(128)S(1)}, s32[32]{0:T(128)}, u32[]{:S(2)}) copy-start(s32[32]{0:T(128)} %param.16) | copy-start | bytes 388
  6.9 19.0 %all-to-all-start = ((f32[8,12,8,256]{3,2,1,0:T(8,128)}), f32[8,12,8,256]{3,2,1,0:T(8,128)S(1)}, u32[]{:S(2)}, u32[]{:S(2)}) async-start(f32[8,12,8,256]{3,2,1,0:T(8,128)} %copy-done.3), calls=%async_computation | async-start | bytes 1572864 | tf_op jit(solution)/shard_map/all_to_all | solution.py:350
  14.5 14.7 %collective-permute-start.2 = (f32[7,4096]{1,0:T(8,128)S(1)}, f32[7,4096]{1,0:T(8,128)S(1)}, u32[]{:S(2)}, u32[]{:S(2)}) collective-permute-start(f32[7,4096]{1,0:T(8,128)S(1)} %get-tuple-element.94), channel_id=1, source_target_pairs={{0,16},{16,0},{1,17},{17,1},{2,18},{18,2},{3,19},{19,3},{4,20},{20... | collective-permute-start | bytes 344072 | tf_op jit(solution)/shard_map/ppermute | solution.py:355
  25.9 13.0 %collective-permute-start = (f32[8,12,8,256]{3,2,1,0:T(8,128)S(1)}, f32[8,12,8,256]{3,2,1,0:T(8,128)}, u32[]{:S(2)}, u32[]{:S(2)}) collective-permute-start(f32[8,12,8,256]{3,2,1,0:T(8,128)S(1)} %all-to-all-done.own_ref), channel_id=1, source_target_pairs={{0,1},{1,0},{2,3},{3,2},{4,5},{5,4},{6,7},{7,6},{8,9},{9,8},{10,11... | collective-permute-start | bytes 2359304 | tf_op jit(solution)/shard_map/ppermute | solution.py:351
  29.2 0.7 copy-start.8
  29.8 8.2 %copy-start.9 = (f32[8]{0:T(128)S(1)}, f32[8]{0:T(128)}, u32[]{:S(2)}) copy-start(f32[8]{0:T(128)} %constant.119.clone) | copy-start | bytes 100
  30.8 25.0 %copy-start.7 = (f32[7,4096]{1,0:T(8,128)}, f32[7,4096]{1,0:T(8,128)S(1)}, u32[]{:S(2)}) copy-start(f32[7,4096]{1,0:T(8,128)S(1)} %get-tuple-element.124) | copy-start | bytes 344068
  31.5 24.2 %collective-permute-start.3 = (f32[2,7,4096]{2,1,0:T(8,128)}, f32[2,7,4096]{2,1,0:T(8,128)}, u32[]{:S(2)}, u32[]{:S(2)}) collective-permute-start(f32[2,7,4096]{2,1,0:T(8,128)} %pad_maximum_fusion), channel_id=1, source_target_pairs={{0,32},{32,0},{64,96},{96,64},{1,33},{33,1},{65,97},{97,65},{2,34}... | collective-permute-start | bytes 688136 | tf_op jit(solution)/shard_map/ppermute | solution.py:360
  33.2 22.5 %collective-permute-start.4 = (f32[2,7,4096]{2,1,0:T(8,128)}, f32[2,7,4096]{2,1,0:T(8,128)}, u32[]{:S(2)}, u32[]{:S(2)}) collective-permute-start(f32[2,7,4096]{2,1,0:T(8,128)} %pad_maximum_fusion), channel_id=1, source_target_pairs={{0,64},{32,96},{64,0},{96,32},{1,65},{33,97},{65,1},{97,33},{2,66}... | collective-permute-start | bytes 688136 | tf_op jit(solution)/shard_map/ppermute | solution.py:360
  36.5 19.2 %collective-permute-start.5 = (f32[2,7,4096]{2,1,0:T(8,128)}, f32[2,7,4096]{2,1,0:T(8,128)}, u32[]{:S(2)}, u32[]{:S(2)}) collective-permute-start(f32[2,7,4096]{2,1,0:T(8,128)} %pad_maximum_fusion), channel_id=1, source_target_pairs={{0,96},{32,64},{64,32},{96,0},{1,97},{33,65},{65,33},{97,1},{2,98}... | collective-permute-start | bytes 688136 | tf_op jit(solution)/shard_map/ppermute | solution.py:360
  38.9 2.8 %copy-start = (bf16[1,7,7,7,8192]{4,3,2,1,0:T(8,128)(2,1)S(1)}, bf16[1,7,7,7,8192]{4,3,2,1,0:T(8,128)(2,1)}, u32[]{:S(2)}) copy-start(bf16[1,7,7,7,8192]{4,3,2,1,0:T(8,128)(2,1)} %coeff_ref.2) | copy-start | bytes 16859140
  50.8 0.9 copy-start.2
  51.7 25.0 %copy-start.4 = (f32[8192]{0:T(1024)S(1)}, f32[8192]{0:T(1024)}, u32[]{:S(2)}) copy-start(f32[8192]{0:T(1024)} %param.14) | copy-start | bytes 98308
  51.7 25.0 %copy-start.5 = (f32[8192]{0:T(1024)S(1)}, f32[8192]{0:T(1024)}, u32[]{:S(2)}) copy-start(f32[8192]{0:T(1024)} %param.15) | copy-start | bytes 98308
  51.7 13.9 %all-to-all-start.1 = ((f32[8,12,8,256]{3,2,1,0:T(8,128)}), f32[8,12,8,256]{3,2,1,0:T(8,128)S(1)}, u32[]{:S(2)}, u32[]{:S(2)}) async-start(f32[8,12,8,256]{3,2,1,0:T(8,128)} %copy-done.2), calls=%async_computation.1 | async-start | bytes 1572864 | tf_op jit(solution)/shard_map/all_to_all | solution.py:350
  62.7 14.0 %collective-permute-start.6 = (f32[7,4096]{1,0:T(8,128)}, f32[7,4096]{1,0:T(8,128)S(1)}, u32[]{:S(2)}, u32[]{:S(2)}) collective-permute-start(f32[7,4096]{1,0:T(8,128)} %bitcast_add_fusion), channel_id=1, source_target_pairs={{0,16},{16,0},{1,17},{17,1},{2,18},{18,2},{3,19},{19,3},{4,20},{20... | collective-permute-start | bytes 344072 | tf_op jit(solution)/shard_map/ppermute | solution.py:371
  65.6 11.0 %collective-permute-start.1 = (f32[8,12,8,256]{3,2,1,0:T(8,128)S(1)}, f32[8,12,8,256]{3,2,1,0:T(8,128)S(1)}, u32[]{:S(2)}, u32[]{:S(2)}) collective-permute-start(f32[8,12,8,256]{3,2,1,0:T(8,128)S(1)} %all-to-all-done.1.own_ref), channel_id=1, source_target_pairs={{0,1},{1,0},{2,3},{3,2},{4,5},{5,4},{6,7},{7,6},{8,9},{9,8},{10,11... | collective-permute-start | bytes 2359304 | tf_op jit(solution)/shard_map/ppermute | solution.py:351
  76.7 2.8 %copy-start.1 = (bf16[1,7,7,7,8192]{4,3,2,1,0:T(8,128)(2,1)S(1)}, bf16[1,7,7,7,8192]{4,3,2,1,0:T(8,128)(2,1)}, u32[]{:S(2)}) copy-start(bf16[1,7,7,7,8192]{4,3,2,1,0:T(8,128)(2,1)} %coeff_ref.3) | copy-start | bytes 16859140
  86.1 17.1 %copy-start.6 = (f32[8,1,7,8192]{3,1,2,0:T(1,128)S(1)}, f32[8,1,7,8192]{3,1,2,0:T(1,128)}, u32[]{:S(2)}) copy-start(f32[8,1,7,8192]{3,1,2,0:T(1,128)} %param.11) | copy-start | bytes 5505028

commit v2 on v0

v2 whole, which is shorter than its diff:
```python
import jax
import jax.numpy as jnp
import numpy as np
from jax import lax
from jax.experimental import pallas as pl
from jax.experimental.pallas import tpu as pltpu
from jax.sharding import Mesh, PartitionSpec as P

EDGE = 16
SQUARE = EDGE * EDGE
CUBE = EDGE * SQUARE
VARS = 7
KRYLOV = 8
INST = 8
BLOCKS = 32
SPACE = 16
CHIP_COUNT = 8
CELLS = 8192
PER = CELLS // CUBE
FACES = 6 * PER
SLABS = CELLS // SQUARE
ENTRIES = float(INST * VARS * CELLS * SPACE)
LANES = 128
GROUPS = CELLS // LANES
ROWS = VARS * GROUPS
ALL = ("z", "xl", "xh", "y", "core")
CHIPS = ("xh", "y")
VMEM = pltpu.VMEM
SMEM = pltpu.SMEM
GUARD = 0.02
CHUNK = 4


def mixing_weights():
    k = np.arange(1, INST)
    parity = np.where(k % 2 == 0, 1.0, -1.0)
    angle = np.pi * k / INST
    rest = 0.5 * parity / np.tan(angle) - 0.125 * parity / np.sin(angle) ** 2
    return [-0.25 * (INST * INST + 2) / 12.0] + [float(v) for v in rest]


def lanes(shape):
    return lax.broadcasted_iota(jnp.int32, shape, len(shape) - 1)


def sublanes(shape):
    return lax.broadcasted_iota(jnp.int32, shape, len(shape) - 2)


def pick(values, index):
    return jnp.take_along_axis(values, index, axis=1)


def fold(totals):
    row = sublanes(totals[0].shape)
    for width in (1, 2, 4):
        first = row % (2 * width) < width
        totals = [
            jnp.where(first, a, b) + pltpu.roll(jnp.where(first, b, a), width, 0)
            for a, b in zip(totals[::2], totals[1::2])
        ]
    return totals[0]


def strips_of(slab, x, strips):
    lane = lanes((8, LANES))
    low, high = (slab[:, :LANES], slab[:, LANES:])
    own = lane // EDGE == x
    upper = lane % EDGE >= 8
    source = lane % 8 * EDGE
    found = (
        pick(low, lane % EDGE),
        pick(high, lane % EDGE + (LANES - EDGE)),
        jnp.where(upper, pick(high, source), pick(low, source)),
        jnp.where(upper, pick(high, source + 15), pick(low, source + 15)),
    )
    if strips is None:
        return list(found)
    return [jnp.where(own, new, old) for new, old in zip(found, strips)]


def store_strips(faces, block, half, strips):
    for number, strip in enumerate(strips):
        faces[block * 6 + 2 + number, :, half * LANES : (half + 1) * LANES] = strip


def send_faces(faces, sent_ref, arrived):
    copies = [
        pltpu.make_async_copy(faces, sent_ref.at[chip], arrived.at[chip]) for chip in range(CHIP_COUNT)
    ]
    for copy in copies:
        copy.start()
    for copy in copies:
        copy.wait()


def first_faces_kernel(basis_ref, sent_ref, padded_ref, dense_ref, field, faces, arrived):
    fetch = pltpu.make_async_copy(
        basis_ref.at[pl.ds((KRYLOV - 1) * ROWS, ROWS)], field.at[pl.ds(0, ROWS)], arrived.at[0]
    )
    fetch.start()
    field[ROWS:] = jnp.zeros((GROUPS, LANES), jnp.float32)
    fetch.wait()
    dense_ref[...] = field[:ROWS]
    for block in range(PER):
        for half in range(2):
            strips = None
            for inner in range(8):
                k = block * EDGE + half * 8 + inner
                slab = jnp.concatenate(
                    [field[pl.ds(2 * k, 8, stride=GROUPS), :], field[pl.ds(2 * k + 1, 8, stride=GROUPS), :]],
                    axis=1,
                )
                padded_ref[:, k * SQUARE : (k + 1) * SQUARE] = slab
                strips = strips_of(slab, inner, strips)
                if half == 0 and inner == 0:
                    faces[block * 6] = slab
                if half == 1 and inner == 7:
                    faces[block * 6 + 1] = slab
            store_strips(faces, block, half, strips)
    send_faces(faces, sent_ref, arrived)


def tables_kernel(ids_ref, neighbour_ref, orient_ref, table_ref, position):
    core = lax.axis_index("core")
    rank = (lax.axis_index("xh") * 4 + lax.axis_index("y")) * 2 + core

    def place(slot, carry):
        position[ids_ref[slot]] = slot
        return carry

    lax.fori_loop(0, BLOCKS, place, 0)
    for number in range(FACES):
        owner = ids_ref[rank * PER + number // 6]
        partner = neighbour_ref[number % 6, owner]
        code = orient_ref[number % 6, owner]
        target = jnp.maximum(partner, 0)
        slot = position[target // 6]
        device = slot // PER
        table_ref[number * 4] = device // 2
        table_ref[number * 4 + 1] = jnp.where(device % 2 == core, 1, 0)
        table_ref[number * 4 + 2] = (slot % PER) * 6 + target % 6
        table_ref[number * 4 + 3] = jnp.where(partner < 0, -1, code)


def fetch_halos(table_ref, own_ref, swapped_ref, halos):
    lane = lanes((8, LANES))
    for number in range(FACES):
        chip = table_ref[number * 4]
        here = table_ref[number * 4 + 1] == 1
        row = table_ref[number * 4 + 2]
        code = table_ref[number * 4 + 3]
        wall = code < 0
        code = jnp.maximum(code, 0)
        source = jnp.where(here, own_ref[chip, row], swapped_ref[chip, row])
        source = jnp.where(wall, 0.0, source)
        low, high = (source[:, :LANES], source[:, LANES:])
        transposed = code % 2 == 1
        flip_a = code // 2 % 2 * (EDGE - 1)
        flip_b = code // 4 * (EDGE - 1)
        for half in range(2):
            a = (lane // EDGE + half * 8) ^ flip_a
            b = (lane % EDGE) ^ flip_b
            index = jnp.where(transposed, b * EDGE + a, a * EDGE + b)
            inside = index % LANES
            halos[number, :, half * LANES : (half + 1) * LANES] = jnp.where(
                index < LANES, pick(low, inside), pick(high, inside)
            )


def inner_kernel(field_ref, coeff_ref, part_ref, across_z_ref, across_y_ref, across_x_ref):
    column = lanes((8, SQUARE))
    z = column % EDGE
    below_zero = jnp.zeros((1, SQUARE), jnp.float32)

    def coeff(s, o, inner):
        value = coeff_ref[0, s, o, :, inner * SQUARE : (inner + 1) * SQUARE].astype(jnp.float32)
        return jnp.concatenate([value, below_zero], axis=0)

    def load(k):
        return field_ref[:, pl.ds(pl.multiple_of(k * SQUARE, SQUARE), SQUARE)]

    for inner in range(CHUNK):
        k = pl.program_id(0) * CHUNK + inner
        block, x = (k // EDGE, k % EDGE)
        place = slice(inner * SQUARE, (inner + 1) * SQUARE)
        centre = load(k)
        operands = [
            centre,
            jnp.where(x == 0, 0.0, load(jnp.maximum(k - 1, 0))),
            jnp.where(x == EDGE - 1, 0.0, load(jnp.minimum(k + 1, SLABS - 1))),
            jnp.where(column < EDGE, 0.0, pltpu.roll(centre, EDGE, 1)),
            jnp.where(column >= SQUARE - EDGE, 0.0, pltpu.roll(centre, SQUARE - EDGE, 1)),
            jnp.where(z == 0, 0.0, pltpu.roll(centre, 1, 1)),
            jnp.where(z == EDGE - 1, 0.0, pltpu.roll(centre, SQUARE - 1, 1)),
        ]
        totals = []
        for o in range(VARS):
            values = [coeff(s, o, inner) for s in range(7)]
            total = values[0] * operands[0]
            for s in range(1, 7):
                total = total + values[s] * operands[s]
            totals.append(total)
            across_z_ref[o, :, place] = jnp.where(
                z == 0, values[5], jnp.where(z == EDGE - 1, values[6], 0.0)
            )
            across_y_ref[o, :, place] = jnp.where(
                column < EDGE, values[3], jnp.where(column >= SQUARE - EDGE, values[4], 0.0)
            )
        part_ref[:, place] = fold(totals + [jnp.zeros((8, SQUARE), jnp.float32)])

        if inner == 0:

            @pl.when(x == 0)
            def _():
                for o in range(VARS):
                    across_x_ref[block * 2, o] = coeff(1, o, inner)

        if inner == CHUNK - 1:

            @pl.when(x == EDGE - 1)
            def _():
                for o in range(VARS):
                    across_x_ref[block * 2 + 1, o] = coeff(2, o, inner)


def outer_slab(part_ref, across_z_ref, across_y_ref, halos, block, half, inner):
    lane = lanes((8, LANES))
    offset = inner * EDGE
    place = pl.ds(pl.multiple_of(block * CUBE + (half * 8 + inner) * SQUARE, SQUARE), SQUARE)
    start = half * LANES

    def strip(face):
        return halos[block * 6 + face, :, start : start + LANES]

    y = lane % EDGE + offset
    z = lane // EDGE + offset
    at_low = lane % EDGE == 0
    across_y = jnp.concatenate([pick(strip(2), y), pick(strip(3), y)], axis=1)
    z_low, z_high = (strip(4), strip(5))
    across_z = jnp.concatenate(
        [
            jnp.where(at_low, pick(z_low, z), pick(z_high, z)),
            jnp.where(at_low, pick(z_low, z + 8), pick(z_high, z + 8)),
        ],
        axis=1,
    )
    totals = [
        across_z_ref[o, :, place] * across_z + across_y_ref[o, :, place] * across_y for o in range(VARS)
    ]
    return part_ref[:, place] + fold(totals + [jnp.zeros((8, SQUARE), jnp.float32)])


def outer_x(across_x_ref, halos, block, side):
    halo = halos[block * 6 + side]
    totals = [across_x_ref[block * 2 + side, o] * halo for o in range(VARS)]
    return fold(totals + [jnp.zeros((8, SQUARE), jnp.float32)])


def outer_blocks(across_x_ref, part_ref, across_z_ref, across_y_ref, halos, each):
    for block in range(PER):
        for half in range(2):
            for inner in range(8):
                slab = outer_slab(part_ref, across_z_ref, across_y_ref, halos, block, half, inner)
                if half == 0 and inner == 0:
                    slab = slab + outer_x(across_x_ref, halos, block, 0)
                if half == 1 and inner == 7:
                    slab = slab + outer_x(across_x_ref, halos, block, 1)
                each(block, half, inner, slab)


def flux_kernel(
    table_ref, own_ref, swapped_ref, part_ref, across_z_ref, across_y_ref, across_x_ref,
    first_ref, sent_ref, halos, faces, arrived
):
    fetch_halos(table_ref, own_ref, swapped_ref, halos)
    held = {}

    def each(block, half, inner, slab):
        k = block * EDGE + half * 8 + inner
        first_ref[:, k * SQUARE : (k + 1) * SQUARE] = slab
        held["strips"] = strips_of(slab, inner, held["strips"] if inner else None)
        if half == 0 and inner == 0:
            faces[block * 6] = slab
        if half == 1 and inner == 7:
            faces[block * 6 + 1] = slab
        if inner == 7:
            store_strips(faces, block, half, held["strips"])

    outer_blocks(across_x_ref, part_ref, across_z_ref, across_y_ref, halos, each)
    send_faces(faces, sent_ref, arrived)


def mix_kernel(own_ref, one_ref, two_ref, three_ref, kept_ref, given_ref):
    z = lax.axis_index("z")
    xl = lax.axis_index("xl")
    table = mixing_weights()

    def weight(offset):
        offset = lax.rem(offset + 2 * INST, INST)
        value = jnp.float32(table[0])
        for k in range(1, INST):
            value = jnp.where(offset == k, jnp.float32(table[k]), value)
        return value

    fields = (own_ref, one_ref, two_ref, three_ref)
    sources = [2 * (z ^ k) + xl for k in range(4)]
    kept = [weight(source - (2 * z + xl)) for source in sources]
    given = [weight(source - (2 * z + 1 - xl)) for source in sources]

    def step(k, carry):
        rows = pl.ds(pl.multiple_of(k * 64, 64), 64)
        values = [field[rows] for field in fields]
        kept_ref[rows] = sum(w * v for w, v in zip(kept, values))
        given_ref[rows] = sum(w * v for w, v in zip(given, values))
        return carry

    lax.fori_loop(0, ROWS // 64, step, 0)


def lane_sums(rows, first_lane):
    totals = jnp.broadcast_to(jnp.sum(rows, axis=1, keepdims=True), rows.shape)
    spot = lanes(rows.shape) == sublanes(rows.shape) + first_lane
    return jnp.sum(jnp.where(spot, totals, 0.0), axis=0, keepdims=True)


def gram_kernel(basis_ref, gram_ref, lines):
    def step(k, totals):
        fields = [
            basis_ref[pl.ds(pl.multiple_of(j * ROWS + k * 8, 8), 8)] for j in range(KRYLOV)
        ]
        out = []
        for i in range(KRYLOV):
            for j in range(i, KRYLOV):
                out.append(totals[len(out)] + fields[i] * fields[j])
        return tuple(out)

    zero = jnp.zeros((8, LANES), jnp.float32)
    totals = lax.fori_loop(0, ROWS // 8, step, (zero,) * (KRYLOV * (KRYLOV + 1) // 2))
    number = 0
    for i in range(KRYLOV):
        for j in range(i, KRYLOV):
            line = jnp.sum(totals[number], axis=0, keepdims=True)
            lines[i * KRYLOV + j : i * KRYLOV + j + 1] = line
            lines[j * KRYLOV + i : j * KRYLOV + i + 1] = line
            number += 1
    gram_ref[...] = jnp.broadcast_to(lane_sums(lines[...], 64), (8, LANES))


def image_kernel(
    table_ref, own_ref, swapped_ref, part_ref, across_z_ref, across_y_ref, across_x_ref,
    basis_ref, pseudo_ref, omega_ref, kept_ref, returned_ref, gram_ref,
    image_ref, sums_ref, halos, section
):
    fetch_halos(table_ref, own_ref, swapped_ref, halos)

    def each(block, half, inner, slab):
        k = block * EDGE + half * 8 + inner
        section[pl.ds(2 * k, 8, stride=GROUPS), :] = slab[:, :LANES]
        section[pl.ds(2 * k + 1, 8, stride=GROUPS), :] = slab[:, LANES:]

    outer_blocks(across_x_ref, part_ref, across_z_ref, across_y_ref, halos, each)

    def step(k, totals):
        start = k * 8
        cells = pl.ds(pl.multiple_of(start % GROUPS, 8), 8)
        rows = pl.ds(pl.multiple_of(start, 8), 8)
        fields = [basis_ref[pl.ds(pl.multiple_of(j * ROWS + start, 8), 8)] for j in range(KRYLOV)]
        spectral = kept_ref[rows] + returned_ref[rows]
        image = pseudo_ref[cells] * fields[KRYLOV - 1] + section[rows] + omega_ref[cells] * spectral
        image_ref[rows] = image
        return tuple(total + field * image for total, field in zip(totals, fields + [image]))

    zero = jnp.zeros((8, LANES), jnp.float32)
    totals = lax.fori_loop(0, ROWS // 8, step, (zero,) * (KRYLOV + 1), unroll=8)
    lines = [jnp.sum(total, axis=0, keepdims=True) for total in totals]
    lines += [jnp.zeros((16 - len(lines), LANES), jnp.float32)]
    sums = jnp.broadcast_to(lane_sums(jnp.concatenate(lines, axis=0), 0), (8, LANES)) + gram_ref[...]
    for group in range(16):
        sums_ref[group * 8 : group * 8 + 8] = sums


def finish_kernel(received_ref, image_ref, basis_ref, next_ref, column_ref):
    sums = jnp.sum(received_ref[...], axis=0, keepdims=True)
    sums = jnp.broadcast_to(sums, (8, LANES)) / ENTRIES
    lane = lanes((8, LANES))
    left = pick(sums, jnp.maximum(lane - 64, 0) // 8)
    right = pick(sums, lane % 8)
    quadratic = jnp.sum(jnp.where(lane >= 64, sums * left * right, 0.0), axis=1, keepdims=True)
    linear = jnp.sum(jnp.where(lane < KRYLOV, sums * sums, 0.0), axis=1, keepdims=True)
    whole_square = sums[:, KRYLOV : KRYLOV + 1]
    squares = whole_square - 2.0 * linear + quadratic
    size = whole_square + 2.0 * linear + jnp.abs(quadratic)
    norm = jnp.sqrt(jnp.maximum(squares, 0.0) + 1e-06)
    column = jnp.where(lane < KRYLOV, sums, jnp.where(lane == KRYLOV, norm, 0.0))
    column_ref[...] = jnp.where(lane == KRYLOV + 1, jnp.where(squares < GUARD * size, 1.0, 0.0), column)
    coeffs = [jnp.broadcast_to(sums[:, j : j + 1], (8, LANES)) for j in range(KRYLOV)]
    scale = jnp.broadcast_to(1.0 / norm, (8, LANES))

    def step(k, carry):
        start = k * 8
        rows = pl.ds(pl.multiple_of(start, 8), 8)
        ortho = image_ref[rows]
        for j in range(KRYLOV):
            ortho = ortho - coeffs[j] * basis_ref[pl.ds(pl.multiple_of(j * ROWS + start, 8), 8)]
        next_ref[rows] = ortho * scale
        return carry

    lax.fori_loop(0, ROWS // 8, step, 0, unroll=8)


def whole(memory=VMEM):
    return pl.BlockSpec(memory_space=memory)


def f32(*shape):
    return jax.ShapeDtypeStruct(shape, jnp.float32)


def params(mib):
    return pltpu.CompilerParams(vmem_limit_bytes=mib * 2**20)


def cost(flops, moved):
    return pl.CostEstimate(flops=flops, bytes_accessed=moved, transcendentals=0)


def swap(size, bit):
    return [(i, i ^ bit) for i in range(size)]


def exchange(sent):
    own = lax.all_to_all(sent, CHIPS, 0, 0)
    return own, lax.ppermute(own, "core", swap(2, 1))


FACES_VMEM = VMEM((FACES, 8, SQUARE), jnp.float32)
SENT = f32(CHIP_COUNT, FACES, 8, SQUARE)


def inner_section(field, coeff, name):
    width = CHUNK * SQUARE
    return pl.pallas_call(
        inner_kernel,
        grid=(SLABS // CHUNK,),
        in_specs=[
            pl.BlockSpec((8, CELLS), lambda i: (0, 0)),
            pl.BlockSpec((1, 7, VARS, VARS, width), lambda i: (0, 0, 0, 0, i)),
        ],
        out_specs=[
            pl.BlockSpec((8, width), lambda i: (0, i)),
            pl.BlockSpec((VARS, 8, width), lambda i: (0, 0, i)),
            pl.BlockSpec((VARS, 8, width), lambda i: (0, 0, i)),
            pl.BlockSpec((2 * PER, VARS, 8, SQUARE), lambda i: (0, 0, 0, 0)),
        ],
        out_shape=[f32(8, CELLS), f32(VARS, 8, CELLS), f32(VARS, 8, CELLS), f32(2 * PER, VARS, 8, SQUARE)],
        compiler_params=params(16),
        cost_estimate=cost(2 * 343 * CELLS, 10 * 2**20),
        name=name,
    )(field, coeff)


def mix(dense):
    parts = [dense] + [lax.ppermute(dense, "z", swap(4, k)) for k in (1, 2, 3)]
    kept, given = pl.pallas_call(
        mix_kernel,
        in_specs=[whole()] * 4,
        out_specs=[whole()] * 2,
        out_shape=[f32(ROWS, LANES)] * 2,
        compiler_params=params(8),
        cost_estimate=cost(16 * ROWS * LANES, 6 * 4 * ROWS * LANES),
        name="mix",
    )(*parts)
    return kept, lax.ppermute(given, "xl", swap(2, 1))


def local(basis, flux, recon, pseudo_time, vol_omega, block_ids, neighbour, orient):
    flat = basis.reshape(KRYLOV * ROWS, LANES)
    sent, padded, dense = pl.pallas_call(
        first_faces_kernel,
        in_specs=[whole(pl.ANY)],
        out_specs=[whole(pl.ANY), whole(), whole()],
        out_shape=[SENT, f32(8, CELLS), f32(ROWS, LANES)],
        scratch_shapes=[VMEM((8 * GROUPS, LANES), jnp.float32), FACES_VMEM, pltpu.SemaphoreType.DMA((CHIP_COUNT,))],
        compiler_params=params(8),
        cost_estimate=cost(10**6, 2 * 2**20),
        name="first_faces",
    )(flat)
    own, swapped = exchange(sent)
    table = pl.pallas_call(
        tables_kernel,
        in_specs=[whole(SMEM)] * 3,
        out_specs=whole(SMEM),
        out_shape=jax.ShapeDtypeStruct((4 * FACES,), jnp.int32),
        scratch_shapes=[SMEM((BLOCKS,), jnp.int32)],
        compiler_params=params(4),
        cost_estimate=cost(10**5, 10**5),
        name="tables",
    )(block_ids, neighbour.T, orient.T)
    kept, returned = mix(dense)
    gram = pl.pallas_call(
        gram_kernel,
        in_specs=[whole()],
        out_specs=whole(),
        out_shape=f32(8, LANES),
        scratch_shapes=[VMEM((KRYLOV * KRYLOV, LANES), jnp.float32)],
        compiler_params=params(8),
        cost_estimate=cost(2 * 36 * VARS * CELLS, 2 * 2**20),
        name="gram",
    )(flat)
    pieces = inner_section(padded, flux, "flux_inner")
    first, sent = pl.pallas_call(
        flux_kernel,
        in_specs=[whole(SMEM)] + [whole()] * 6,
        out_specs=[whole(), whole(pl.ANY)],
        out_shape=[f32(8, CELLS), SENT],
        scratch_shapes=[FACES_VMEM, FACES_VMEM, pltpu.SemaphoreType.DMA((CHIP_COUNT,))],
        compiler_params=params(16),
        cost_estimate=cost(10**6, 4 * 2**20),
        name="flux_outer",
    )(table, own, swapped, *pieces)
    own, swapped = exchange(sent)
    pieces = inner_section(first, recon, "recon_inner")
    image, sums = pl.pallas_call(
        image_kernel,
        in_specs=[whole(SMEM)] + [whole()] * 12,
        out_specs=[whole(), whole()],
        out_shape=[f32(ROWS, LANES), f32(LANES, LANES)],
        scratch_shapes=[FACES_VMEM, VMEM((8 * GROUPS, LANES), jnp.float32)],
        compiler_params=params(16),
        cost_estimate=cost(10**6, 6 * 2**20),
        name="image",
    )(
        table, own, swapped, *pieces,
        flat, pseudo_time.reshape(GROUPS, LANES), vol_omega.reshape(GROUPS, LANES), kept, returned, gram,
    )
    received = lax.all_to_all(sums, ALL, 0, 0)
    following, column = pl.pallas_call(
        finish_kernel,
        in_specs=[whole()] * 3,
        out_specs=[whole(), whole()],
        out_shape=[f32(ROWS, LANES), f32(8, LANES)],
        compiler_params=params(8),
        cost_estimate=cost(10**6, 3 * 2**20),
        name="finish",
    )(received, image, flat)

    def direct(state):
        coeffs = state[1][:KRYLOV]
        ortho = image - jnp.einsum(
            "k,krl->rl", coeffs, flat.reshape(KRYLOV, ROWS, LANES), precision=lax.Precision.HIGHEST
        )
        squares = lax.psum(jnp.sum(ortho * ortho), ALL) / ENTRIES
        norm = jnp.sqrt(squares + 1e-06)
        return (ortho / norm, jnp.concatenate([coeffs, norm[None], jnp.zeros((1,), jnp.float32)]))

    following, hessenberg = lax.while_loop(
        lambda state: state[1][KRYLOV + 1] > 0.5, direct, (following, column[0, : KRYLOV + 2])
    )
    return following.reshape(1, VARS, CELLS), hessenberg[: KRYLOV + 1]


def solution(mesh):
    fine = Mesh(mesh.devices.reshape(4, 2, 2, 4, 2), ALL)
    inst, space = (("z", "xl"), ("xh", "y", "core"))
    placed = (
        P(None, inst, None, space),
        P(inst, None, None, None, space),
        P(inst, None, None, None, space),
        P(space),
        P(space),
        P(),
        P(),
        P(),
    )
    return jax.shard_map(
        local,
        mesh=fine,
        in_specs=placed,
        out_specs=(P(inst, None, space), P()),
        check_vma=False,
    )
```

time: 326 us -> 100 us (0.31)
  waiting for transfers between devices: 114 us -> 13.5 us
  blocking collectives: 129 us -> 51 us
  local copies, waits for them, and re-layouts: 36 us -> 4.61 us
  other arithmetic: 23.3 us -> 0.01 us
  Pallas kernels: 0 us -> 19.8 us
  between operations: 15.4 us -> 0.78 us
  starting transfers between devices: 0.12 us -> 9.52 us
  matrix products: 7.25 us -> 0 us
    psum x2 -> x0, blocking collectives: 129 us -> none  [the longest x1 64.8 us: local(): coeffs = lax.psum(partial_dots, ('inst', 'space')) / entries]
    all_gather x3 -> x0, waiting for transfers between devices: 114 us -> none  [the longest x2 89.2 us: section(): all_faces = lax.all_gather(faces, 'space', axis=0, tiled=True)]
    all_to_all x0 -> x3, blocking collectives: none -> 51 us  [the longest x2 36 us: exchange(): own = lax.all_to_all(sent, CHIPS, 0, 0)]
    pallas_call x0 -> x9, Pallas kernels: none -> 19.8 us  [the longest x2 6.46 us: inner_section(): pl.pallas_call(inner_kernel, grid=(SLABS // CHUNK,), in_specs=[pl.BlockSp...]
    reduce_sum x8 -> x0, other arithmetic: 17 us -> none  [the longest x2 12.4 us: apply_section(): jnp.sum(coeffs[stencil_pos].astype(jnp.float32) * values[None], axis=1)]
    ppermute x0 -> x6, waiting for transfers between devices: none -> 13.5 us  [the longest x3 12.7 us: mix(): parts = [dense] + [lax.ppermute(dense, 'z', swap(4, k)) for k in (1, 2, 3)]]
    ppermute x0 -> x6, starting transfers between devices: none -> 9.52 us  [the longest x3 4.94 us: mix(): parts = [dense] + [lax.ppermute(dense, 'z', swap(4, k)) for k in (1, 2, 3)]]
    reshape x18 -> x0, local copies, waits for them, and re-layouts: 8.8 us -> none  [the longest x2 3.56 us: neighbour_fields(): jnp.repeat(halos[5].reshape(grid_shape), edge, axis=3)]
  transfers between devices with their start and end apart: 3 -> 6, of which waited for: 3 -> 4; matrix products, arithmetic and copies ran while one was open for 10% -> 0% of each run, Pallas kernels for 0% -> 10%
where the time goes in v2:
time: 100 us; the launch traced here: 99.7 us
  blocking collectives  51 us (51%)
  Pallas kernels  19.8 us (20%)
  waiting for transfers between devices  13.5 us (14%)
  starting transfers between devices  9.52 us (10%)
  local copies, waits for them, and re-layouts  4.61 us (5%)
    all_to_all x2, blocking collectives, exchange(): own = lax.all_to_all(sent, CHIPS, 0, 0)  36 us
    all_to_all x1, blocking collectives, local(): received = lax.all_to_all(sums, ALL, 0, 0)  15 us
    ppermute x3, waiting for transfers between devices, mix(): parts = [dense] + [lax.ppermute(dense, 'z', swap(4, k)) for k in (1, 2, 3)]  12.7 us
    pallas_call x2, Pallas kernels, inner_section(): pl.pallas_call(inner_kernel, grid=(SLABS // CHUNK,), in_specs=[pl.BlockSp...  6.46 us
    ppermute x3, starting transfers between devices, mix(): parts = [dense] + [lax.ppermute(dense, 'z', swap(4, k)) for k in (1, 2, 3)]  4.94 us
    pallas_call x1, Pallas kernels, local(): pl.pallas_call(flux_kernel, in_specs=[whole(SMEM)] + [whole()] * 6, out_s...  4.49 us
    ppermute x2, starting transfers between devices, exchange(): return (own, lax.ppermute(own, 'core', swap(2, 1)))  4.18 us
    unnamed x18, local copies, waits for them, and re-layouts  2.86 us
  transfers between devices with their start and end apart: 6, of which 4 were waited for; matrix products, arithmetic and copies ran while one was open for 0% of the time, Pallas kernels for 10%

profile of v2, /device:TPU:1, one launch (start us, length us, event | category | flops | bytes accessed | tf_op | source)
XLA Modules:
  0.0 99.7 jit_solution(1238486514428135619)
XLA Ops:
  0.7 2.7 %first_faces.1 = (f32[8,12,8,256]{3,2,1,0:T(8,128)S(1)}, f32[8,8192]{1,0:T(8,128)S(1)}, f32[448,128]{1,0:T(8,128)S(1)}) custom-call(f32[3584,128]{1,0:T(8,128)} %bitcast.41), custom_call_target="tpu_custom_call" | custom-call | flops 1000000 | bytes 2097152 | tf_op jit(solution)/shard_map/first_faces/pallas_call | solution.py:479
  3.3 20.1 %all_to_all.21.own_ref = f32[8,12,8,256]{3,2,1,0:T(8,128)S(1)} all-to-all(f32[8,12,8,256]{3,2,1,0:T(8,128)S(1)} %get-tuple-element.43), channel_id=1, replica_groups=mesh['z'=4,'xl'=2,'xh'=2,'y'=4,'core'=2] {'xh','y'}, dimensions={0} | all-to-all | bytes 1572864 | tf_op jit(solution)/shard_map/all_to_all | solution.py:433
  23.4 2.5 %collective-permute-start = (f32[8,12,8,256]{3,2,1,0:T(8,128)S(1)}, f32[8,12,8,256]{3,2,1,0:T(8,128)S(1)}, u32[]{:S(2)}, u32[]{:S(2)}) collective-permute-start(f32[8,12,8,256]{3,2,1,0:T(8,128)S(1)} %all_to_all.21.own_ref), channel_id=1, source_target_pairs={{0,1},{1,0},{2,3},{3,2},{4,5},{5,4},{6,7},{7,6},{8,9},{9,8},{10,11... | collective-permute-start | bytes 2359304 | tf_op jit(solution)/shard_map/ppermute | solution.py:434
  25.9 1.8 %tables.1.table_ref = s32[48]{0:T(128)S(1)} custom-call(s32[32]{0:T(128)S(1)} %copy-done.5, s32[6,32]{1,0:T(8,128)S(1)} %bitcast.39, s32[6,32]{1,0:T(8,128)S(1)} %bitcast.40), custom_call_target="tpu_custom_call" | custom-call | flops 100000 | bytes 100000 | tf_op jit(solution)/shard_map/tables/pallas_call | solution.py:490
  27.7 0.0 copy-start
  27.8 2.8 %copy-done = bf16[1,7,7,7,8192]{4,3,2,1,0:T(8,128)(2,1)S(1)} copy-done((bf16[1,7,7,7,8192]{4,3,2,1,0:T(8,128)(2,1)S(1)}, bf16[1,7,7,7,8192]{4,3,2,1,0:T(8,128)(2,1)}, u32[]{:S(2)}) %copy-start) | copy-done | bytes 5619736
  30.6 3.2 %flux_inner.1 = (f32[8,8192]{1,0:T(8,128)S(1)}, f32[7,8,8192]{2,1,0:T(8,128)S(1)}, f32[7,8,8192]{2,1,0:T(8,128)S(1)}, f32[4,7,8,256]{3,2,1,0:T(8,128)S(1)}) custom-call(f32[8,8192]{1,0:T(8,128)S(1)} %get-tuple-element.44.field_ref, bf16[1,7,7,7,8192]{4,3,2,1,0:T(8,128)(2,1)S(1)} %copy-done), custom_call_target="tpu_custom_call" | custom-call | flops 5619712 | bytes 10485760 | tf_op jit(solution)/shard_map/flux_inner/pallas_call | solution.py:443
  33.8 0.0 collective-permute-done.swapped_ref
  33.8 0.0 slice-start.1
  33.8 4.5 %flux_outer.1 = (f32[8,8192]{1,0:T(8,128)S(1)}, f32[8,12,8,256]{3,2,1,0:T(8,128)S(1)}) custom-call(s32[48]{0:T(128)S(1)} %tables.1.table_ref, f32[8,12,8,256]{3,2,1,0:T(8,128)S(1)} %all_to_all.21.own_ref, f32[8,12,8,256]{3,2,1,0:T(8,128)S(1)} %collective-permute-done.swapped_ref, f32[8,8192]{1,0:T(8,128)S(1)} %get-tuple-element.45.part_ref, ...), custom_call_target="tpu_custom_call" | custom-call | flops 1000000 | bytes 4194304 | tf_op jit(solution)/shard_map/flux_outer/pallas_call | solution.py:512
  38.3 0.0 copy-start.6
  38.3 15.9 %all_to_all.22.own_ref = f32[8,12,8,256]{3,2,1,0:T(8,128)S(1)} all-to-all(f32[8,12,8,256]{3,2,1,0:T(8,128)S(1)} %get-tuple-element.49), channel_id=1, replica_groups=mesh['z'=4,'xl'=2,'xh'=2,'y'=4,'core'=2] {'xh','y'}, dimensions={0} | all-to-all | bytes 1572864 | tf_op jit(solution)/shard_map/all_to_all | solution.py:433
  54.3 1.7 %collective-permute-start.1 = (f32[8,12,8,256]{3,2,1,0:T(8,128)S(1)}, f32[8,12,8,256]{3,2,1,0:T(8,128)S(1)}, u32[]{:S(2)}, u32[]{:S(2)}) collective-permute-start(f32[8,12,8,256]{3,2,1,0:T(8,128)S(1)} %all_to_all.22.own_ref), channel_id=1, source_target_pairs={{0,1},{1,0},{2,3},{3,2},{4,5},{5,4},{6,7},{7,6},{8,9},{9,8},{10,11... | collective-permute-start | bytes 2359304 | tf_op jit(solution)/shard_map/ppermute | solution.py:434
  55.9 1.6 %collective-permute-start.2 = (f32[448,128]{1,0:T(8,128)S(1)}, f32[448,128]{1,0:T(8,128)S(1)}, u32[]{:S(2)}, u32[]{:S(2)}) collective-permute-start(f32[448,128]{1,0:T(8,128)S(1)} %get-tuple-element.55.own_ref), channel_id=1, source_target_pairs={{0,32},{32,0},{64,96},{96,64},{1,33},{33,1},{65,97},{97,65},{2,34}... | collective-permute-start | bytes 688136 | tf_op jit(solution)/shard_map/ppermute | solution.py:464
  57.6 3.3 %collective-permute-start.3 = (f32[448,128]{1,0:T(8,128)S(1)}, f32[448,128]{1,0:T(8,128)S(1)}, u32[]{:S(2)}, u32[]{:S(2)}) collective-permute-start(f32[448,128]{1,0:T(8,128)S(1)} %get-tuple-element.55.own_ref), channel_id=1, source_target_pairs={{0,64},{32,96},{64,0},{96,32},{1,65},{33,97},{65,1},{97,33},{2,66}... | collective-permute-start | bytes 688136 | tf_op jit(solution)/shard_map/ppermute | solution.py:464
  60.9 0.0 collective-permute-start.4
  60.9 2.6 %collective-permute-done.2.one_ref = f32[448,128]{1,0:T(8,128)S(1)} collective-permute-done((f32[448,128]{1,0:T(8,128)S(1)}, f32[448,128]{1,0:T(8,128)S(1)}, u32[]{:S(2)}, u32[]{:S(2)}) %collective-permute-start.2) | collective-permute-done | bytes 229408 | tf_op jit(solution)/shard_map/ppermute | solution.py:464
  63.4 8.2 %collective-permute-done.3.two_ref = f32[448,128]{1,0:T(8,128)S(1)} collective-permute-done((f32[448,128]{1,0:T(8,128)S(1)}, f32[448,128]{1,0:T(8,128)S(1)}, u32[]{:S(2)}, u32[]{:S(2)}) %collective-permute-start.3) | collective-permute-done | bytes 229408 | tf_op jit(solution)/shard_map/ppermute | solution.py:464
  71.6 2.0 %collective-permute-done.4.three_ref = f32[448,128]{1,0:T(8,128)S(1)} collective-permute-done((f32[448,128]{1,0:T(8,128)S(1)}, f32[448,128]{1,0:T(8,128)S(1)}, u32[]{:S(2)}, u32[]{:S(2)}) %collective-permute-start.4) | collective-permute-done | bytes 229408 | tf_op jit(solution)/shard_map/ppermute | solution.py:464
  73.6 0.1 mix.1
  73.7 0.4 collective-permute-start.5
  74.1 1.3 %gram.1.gram_ref = f32[8,128]{1,0:T(8,128)S(1)} custom-call(f32[3584,128]{1,0:T(8,128)S(1)} %bitcast.42), custom_call_target="tpu_custom_call" | custom-call | flops 4128768 | bytes 2097152 | tf_op jit(solution)/shard_map/gram/pallas_call | solution.py:501
  75.5 0.0 copy-start.1
  75.5 0.0 copy-start.2
  75.5 3.2 %recon_inner.1 = (f32[8,8192]{1,0:T(8,128)S(1)}, f32[7,8,8192]{2,1,0:T(8,128)S(1)}, f32[7,8,8192]{2,1,0:T(8,128)S(1)}, f32[4,7,8,256]{3,2,1,0:T(8,128)S(1)}) custom-call(f32[8,8192]{1,0:T(8,128)S(1)} %get-tuple-element.50.field_ref, bf16[1,7,7,7,8192]{4,3,2,1,0:T(8,128)(2,1)S(1)} %bitcast.34), custom_call_target="tpu_custom_call" | custom-call | flops 5619712 | bytes 10485760 | tf_op jit(solution)/shard_map/recon_inner/pallas_call | solution.py:443
  78.7 0.7 collective-permute-done.5.returned_ref
  79.5 1.8 %image.1 = (f32[448,128]{1,0:T(8,128)S(1)}, f32[128,128]{1,0:T(8,128)S(1)}) custom-call(s32[48]{0:T(128)S(1)} %tables.1.table_ref, f32[8,12,8,256]{3,2,1,0:T(8,128)S(1)} %all_to_all.22.own_ref, f32[8,12,8,256]{3,2,1,0:T(8,128)S(1)} %collective-permute-done.1.swapped_ref, f32[8,8192]{1,0:T(8,128)S(1)} %get-tuple-element.51.part_ref, ...), custom_call_target="tpu_custom_call" | custom-call | flops 1000000 | bytes 6291456 | tf_op jit(solution)/shard_map/image/pallas_call | solution.py:524
  81.3 15.0 %all_to_all.23 = f32[128,1,128]{2,1,0:T(1,128)S(1)} all-to-all(f32[128,1,128]{2,1,0:T(1,128)S(1)} %bitcast.36), channel_id=1, replica_groups=mesh['z'=4,'xl'=2,'xh'=2,'y'=4,'core'=2] {'z','xl','xh','y','core'}, dimensions={0} | all-to-all | bytes 131072 | tf_op jit(solution)/shard_map/all_to_all | solution.py:537
  96.3 1.1 %finish.1 = (f32[448,128]{1,0:T(8,128)}, f32[8,128]{1,0:T(8,128)S(1)}) custom-call(f32[128,128]{1,0:T(8,128)S(1)} %bitcast.35, f32[448,128]{1,0:T(8,128)S(1)} %get-tuple-element.104.image_ref, f32[3584,128]{1,0:T(8,128)S(1)} %bitcast.44), custom_call_target="tpu_custom_call" | custom-call | flops 1000000 | bytes 3145728 | tf_op jit(solution)/shard_map/finish/pallas_call | solution.py:538
  97.4 0.5 slice_bitcast_fusion
  97.9 1.8 %while.10 = (f32[448,128]{1,0:T(8,128)}, f32[10]{0:T(128)}, f32[8,1,7,8192]{3,1,2,0:T(1,128)S(1)}, f32[448,128]{1,0:T(8,128)S(1)}, f32[]{:T(128)}, /*index=5*/f32[]{:T(128)}, f32[1]{0:T(128)}) while((f32[448,128]{1,0:T(8,128)}, f32[10]{0:T(128)}, f32[8,1,7,8192]{3,1,2,0:T(1,128)S(1)}, f32[448,128]{1,0:T(8,128)S(1)}, f32[]{:T(128)}, ...), condition=%wide.region_3.0_spmd, body=%wide.region_0.0_spmd.sunk | while | flops 5734423 | bytes 3211569 | solution.py:557
  97.9 1.2 %slice.19 = f32[1]{0:T(128)} slice(f32[10]{0:T(128)} %get-tuple-element.78), slice={[9:10]} | slice | bytes 8 | tf_op jit(solution)/shard_map/while/cond/slice | solution.py:558
  (14 shorter events, 0.0 us)
Async XLA Ops:
  0.6 25.3 %copy-start.3 = (s32[32,6]{0,1:T(8,128)S(1)}, s32[32,6]{0,1:T(8,128)}, u32[]{:S(2)}) copy-start(s32[32,6]{0,1:T(8,128)} %param.16) | copy-start | bytes 2308
  0.6 25.3 %copy-start.4 = (s32[32,6]{0,1:T(8,128)S(1)}, s32[32,6]{0,1:T(8,128)}, u32[]{:S(2)}) copy-start(s32[32,6]{0,1:T(8,128)} %param.17) | copy-start | bytes 2308
  0.7 25.3 %copy-start.5 = (s32[32]{0:T(128)S(1)}, s32[32]{0:T(128)}, u32[]{:S(2)}) copy-start(s32[32]{0:T(128)} %ids_ref.1) | copy-start | bytes 388
  23.4 10.4 %collective-permute-start = (f32[8,12,8,256]{3,2,1,0:T(8,128)S(1)}, f32[8,12,8,256]{3,2,1,0:T(8,128)S(1)}, u32[]{:S(2)}, u32[]{:S(2)}) collective-permute-start(f32[8,12,8,256]{3,2,1,0:T(8,128)S(1)} %all_to_all.21.own_ref), channel_id=1, source_target_pairs={{0,1},{1,0},{2,3},{3,2},{4,5},{5,4},{6,7},{7,6},{8,9},{9,8},{10,11... | collective-permute-start | bytes 2359304 | tf_op jit(solution)/shard_map/ppermute | solution.py:434
  27.7 2.8 %copy-start = (bf16[1,7,7,7,8192]{4,3,2,1,0:T(8,128)(2,1)S(1)}, bf16[1,7,7,7,8192]{4,3,2,1,0:T(8,128)(2,1)}, u32[]{:S(2)}) copy-start(bf16[1,7,7,7,8192]{4,3,2,1,0:T(8,128)(2,1)} %coeff_ref.2) | copy-start | bytes 16859140
  30.6 44.9 %slice-start = ((s8[6422528]{0:T(1024)(128)(4,1)}), s8[4194304]{0:T(1024)(128)(4,1)S(1)}, s32[]{:S(2)}) async-start(s8[6422528]{0:T(1024)(128)(4,1)} %bitcast.33), calls=%async_computation.3 | async-start | bytes 8388608
  33.8 41.6 %slice-start.1 = ((s8[6422528]{0:T(1024)(128)(4,1)}), s8[2228224]{0:T(1024)(128)(4,1)S(1)}, s32[]{:S(2)}) async-start(s8[6422528]{0:T(1024)(128)(4,1)} %bitcast.33), calls=%async_computation.4 | async-start | bytes 4456448
  38.3 35.8 %copy-start.6 = (f32[8,1,7,8192]{3,1,2,0:T(1,128)S(1)}, f32[8,1,7,8192]{3,1,2,0:T(1,128)}, u32[]{:S(2)}) copy-start(f32[8,1,7,8192]{3,1,2,0:T(1,128)} %param.10) | copy-start | bytes 5505028
  54.3 25.2 %collective-permute-start.1 = (f32[8,12,8,256]{3,2,1,0:T(8,128)S(1)}, f32[8,12,8,256]{3,2,1,0:T(8,128)S(1)}, u32[]{:S(2)}, u32[]{:S(2)}) collective-permute-start(f32[8,12,8,256]{3,2,1,0:T(8,128)S(1)} %all_to_all.22.own_ref), channel_id=1, source_target_pairs={{0,1},{1,0},{2,3},{3,2},{4,5},{5,4},{6,7},{7,6},{8,9},{9,8},{10,11... | collective-permute-start | bytes 2359304 | tf_op jit(solution)/shard_map/ppermute | solution.py:434
  55.9 7.5 %collective-permute-start.2 = (f32[448,128]{1,0:T(8,128)S(1)}, f32[448,128]{1,0:T(8,128)S(1)}, u32[]{:S(2)}, u32[]{:S(2)}) collective-permute-start(f32[448,128]{1,0:T(8,128)S(1)} %get-tuple-element.55.own_ref), channel_id=1, source_target_pairs={{0,32},{32,0},{64,96},{96,64},{1,33},{33,1},{65,97},{97,65},{2,34}... | collective-permute-start | bytes 688136 | tf_op jit(solution)/shard_map/ppermute | solution.py:464
  57.6 14.0 %collective-permute-start.3 = (f32[448,128]{1,0:T(8,128)S(1)}, f32[448,128]{1,0:T(8,128)S(1)}, u32[]{:S(2)}, u32[]{:S(2)}) collective-permute-start(f32[448,128]{1,0:T(8,128)S(1)} %get-tuple-element.55.own_ref), channel_id=1, source_target_pairs={{0,64},{32,96},{64,0},{96,32},{1,65},{33,97},{65,1},{97,33},{2,66}... | collective-permute-start | bytes 688136 | tf_op jit(solution)/shard_map/ppermute | solution.py:464
  60.9 12.7 %collective-permute-start.4 = (f32[448,128]{1,0:T(8,128)S(1)}, f32[448,128]{1,0:T(8,128)S(1)}, u32[]{:S(2)}, u32[]{:S(2)}) collective-permute-start(f32[448,128]{1,0:T(8,128)S(1)} %get-tuple-element.55.own_ref), channel_id=1, source_target_pairs={{0,96},{32,64},{64,32},{96,0},{1,97},{33,65},{65,33},{97,1},{2,98}... | collective-permute-start | bytes 688136 | tf_op jit(solution)/shard_map/ppermute | solution.py:464
  73.7 5.8 %collective-permute-start.5 = (f32[448,128]{1,0:T(8,128)S(1)}, f32[448,128]{1,0:T(8,128)S(1)}, u32[]{:S(2)}, u32[]{:S(2)}) collective-permute-start(f32[448,128]{1,0:T(8,128)S(1)} %get-tuple-element.57), channel_id=1, source_target_pairs={{0,16},{16,0},{1,17},{17,1},{2,18},{18,2},{3,19},{19,3},{4,20},{20... | collective-permute-start | bytes 688136 | tf_op jit(solution)/shard_map/ppermute | solution.py:474
  75.5 4.0 %copy-start.1 = (f32[8192]{0:T(1024)S(1)}, f32[8192]{0:T(1024)}, u32[]{:S(2)}) copy-start(f32[8192]{0:T(1024)} %param.13) | copy-start | bytes 98308
  75.5 4.0 %copy-start.2 = (f32[8192]{0:T(1024)S(1)}, f32[8192]{0:T(1024)}, u32[]{:S(2)}) copy-start(f32[8192]{0:T(1024)} %param.14) | copy-start | bytes 98308

commit v3 on v2

v3 whole, which is shorter than its diff:
```python
import jax
import jax.numpy as jnp
import numpy as np
from jax import lax
from jax.experimental import pallas as pl
from jax.experimental.pallas import tpu as pltpu
from jax.sharding import Mesh, PartitionSpec as P

EDGE = 16
SQUARE = EDGE * EDGE
CUBE = EDGE * SQUARE
VARS = 7
KRYLOV = 8
INST = 8
BLOCKS = 32
SPACE = 16
CHIP_COUNT = 8
CELLS = 8192
PER = CELLS // CUBE
FACES = 6 * PER
SLABS = CELLS // SQUARE
ENTRIES = float(INST * VARS * CELLS * SPACE)
LANES = 128
GROUPS = CELLS // LANES
ROWS = VARS * GROUPS
ALL = ("z", "xl", "xh", "y", "core")
CHIPS = ("xh", "y")
VMEM = pltpu.VMEM
SMEM = pltpu.SMEM
GUARD = 0.02
CHUNK = 4
FLUX_INNER = 10**7
INNER_MIB = 50
OUTER_MIB = 16
MIX = 10**6
FLUX_OUTER = 10**6
RECON_INNER = 6 * 10**9


def mixing_weights():
    k = np.arange(1, INST)
    parity = np.where(k % 2 == 0, 1.0, -1.0)
    angle = np.pi * k / INST
    rest = 0.5 * parity / np.tan(angle) - 0.125 * parity / np.sin(angle) ** 2
    return [-0.25 * (INST * INST + 2) / 12.0] + [float(v) for v in rest]


def lanes(shape):
    return lax.broadcasted_iota(jnp.int32, shape, len(shape) - 1)


def sublanes(shape):
    return lax.broadcasted_iota(jnp.int32, shape, len(shape) - 2)


def pick(values, index):
    return jnp.take_along_axis(values, index, axis=1)


def fold(totals):
    row = sublanes(totals[0].shape)
    for width in (1, 2, 4):
        first = row % (2 * width) < width
        totals = [
            jnp.where(first, a, b) + pltpu.roll(jnp.where(first, b, a), width, 0)
            for a, b in zip(totals[::2], totals[1::2])
        ]
    return totals[0]


def strips_of(slab, x, strips):
    lane = lanes((8, LANES))
    low, high = (slab[:, :LANES], slab[:, LANES:])
    own = lane >> 4 == x
    upper = lane & 8 != 0
    z = lane & 15
    source = (lane & 7) << 4
    found = (
        pick(low, z),
        pick(high, z + (LANES - EDGE)),
        jnp.where(upper, pick(high, source), pick(low, source)),
        jnp.where(upper, pick(high, source + 15), pick(low, source + 15)),
    )
    if strips is None:
        return list(found)
    return [jnp.where(own, new, old) for new, old in zip(found, strips)]


def collect_block(field_ref, faces, block):
    start = block * CUBE
    faces[block * 6] = field_ref[:, start : start + SQUARE]
    faces[block * 6 + 1] = field_ref[:, start + CUBE - SQUARE : start + CUBE]
    for half in range(2):
        strips = None
        for inner in range(8):
            place = start + (half * 8 + inner) * SQUARE
            strips = strips_of(field_ref[:, place : place + SQUARE], inner, strips)
        for number, strip in enumerate(strips):
            faces[block * 6 + 2 + number, :, half * LANES : (half + 1) * LANES] = strip


def send_block(faces, sent_ref, arrived, block):
    rows = pl.ds(block * 6, 6)
    copies = [
        pltpu.make_async_copy(faces.at[rows], sent_ref.at[chip, rows], arrived.at[block, chip])
        for chip in range(CHIP_COUNT)
    ]
    for copy in copies:
        copy.start()
    return copies


def first_faces_kernel(basis_ref, sent_ref, padded_ref, dense_ref, field, faces, arrived):
    fetch = pltpu.make_async_copy(
        basis_ref.at[pl.ds((KRYLOV - 1) * ROWS, ROWS)], field.at[pl.ds(0, ROWS)], arrived.at[0, 0]
    )
    fetch.start()
    field[ROWS:] = jnp.zeros((GROUPS, LANES), jnp.float32)
    fetch.wait()
    copies = []
    for block in range(PER):
        for group in range(block * 32, block * 32 + 32):
            padded_ref[:, group * LANES : (group + 1) * LANES] = field[pl.ds(group, 8, stride=GROUPS), :]
        collect_block(padded_ref, faces, block)
        copies += send_block(faces, sent_ref, arrived, block)
    dense_ref[...] = field[:ROWS]
    for copy in copies:
        copy.wait()


def tables_kernel(ids_ref, neighbour_ref, orient_ref, table_ref, position):
    core = lax.axis_index("core")
    rank = (lax.axis_index("xh") * 4 + lax.axis_index("y")) * 2 + core

    def place(slot, carry):
        position[ids_ref[slot]] = slot
        return carry

    lax.fori_loop(0, BLOCKS, place, 0)
    for number in range(FACES):
        owner = ids_ref[rank * PER + number // 6]
        partner = neighbour_ref[number % 6, owner]
        code = orient_ref[number % 6, owner]
        target = jnp.maximum(partner, 0)
        slot = position[target // 6]
        device = slot // PER
        table_ref[number * 4] = device // 2
        table_ref[number * 4 + 1] = jnp.where(device % 2 == core, 1, 0)
        table_ref[number * 4 + 2] = (slot % PER) * 6 + target % 6
        table_ref[number * 4 + 3] = jnp.where(partner < 0, -1, code)


def fetch_halos(table_ref, own_ref, swapped_ref, halos):
    lane = lanes((8, LANES))
    for number in range(FACES):
        chip = table_ref[number * 4]
        here = table_ref[number * 4 + 1] == 1
        row = table_ref[number * 4 + 2]
        code = table_ref[number * 4 + 3]
        wall = code < 0
        code = jnp.maximum(code, 0)
        source = jnp.where(here, own_ref[chip, row], swapped_ref[chip, row])
        source = jnp.where(wall, 0.0, source)
        low, high = (source[:, :LANES], source[:, LANES:])
        transposed = code & 1 == 1
        flip_a = (code >> 1 & 1) * (EDGE - 1)
        flip_b = (code >> 2) * (EDGE - 1)
        for half in range(2):
            a = ((lane >> 4) + half * 8) ^ flip_a
            b = (lane & 15) ^ flip_b
            index = jnp.where(transposed, (b << 4) + a, (a << 4) + b)
            inside = index & (LANES - 1)
            halos[number, :, half * LANES : (half + 1) * LANES] = jnp.where(
                index < LANES, pick(low, inside), pick(high, inside)
            )


def inner_kernel(
    field_ref, coeff_ref, part_ref, across_z_ref, across_y_ref, across_x_ref, token_ref, held, arrived
):
    column = lanes((8, SQUARE))
    z = column & 15
    width = CHUNK * SQUARE
    chunks = SLABS // CHUNK
    copies = [
        pltpu.make_async_copy(coeff_ref.at[0, :, :, :, pl.ds(i * width, width)], held.at[i], arrived.at[i])
        for i in range(chunks)
    ]
    for copy in copies:
        copy.start()

    def load(k):
        return field_ref[:, pl.ds(pl.multiple_of(k * SQUARE, SQUARE), SQUARE)]

    def chunk_step(chunk, carry):
        pltpu.make_async_copy(
            coeff_ref.at[0, :, :, :, pl.ds(0, width)], held.at[chunk], arrived.at[chunk]
        ).wait()
        for inner in range(CHUNK):

            def coeff(s, o):
                value = held[chunk, s, o, :, inner * SQUARE : (inner + 1) * SQUARE].astype(jnp.float32)
                return jnp.concatenate([value, jnp.zeros((1, SQUARE), jnp.float32)], axis=0)

            k = chunk * CHUNK + inner
            block, x = (k // EDGE, k % EDGE)
            place = pl.ds(pl.multiple_of(k * SQUARE, SQUARE), SQUARE)
            centre = load(k)
            below, above = (load(jnp.maximum(k - 1, 0)), load(jnp.minimum(k + 1, SLABS - 1)))
            if inner == 0:
                below = jnp.where(x == 0, 0.0, below)
            if inner == CHUNK - 1:
                above = jnp.where(x == EDGE - 1, 0.0, above)
            operands = [
                centre,
                below,
                above,
                jnp.where(column < EDGE, 0.0, pltpu.roll(centre, EDGE, 1)),
                jnp.where(column >= SQUARE - EDGE, 0.0, pltpu.roll(centre, SQUARE - EDGE, 1)),
                jnp.where(z == 0, 0.0, pltpu.roll(centre, 1, 1)),
                jnp.where(z == EDGE - 1, 0.0, pltpu.roll(centre, SQUARE - 1, 1)),
            ]
            totals = []
            for o in range(VARS):
                values = [coeff(s, o) for s in range(7)]
                total = values[0] * operands[0]
                for s in range(1, 7):
                    total = total + values[s] * operands[s]
                totals.append(total)
                across_z_ref[o, :, place] = jnp.where(
                    z == 0, values[5], jnp.where(z == EDGE - 1, values[6], 0.0)
                ).astype(jnp.bfloat16)
                across_y_ref[o, :, place] = jnp.where(
                    column < EDGE, values[3], jnp.where(column >= SQUARE - EDGE, values[4], 0.0)
                ).astype(jnp.bfloat16)
            part_ref[:, place] = fold(totals + [jnp.zeros((8, SQUARE), jnp.float32)])

            if inner == 0:

                @pl.when(x == 0)
                def _():
                    for o in range(VARS):
                        across_x_ref[block * 2, o] = coeff(1, o).astype(jnp.bfloat16)

            if inner == CHUNK - 1:

                @pl.when(x == EDGE - 1)
                def _():
                    for o in range(VARS):
                        across_x_ref[block * 2 + 1, o] = coeff(2, o).astype(jnp.bfloat16)

        return carry

    lax.fori_loop(0, chunks, chunk_step, 0)
    token_ref[...] = jnp.zeros_like(token_ref)


def outer_slab(part_ref, across_z_ref, across_y_ref, halos, block, half, inner):
    lane = lanes((8, LANES))
    offset = inner * EDGE
    start = block * CUBE + (half * 8 + inner) * SQUARE
    place = slice(start, start + SQUARE)

    def strip(face):
        return halos[block * 6 + face, :, half * LANES : (half + 1) * LANES]

    y = (lane & 15) + offset
    z = (lane >> 4) + offset
    at_low = lane & 15 == 0
    across_y = jnp.concatenate([pick(strip(2), y), pick(strip(3), y)], axis=1)
    z_low, z_high = (strip(4), strip(5))
    across_z = jnp.concatenate(
        [
            jnp.where(at_low, pick(z_low, z), pick(z_high, z)),
            jnp.where(at_low, pick(z_low, z + 8), pick(z_high, z + 8)),
        ],
        axis=1,
    )
    totals = [
        across_z_ref[o, :, place].astype(jnp.float32) * across_z
        + across_y_ref[o, :, place].astype(jnp.float32) * across_y
        for o in range(VARS)
    ]
    return part_ref[:, place] + fold(totals + [jnp.zeros((8, SQUARE), jnp.float32)])


def outer_x(across_x_ref, halos, block, side):
    halo = halos[block * 6 + side]
    totals = [across_x_ref[block * 2 + side, o].astype(jnp.float32) * halo for o in range(VARS)]
    return fold(totals + [jnp.zeros((8, SQUARE), jnp.float32)])


def outer_block(across_x_ref, part_ref, across_z_ref, across_y_ref, halos, block, put):
    for half in range(2):
        for inner in range(8):
            slab = outer_slab(part_ref, across_z_ref, across_y_ref, halos, block, half, inner)
            if half == 0 and inner == 0:
                slab = slab + outer_x(across_x_ref, halos, block, 0)
            if half == 1 and inner == 7:
                slab = slab + outer_x(across_x_ref, halos, block, 1)
            put(block * EDGE + half * 8 + inner, slab)


def flux_kernel(
    table_ref, own_ref, swapped_ref, part_ref, across_z_ref, across_y_ref, across_x_ref, token_ref,
    first_ref, sent_ref, halos, faces, arrived
):
    fetch_halos(table_ref, own_ref, swapped_ref, halos)

    def put(k, slab):
        first_ref[:, k * SQUARE : (k + 1) * SQUARE] = slab

    copies = []
    for block in range(PER):
        outer_block(across_x_ref, part_ref, across_z_ref, across_y_ref, halos, block, put)
        collect_block(first_ref, faces, block)
        copies += send_block(faces, sent_ref, arrived, block)
    for copy in copies:
        copy.wait()


def mix_kernel(own_ref, one_ref, two_ref, three_ref, first_ref, kept_ref, given_ref):
    z = lax.axis_index("z")
    xl = lax.axis_index("xl")
    table = mixing_weights()

    def weight(offset):
        offset = lax.rem(offset + 2 * INST, INST)
        value = jnp.float32(table[0])
        for k in range(1, INST):
            value = jnp.where(offset == k, jnp.float32(table[k]), value)
        return value

    fields = (own_ref, one_ref, two_ref, three_ref)
    sources = [2 * (z ^ k) + xl for k in range(4)]
    kept = [weight(source - (2 * z + xl)) for source in sources]
    given = [weight(source - (2 * z + 1 - xl)) for source in sources]

    def step(k, carry):
        rows = pl.ds(pl.multiple_of(k * 64, 64), 64)
        values = [field[rows] for field in fields]
        kept_ref[rows] = sum(w * v for w, v in zip(kept, values))
        given_ref[rows] = sum(w * v for w, v in zip(given, values))
        return carry

    lax.fori_loop(0, ROWS // 64, step, 0)


def lane_sums(rows, first_lane):
    totals = jnp.broadcast_to(jnp.sum(rows, axis=1, keepdims=True), rows.shape)
    spot = lanes(rows.shape) == sublanes(rows.shape) + first_lane
    return jnp.sum(jnp.where(spot, totals, 0.0), axis=0, keepdims=True)


def gram_kernel(flat_ref, basis_ref, gram_ref, lines, arrived):
    copy = pltpu.make_async_copy(flat_ref, basis_ref, arrived)
    copy.start()
    copy.wait()

    def step(k, totals):
        fields = [
            basis_ref[pl.ds(pl.multiple_of(j * ROWS + k * 8, 8), 8)] for j in range(KRYLOV)
        ]
        out = []
        for i in range(KRYLOV):
            for j in range(i, KRYLOV):
                out.append(totals[len(out)] + fields[i] * fields[j])
        return tuple(out)

    zero = jnp.zeros((8, LANES), jnp.float32)
    totals = lax.fori_loop(0, ROWS // 8, step, (zero,) * (KRYLOV * (KRYLOV + 1) // 2))
    number = 0
    for i in range(KRYLOV):
        for j in range(i, KRYLOV):
            line = jnp.sum(totals[number], axis=0, keepdims=True)
            lines[i * KRYLOV + j : i * KRYLOV + j + 1] = line
            lines[j * KRYLOV + i : j * KRYLOV + i + 1] = line
            number += 1
    gram_ref[...] = jnp.broadcast_to(lane_sums(lines[...], 64), (8, LANES))


def image_kernel(
    table_ref, own_ref, swapped_ref, part_ref, across_z_ref, across_y_ref, across_x_ref,
    basis_ref, pseudo_ref, omega_ref, kept_ref, returned_ref, gram_ref, token_ref,
    image_ref, sums_ref, halos, section
):
    fetch_halos(table_ref, own_ref, swapped_ref, halos)

    def put(k, slab):
        section[pl.ds(2 * k, 8, stride=GROUPS), :] = slab[:, :LANES]
        section[pl.ds(2 * k + 1, 8, stride=GROUPS), :] = slab[:, LANES:]

    for block in range(PER):
        outer_block(across_x_ref, part_ref, across_z_ref, across_y_ref, halos, block, put)

    def step(k, totals):
        start = k * 8
        cells = pl.ds(pl.multiple_of(start % GROUPS, 8), 8)
        rows = pl.ds(pl.multiple_of(start, 8), 8)
        fields = [basis_ref[pl.ds(pl.multiple_of(j * ROWS + start, 8), 8)] for j in range(KRYLOV)]
        spectral = kept_ref[rows] + returned_ref[rows]
        image = pseudo_ref[cells] * fields[KRYLOV - 1] + section[rows] + omega_ref[cells] * spectral
        image_ref[rows] = image
        return tuple(total + field * image for total, field in zip(totals, fields + [image]))

    zero = jnp.zeros((8, LANES), jnp.float32)
    totals = lax.fori_loop(0, ROWS // 8, step, (zero,) * (KRYLOV + 1), unroll=8)
    lines = [jnp.sum(total, axis=0, keepdims=True) for total in totals]
    lines += [jnp.zeros((16 - len(lines), LANES), jnp.float32)]
    sums = jnp.broadcast_to(lane_sums(jnp.concatenate(lines, axis=0), 0), (8, LANES)) + gram_ref[...]
    for group in range(16):
        sums_ref[group * 8 : group * 8 + 8] = sums


def finish_kernel(received_ref, image_ref, basis_ref, next_ref, column_ref, flag_ref, column_held, sent):
    sums = jnp.sum(received_ref[...], axis=0, keepdims=True)
    sums = jnp.broadcast_to(sums, (8, LANES)) / ENTRIES
    lane = lanes((8, LANES))
    left = pick(sums, jnp.maximum(lane - 64, 0) // 8)
    right = pick(sums, lane % 8)
    quadratic = jnp.sum(jnp.where(lane >= 64, sums * left * right, 0.0), axis=1, keepdims=True)
    linear = jnp.sum(jnp.where(lane < KRYLOV, sums * sums, 0.0), axis=1, keepdims=True)
    whole_square = sums[:, KRYLOV : KRYLOV + 1]
    squares = whole_square - 2.0 * linear + quadratic
    size = whole_square + 2.0 * linear + jnp.abs(quadratic)
    norm = jnp.sqrt(jnp.maximum(squares, 0.0) + 1e-06)
    column = jnp.where(lane < KRYLOV, sums, jnp.where(lane == KRYLOV, norm, 0.0))
    column_held[...] = column[:1, : KRYLOV + 1]
    copy = pltpu.make_async_copy(column_held, column_ref, sent)
    copy.start()
    flag_ref[0] = jnp.sum(jnp.where(squares[:1] < GUARD * size[:1], 1.0, 0.0)).astype(jnp.int32)
    coeffs = [jnp.broadcast_to(sums[:, j : j + 1], (8, LANES)) for j in range(KRYLOV)]
    scale = jnp.broadcast_to(1.0 / norm, (8, LANES))

    def step(k, carry):
        start = k * 8
        rows = pl.ds(pl.multiple_of(start, 8), 8)
        ortho = image_ref[rows]
        for j in range(KRYLOV):
            ortho = ortho - coeffs[j] * basis_ref[pl.ds(pl.multiple_of(j * ROWS + start, 8), 8)]
        next_ref[rows] = ortho * scale
        return carry

    lax.fori_loop(0, ROWS // 8, step, 0, unroll=8)
    copy.wait()


def whole(memory=VMEM):
    return pl.BlockSpec(memory_space=memory)


def f32(*shape):
    return jax.ShapeDtypeStruct(shape, jnp.float32)


def bf16(*shape):
    return jax.ShapeDtypeStruct(shape, jnp.bfloat16)


def params(mib):
    return pltpu.CompilerParams(vmem_limit_bytes=mib * 2**20)


def cost(flops, moved):
    return pl.CostEstimate(flops=flops, bytes_accessed=moved, transcendentals=0)


def swap(size, bit):
    return [(i, i ^ bit) for i in range(size)]


def exchange(sent):
    return lax.all_to_all(sent, CHIPS, 0, 0)


def after(value, others):
    return lax.optimization_barrier((value, others))


def swap_cores(own):
    return lax.ppermute(own, "core", swap(2, 1))


FACES_VMEM = VMEM((FACES, 8, SQUARE), jnp.float32)
SENT = f32(CHIP_COUNT, FACES, 8, SQUARE)


def inner_section(field, coeff, name, flops):
    chunks = SLABS // CHUNK
    return pl.pallas_call(
        inner_kernel,
        in_specs=[whole(), whole(pltpu.HBM)],
        out_specs=[whole()] * 5,
        out_shape=[
            f32(8, CELLS), bf16(VARS, 8, CELLS), bf16(VARS, 8, CELLS), bf16(2 * PER, VARS, 8, SQUARE), f32(8, LANES),
        ],
        scratch_shapes=[
            VMEM((chunks, 7, VARS, VARS, CHUNK * SQUARE), jnp.bfloat16),
            pltpu.SemaphoreType.DMA((chunks,)),
        ],
        compiler_params=params(INNER_MIB),
        cost_estimate=cost(flops, 8 * 2**20),
        name=name,
    )(field, coeff)


def mix(parts, first):
    kept, given = pl.pallas_call(
        mix_kernel,
        in_specs=[whole()] * 4 + [whole(pl.ANY)],
        out_specs=[whole()] * 2,
        out_shape=[f32(ROWS, LANES), f32(ROWS, LANES)],
        compiler_params=params(8),
        cost_estimate=cost(MIX, 6 * 4 * ROWS * LANES),
        name="mix",
    )(*parts, first)
    return kept, lax.ppermute(given, "xl", swap(2, 1))


def local(basis, flux, recon, pseudo_time, vol_omega, block_ids, neighbour, orient):
    flat = basis.reshape(KRYLOV * ROWS, LANES)
    sent, padded, dense = pl.pallas_call(
        first_faces_kernel,
        in_specs=[whole(pl.ANY)],
        out_specs=[whole(pl.ANY), whole(), whole()],
        out_shape=[SENT, f32(8, CELLS), f32(ROWS, LANES)],
        scratch_shapes=[VMEM((8 * GROUPS, LANES), jnp.float32), FACES_VMEM, pltpu.SemaphoreType.DMA((PER, CHIP_COUNT))],
        compiler_params=params(8),
        cost_estimate=cost(10**6, 2 * 2**20),
        name="first_faces",
    )(flat)
    own = exchange(sent)
    table = pl.pallas_call(
        tables_kernel,
        in_specs=[whole(SMEM)] * 3,
        out_specs=whole(SMEM),
        out_shape=jax.ShapeDtypeStruct((4 * FACES,), jnp.int32),
        scratch_shapes=[SMEM((BLOCKS,), jnp.int32)],
        compiler_params=params(4),
        cost_estimate=cost(10**5, 10**5),
        name="tables",
    )(block_ids, neighbour.T, orient.T)
    held, gram = pl.pallas_call(
        gram_kernel,
        in_specs=[whole(pl.ANY)],
        out_specs=[whole(), whole()],
        out_shape=[f32(KRYLOV * ROWS, LANES), f32(8, LANES)],
        scratch_shapes=[VMEM((KRYLOV * KRYLOV, LANES), jnp.float32), pltpu.SemaphoreType.DMA],
        compiler_params=params(8),
        cost_estimate=cost(2 * 36 * VARS * CELLS, 2 * 2**20),
        name="gram",
    )(flat)
    *pieces, token = inner_section(padded, flux, "flux_inner", FLUX_INNER)
    one, two, three = [lax.ppermute(dense, "z", swap(4, k)) for k in (1, 2, 3)]
    own, (token, table, one, three) = after(own, (token, table, one, three))
    parts = (dense, one, two, three)
    swapped = swap_cores(own)
    first, sent = pl.pallas_call(
        flux_kernel,
        in_specs=[whole(SMEM)] + [whole()] * 6 + [whole(pl.ANY)],
        out_specs=[whole(), whole(pl.ANY)],
        out_shape=[f32(8, CELLS), SENT],
        scratch_shapes=[FACES_VMEM, FACES_VMEM, pltpu.SemaphoreType.DMA((PER, CHIP_COUNT))],
        compiler_params=params(OUTER_MIB),
        cost_estimate=cost(FLUX_OUTER, 4 * 2**20),
        name="flux_outer",
    )(table, own, swapped, *pieces, token)
    own = exchange(sent)
    kept, returned = mix(parts, first)
    *pieces, token = inner_section(first, recon, "recon_inner", RECON_INNER)
    own, (token, returned) = after(own, (token, returned))
    swapped = swap_cores(own)
    image, sums = pl.pallas_call(
        image_kernel,
        in_specs=[whole(SMEM)] + [whole()] * 12 + [whole(pl.ANY)],
        out_specs=[whole(), whole()],
        out_shape=[f32(ROWS, LANES), f32(LANES, LANES)],
        scratch_shapes=[FACES_VMEM, VMEM((8 * GROUPS, LANES), jnp.float32)],
        compiler_params=params(OUTER_MIB),
        cost_estimate=cost(10**6, 6 * 2**20),
        name="image",
    )(
        table, own, swapped, *pieces,
        held, pseudo_time.reshape(GROUPS, LANES), vol_omega.reshape(GROUPS, LANES), kept, returned, gram, token,
    )
    received = lax.all_to_all(sums, ALL, 0, 0)
    following, column, flag = pl.pallas_call(
        finish_kernel,
        in_specs=[whole()] * 3,
        out_specs=[whole(), whole(pl.ANY), whole(SMEM)],
        out_shape=[f32(ROWS, LANES), f32(1, KRYLOV + 1), jax.ShapeDtypeStruct((1,), jnp.int32)],
        scratch_shapes=[VMEM((1, KRYLOV + 1), jnp.float32), pltpu.SemaphoreType.DMA],
        compiler_params=params(8),
        cost_estimate=cost(10**6, 3 * 2**20),
        name="finish",
    )(received, image, held)

    def direct(state):
        coeffs = state[1][0, :KRYLOV]
        ortho = image - jnp.einsum(
            "k,krl->rl", coeffs, flat.reshape(KRYLOV, ROWS, LANES), precision=lax.Precision.HIGHEST
        )
        squares = lax.psum(jnp.sum(ortho * ortho), ALL) / ENTRIES
        norm = jnp.sqrt(squares + 1e-06)
        return (ortho / norm, jnp.concatenate([coeffs, norm[None]])[None], jnp.zeros((), jnp.int32))

    following, column, _ = lax.while_loop(
        lambda state: state[2] > 0, direct, (following, column, flag[0])
    )
    return following.reshape(1, VARS, CELLS), column[0]


def solution(mesh):
    fine = Mesh(mesh.devices.reshape(4, 2, 2, 4, 2), ALL)
    inst, space = (("z", "xl"), ("xh", "y", "core"))
    placed = (
        P(None, inst, None, space),
        P(inst, None, None, None, space),
        P(inst, None, None, None, space),
        P(space),
        P(space),
        P(),
        P(),
        P(),
    )
    return jax.shard_map(
        local,
        mesh=fine,
        in_specs=placed,
        out_specs=(P(inst, None, space), P()),
        check_vma=False,
    )
```

time: 100 us -> 76.4 us (0.76)
  blocking collectives: 51 us -> 18.6 us
  starting transfers between devices: 9.52 us -> 22.9 us
  waiting for transfers between devices: 13.5 us -> 7.15 us
  Pallas kernels: 19.8 us -> 21.3 us
    all_to_all x2 -> x0, blocking collectives: 36 us -> none  [exchange(): own = lax.all_to_all(sent, CHIPS, 0, 0)]
    ppermute x5, waiting for transfers between devices: 12.7 us -> 0.01 us  [the longest x3 0.01 us: local(): one, two, three = [lax.ppermute(dense, 'z', swap(4, k)) for k in (1, 2, 3)]]
    all_to_all x0 -> x2, starting transfers between devices: none -> 11 us  [exchange(): return lax.all_to_all(sent, CHIPS, 0, 0)]
    ppermute x1, waiting for transfers between devices: 0.75 us -> 6.62 us  [mix(): return (kept, lax.ppermute(given, 'xl', swap(2, 1)))]
    all_to_all x1, blocking collectives: 15 us -> 18.6 us  [local(): received = lax.all_to_all(sums, ALL, 0, 0)]
    ppermute x5, starting transfers between devices: 9.12 us -> 11.5 us  [the longest x3 7.48 us: local(): one, two, three = [lax.ppermute(dense, 'z', swap(4, k)) for k in (1, 2, 3)]]
    unnamed x18 -> x28, local copies, waits for them, and re-layouts: 2.86 us -> 4.48 us
    pallas_call x6, Pallas kernels: 14.2 us -> 15.8 us  [the longest x2 7.48 us: inner_section(): pl.pallas_call(inner_kernel, in_specs=[whole(), whole(pltpu.HBM)], out_sp...]
  transfers between devices with their start and end apart: 6 -> 8, of which waited for: 4 -> 2; matrix products, arithmetic and copies ran while one was open for 0% -> 0% of each run, Pallas kernels for 10% -> 21%
where the time goes in v3:
time: 76.4 us; the launch traced here: 75.9 us
  starting transfers between devices  22.9 us (30%)
  Pallas kernels  21.3 us (28%)
  blocking collectives  18.6 us (24%)
  waiting for transfers between devices  7.15 us (9%)
  local copies, waits for them, and re-layouts  4.48 us (6%)
  between operations  0.88 us (1%)
    all_to_all x1, blocking collectives, local(): received = lax.all_to_all(sums, ALL, 0, 0)  18.6 us
    all_to_all x2, starting transfers between devices, exchange(): return lax.all_to_all(sent, CHIPS, 0, 0)  11 us
    pallas_call x2, Pallas kernels, inner_section(): pl.pallas_call(inner_kernel, in_specs=[whole(), whole(pltpu.HBM)], out_sp...  7.48 us
    ppermute x3, starting transfers between devices, local(): one, two, three = [lax.ppermute(dense, 'z', swap(4, k)) for k in (1, 2, 3)]  7.48 us
    ppermute x1, waiting for transfers between devices, mix(): return (kept, lax.ppermute(given, 'xl', swap(2, 1)))  6.62 us
    unnamed x28, local copies, waits for them, and re-layouts  4.48 us
    ppermute x2, starting transfers between devices, swap_cores(): return lax.ppermute(own, 'core', swap(2, 1))  4.03 us
    pallas_call x1, Pallas kernels, local(): pl.pallas_call(gram_kernel, in_specs=[whole(pl.ANY)], out_specs=[whole(),...  2.82 us
  transfers between devices with their start and end apart: 8, of which 2 were waited for; matrix products, arithmetic and copies ran while one was open for 0% of the time, Pallas kernels for 21%

profile of v3, /device:TPU:1, one launch (start us, length us, event | category | flops | bytes accessed | tf_op | source)
XLA Modules:
  0.0 75.9 jit_solution(10428262311116641165)
XLA Ops:
  0.7 2.5 %first_faces.1 = (f32[8,12,8,256]{3,2,1,0:T(8,128)}, f32[8,8192]{1,0:T(8,128)S(1)}, f32[448,128]{1,0:T(8,128)S(1)}) custom-call(f32[3584,128]{1,0:T(8,128)} %bitcast.30), custom_call_target="tpu_custom_call" | custom-call | flops 1000000 | bytes 2097152 | tf_op jit(solution)/shard_map/first_faces/pallas_call | solution.py:522
  3.1 7.5 %all-to-all-start = ((f32[8,12,8,256]{3,2,1,0:T(8,128)}), f32[8,12,8,256]{3,2,1,0:T(8,128)S(1)}, u32[]{:S(2)}, u32[]{:S(2)}) async-start(f32[8,12,8,256]{3,2,1,0:T(8,128)} %get-tuple-element.60), calls=%async_computation | async-start | bytes 1572864 | tf_op jit(solution)/shard_map/all_to_all | solution.py:473
  10.6 1.6 %collective-permute-start = (f32[448,128]{1,0:T(8,128)S(1)}, f32[448,128]{1,0:T(8,128)S(1)}, u32[]{:S(2)}, u32[]{:S(2)}) collective-permute-start(f32[448,128]{1,0:T(8,128)S(1)} %get-tuple-element.63.own_ref), channel_id=1, source_target_pairs={{0,32},{32,0},{64,96},{96,64},{1,33},{33,1},{65,97},{97,65},{2,34}... | collective-permute-start | bytes 688136 | tf_op jit(solution)/shard_map/ppermute | solution.py:554
  12.3 2.2 %collective-permute-start.1 = (f32[448,128]{1,0:T(8,128)S(1)}, f32[448,128]{1,0:T(8,128)S(1)}, u32[]{:S(2)}, u32[]{:S(2)}) collective-permute-start(f32[448,128]{1,0:T(8,128)S(1)} %get-tuple-element.63.own_ref), channel_id=1, source_target_pairs={{0,96},{32,64},{64,32},{96,0},{1,97},{33,65},{65,33},{97,1},{2,98}... | collective-permute-start | bytes 688136 | tf_op jit(solution)/shard_map/ppermute | solution.py:554
  14.5 1.8 %tables.1.table_ref = s32[48]{0:T(128)S(1)} custom-call(s32[32]{0:T(128)S(1)} %copy-done.10, s32[6,32]{1,0:T(8,128)S(1)} %bitcast.28, s32[6,32]{1,0:T(8,128)S(1)} %bitcast.29), custom_call_target="tpu_custom_call" | custom-call | flops 100000 | bytes 100000 | tf_op jit(solution)/shard_map/tables/pallas_call | solution.py:533
  16.3 3.7 %flux_inner.1 = (f32[8,8192]{1,0:T(8,128)S(1)}, bf16[7,8,8192]{2,1,0:T(8,128)(2,1)S(1)}, bf16[7,8,8192]{2,1,0:T(8,128)(2,1)S(1)}, bf16[4,7,8,256]{3,2,1,0:T(8,128)(2,1)S(1)}, f32[8,128]{1,0:T(8,128)S(1)}) custom-call(f32[8,8192]{1,0:T(8,128)S(1)} %get-tuple-element.61.field_ref, bf16[1,7,7,7,8192]{4,3,2,1,0:T(8,128)(2,1)} %coeff_ref.2), custom_call_target="tpu_custom_call" | custom-call | flops 10000000 | bytes 8388608 | tf_op jit(solution)/shard_map/flux_inner/pallas_call | solution.py:490
  20.1 0.0 copy-start
  20.1 0.7 copy-done
  20.8 0.7 copy-done.2
  21.5 0.5 all-to-all-done.own_ref
  22.0 3.0 %collective-permute-start.2 = (f32[8,12,8,256]{3,2,1,0:T(8,128)S(1)}, f32[8,12,8,256]{3,2,1,0:T(8,128)S(1)}, u32[]{:S(2)}, u32[]{:S(2)}) collective-permute-start(f32[8,12,8,256]{3,2,1,0:T(8,128)S(1)} %all-to-all-done.own_ref), channel_id=1, source_target_pairs={{0,1},{1,0},{2,3},{3,2},{4,5},{5,4},{6,7},{7,6},{8,9},{9,8},{10,11... | collective-permute-start | bytes 2359304 | tf_op jit(solution)/shard_map/ppermute | solution.py:481
  25.0 3.6 %collective-permute-start.3 = (f32[448,128]{1,0:T(8,128)S(1)}, f32[448,128]{1,0:T(8,128)}, u32[]{:S(2)}, u32[]{:S(2)}) collective-permute-start(f32[448,128]{1,0:T(8,128)S(1)} %get-tuple-element.63.own_ref), channel_id=1, source_target_pairs={{0,64},{32,96},{64,0},{96,32},{1,65},{33,97},{65,1},{97,33},{2,66}... | collective-permute-start | bytes 688136 | tf_op jit(solution)/shard_map/ppermute | solution.py:554
  28.6 2.6 %flux_outer.1 = (f32[8,8192]{1,0:T(8,128)S(1)}, f32[8,12,8,256]{3,2,1,0:T(8,128)}) custom-call(s32[48]{0:T(128)S(1)} %tables.1.table_ref, f32[8,12,8,256]{3,2,1,0:T(8,128)S(1)} %all-to-all-done.own_ref, f32[8,12,8,256]{3,2,1,0:T(8,128)S(1)} %collective-permute-done.2.swapped_ref, f32[8,8192]{1,0:T(8,128)S(1)} %get-tuple-element.66.part_ref, ...), custom_call_target="tpu_custom_call" | custom-call | flops 1000000 | bytes 4194304 | tf_op jit(solution)/shard_map/flux_outer/pallas_call | solution.py:558
  31.2 3.6 %all-to-all-start.1 = ((f32[8,12,8,256]{3,2,1,0:T(8,128)}), f32[8,12,8,256]{3,2,1,0:T(8,128)S(1)}, u32[]{:S(2)}, u32[]{:S(2)}) async-start(f32[8,12,8,256]{3,2,1,0:T(8,128)} %get-tuple-element.71), calls=%async_computation.1 | async-start | bytes 1572864 | tf_op jit(solution)/shard_map/all_to_all | solution.py:473
  34.8 0.0 copy-start.1
  34.8 0.9 %copy-done.1 = f32[448,128]{1,0:T(8,128)S(1)} copy-done((f32[448,128]{1,0:T(8,128)S(1)}, f32[448,128]{1,0:T(8,128)}, u32[]{:S(2)}) %copy-start.1) | copy-done | bytes 229400
  35.7 0.9 %copy-done.3 = f32[448,128]{1,0:T(8,128)S(1)} copy-done((f32[448,128]{1,0:T(8,128)S(1)}, f32[448,128]{1,0:T(8,128)}, u32[]{:S(2)}) %copy-start.3) | copy-done | bytes 229400
  36.7 1.1 %mix.1 = (f32[448,128]{1,0:T(8,128)S(1)}, f32[448,128]{1,0:T(8,128)S(1)}) custom-call(f32[448,128]{1,0:T(8,128)S(1)} %get-tuple-element.63.own_ref, f32[448,128]{1,0:T(8,128)S(1)} %copy-done.1, f32[448,128]{1,0:T(8,128)} %collective-permute-done.3.two_ref, f32[448,128]{1,0:T(8,128)S(1)} %copy-done.3, f32[8,8192]{1,0:T(8,128)S(1)} %get-tuple-element.72.field_ref.first_ref), custom_call_target="tpu_custom_call" | custom-call | flops 1000000 | bytes 1376256 | tf_op jit(solution)/shard_map/mix/pallas_call | solution.py:508
  37.8 0.7 copy-done.4
  38.4 0.3 collective-permute-start.4
  38.8 3.7 %recon_inner.1 = (f32[8,8192]{1,0:T(8,128)S(1)}, bf16[7,8,8192]{2,1,0:T(8,128)(2,1)S(1)}, bf16[7,8,8192]{2,1,0:T(8,128)(2,1)S(1)}, bf16[4,7,8,256]{3,2,1,0:T(8,128)(2,1)S(1)}, f32[8,128]{1,0:T(8,128)S(1)}) custom-call(f32[8,8192]{1,0:T(8,128)S(1)} %get-tuple-element.72.field_ref.first_ref, bf16[1,7,7,7,8192]{4,3,2,1,0:T(8,128)(2,1)} %coeff_ref.3), custom_call_target="tpu_custom_call" | custom-call | flops 6000000000 | bytes 8388608 | tf_op jit(solution)/shard_map/recon_inner/pallas_call | solution.py:490
  42.5 0.0 copy-start.5
  42.5 0.0 copy-start.6
  42.5 6.6 %collective-permute-done.4.returned_ref = f32[448,128]{1,0:T(8,128)S(1)} collective-permute-done((f32[448,128]{1,0:T(8,128)S(1)}, f32[448,128]{1,0:T(8,128)S(1)}, u32[]{:S(2)}, u32[]{:S(2)}) %collective-permute-start.4) | collective-permute-done | bytes 229408 | tf_op jit(solution)/shard_map/ppermute | solution.py:517
  49.2 1.1 %collective-permute-start.5 = (f32[8,12,8,256]{3,2,1,0:T(8,128)S(1)}, f32[8,12,8,256]{3,2,1,0:T(8,128)S(1)}, u32[]{:S(2)}, u32[]{:S(2)}) collective-permute-start(f32[8,12,8,256]{3,2,1,0:T(8,128)S(1)} %all-to-all-done.1.own_ref), channel_id=1, source_target_pairs={{0,1},{1,0},{2,3},{3,2},{4,5},{5,4},{6,7},{7,6},{8,9},{9,8},{10,11... | collective-permute-start | bytes 2359304 | tf_op jit(solution)/shard_map/ppermute | solution.py:481
  50.2 2.8 %gram.1 = (f32[3584,128]{1,0:T(8,128)S(1)}, f32[8,128]{1,0:T(8,128)S(1)}) custom-call(f32[3584,128]{1,0:T(8,128)} %bitcast.31), custom_call_target="tpu_custom_call" | custom-call | flops 4128768 | bytes 2097152 | tf_op jit(solution)/shard_map/gram/pallas_call | solution.py:543
  53.1 1.8 %image.1 = (f32[448,128]{1,0:T(8,128)S(1)}, f32[128,128]{1,0:T(8,128)S(1)}) custom-call(s32[48]{0:T(128)S(1)} %tables.1.table_ref, f32[8,12,8,256]{3,2,1,0:T(8,128)S(1)} %all-to-all-done.1.own_ref, f32[8,12,8,256]{3,2,1,0:T(8,128)S(1)} %collective-permute-done.5.swapped_ref, f32[8,8192]{1,0:T(8,128)S(1)} %get-tuple-element.78.part_ref, ...), custom_call_target="tpu_custom_call" | custom-call | flops 1000000 | bytes 6291456 | tf_op jit(solution)/shard_map/image/pallas_call | solution.py:573
  54.9 0.0 copy-start.11
  54.9 18.6 %all_to_all.21 = f32[128,1,128]{2,1,0:T(1,128)S(1)} all-to-all(f32[128,1,128]{2,1,0:T(1,128)S(1)} %bitcast.25), channel_id=1, replica_groups=mesh['z'=4,'xl'=2,'xh'=2,'y'=4,'core'=2] {'z','xl','xh','y','core'}, dimensions={0} | all-to-all | bytes 131072 | tf_op jit(solution)/shard_map/all_to_all | solution.py:586
  73.5 1.3 %finish.1 = (f32[448,128]{1,0:T(8,128)}, f32[1,9]{1,0:T(1,128)S(1)}, s32[1]{0:T(128)}) custom-call(f32[128,128]{1,0:T(8,128)S(1)} %bitcast.24, f32[448,128]{1,0:T(8,128)S(1)} %get-tuple-element.115.image_ref, f32[3584,128]{1,0:T(8,128)S(1)} %get-tuple-element.82.basis_ref), custom_call_target="tpu_custom_call" | custom-call | flops 1000000 | bytes 3145728 | tf_op jit(solution)/shard_map/finish/pallas_call | solution.py:587
  74.8 0.7 while.11
  75.4 0.5 copy-done.14
  (23 shorter events, 0.1 us)
Async XLA Ops:
  0.6 13.9 %copy-start.8 = (s32[32,6]{0,1:T(8,128)S(1)}, s32[32,6]{0,1:T(8,128)}, u32[]{:S(2)}) copy-start(s32[32,6]{0,1:T(8,128)} %param.16) | copy-start | bytes 2308
  0.6 13.9 %copy-start.9 = (s32[32,6]{0,1:T(8,128)S(1)}, s32[32,6]{0,1:T(8,128)}, u32[]{:S(2)}) copy-start(s32[32,6]{0,1:T(8,128)} %param.17) | copy-start | bytes 2308
  0.7 13.9 %copy-start.10 = (s32[32]{0:T(128)S(1)}, s32[32]{0:T(128)}, u32[]{:S(2)}) copy-start(s32[32]{0:T(128)} %ids_ref.1) | copy-start | bytes 388
  3.1 18.9 %all-to-all-start = ((f32[8,12,8,256]{3,2,1,0:T(8,128)}), f32[8,12,8,256]{3,2,1,0:T(8,128)S(1)}, u32[]{:S(2)}, u32[]{:S(2)}) async-start(f32[8,12,8,256]{3,2,1,0:T(8,128)} %get-tuple-element.60), calls=%async_computation | async-start | bytes 1572864 | tf_op jit(solution)/shard_map/all_to_all | solution.py:473
  10.6 9.5 %collective-permute-start = (f32[448,128]{1,0:T(8,128)S(1)}, f32[448,128]{1,0:T(8,128)S(1)}, u32[]{:S(2)}, u32[]{:S(2)}) collective-permute-start(f32[448,128]{1,0:T(8,128)S(1)} %get-tuple-element.63.own_ref), channel_id=1, source_target_pairs={{0,32},{32,0},{64,96},{96,64},{1,33},{33,1},{65,97},{97,65},{2,34}... | collective-permute-start | bytes 688136 | tf_op jit(solution)/shard_map/ppermute | solution.py:554
  12.3 8.5 %collective-permute-start.1 = (f32[448,128]{1,0:T(8,128)S(1)}, f32[448,128]{1,0:T(8,128)S(1)}, u32[]{:S(2)}, u32[]{:S(2)}) collective-permute-start(f32[448,128]{1,0:T(8,128)S(1)} %get-tuple-element.63.own_ref), channel_id=1, source_target_pairs={{0,96},{32,64},{64,32},{96,0},{1,97},{33,65},{65,33},{97,1},{2,98}... | collective-permute-start | bytes 688136 | tf_op jit(solution)/shard_map/ppermute | solution.py:554
  20.1 0.7 copy-start
  20.8 0.7 copy-start.2
  22.0 6.6 %collective-permute-start.2 = (f32[8,12,8,256]{3,2,1,0:T(8,128)S(1)}, f32[8,12,8,256]{3,2,1,0:T(8,128)S(1)}, u32[]{:S(2)}, u32[]{:S(2)}) collective-permute-start(f32[8,12,8,256]{3,2,1,0:T(8,128)S(1)} %all-to-all-done.own_ref), channel_id=1, source_target_pairs={{0,1},{1,0},{2,3},{3,2},{4,5},{5,4},{6,7},{7,6},{8,9},{9,8},{10,11... | collective-permute-start | bytes 2359304 | tf_op jit(solution)/shard_map/ppermute | solution.py:481
  25.0 9.8 %collective-permute-start.3 = (f32[448,128]{1,0:T(8,128)S(1)}, f32[448,128]{1,0:T(8,128)}, u32[]{:S(2)}, u32[]{:S(2)}) collective-permute-start(f32[448,128]{1,0:T(8,128)S(1)} %get-tuple-element.63.own_ref), channel_id=1, source_target_pairs={{0,64},{32,96},{64,0},{96,32},{1,65},{33,97},{65,1},{97,33},{2,66}... | collective-permute-start | bytes 688136 | tf_op jit(solution)/shard_map/ppermute | solution.py:554
  31.2 17.9 %all-to-all-start.1 = ((f32[8,12,8,256]{3,2,1,0:T(8,128)}), f32[8,12,8,256]{3,2,1,0:T(8,128)S(1)}, u32[]{:S(2)}, u32[]{:S(2)}) async-start(f32[8,12,8,256]{3,2,1,0:T(8,128)} %get-tuple-element.71), calls=%async_computation.1 | async-start | bytes 1572864 | tf_op jit(solution)/shard_map/all_to_all | solution.py:473
  34.8 0.9 %copy-start.1 = (f32[448,128]{1,0:T(8,128)S(1)}, f32[448,128]{1,0:T(8,128)}, u32[]{:S(2)}) copy-start(f32[448,128]{1,0:T(8,128)} %copy-done) | copy-start | bytes 688132
  35.7 0.9 %copy-start.3 = (f32[448,128]{1,0:T(8,128)S(1)}, f32[448,128]{1,0:T(8,128)}, u32[]{:S(2)}) copy-start(f32[448,128]{1,0:T(8,128)} %copy-done.2) | copy-start | bytes 688132
  37.7 0.7 copy-start.4
  38.4 10.7 %collective-permute-start.4 = (f32[448,128]{1,0:T(8,128)S(1)}, f32[448,128]{1,0:T(8,128)S(1)}, u32[]{:S(2)}, u32[]{:S(2)}) collective-permute-start(f32[448,128]{1,0:T(8,128)S(1)} %get-tuple-element.76), channel_id=1, source_target_pairs={{0,16},{16,0},{1,17},{17,1},{2,18},{18,2},{3,19},{19,3},{4,20},{20... | collective-permute-start | bytes 688136 | tf_op jit(solution)/shard_map/ppermute | solution.py:517
  42.5 10.6 %copy-start.5 = (f32[448,128]{1,0:T(8,128)S(1)}, f32[448,128]{1,0:T(8,128)}, u32[]{:S(2)}) copy-start(f32[448,128]{1,0:T(8,128)} %copy-done.4) | copy-start | bytes 688132
  42.5 10.6 %copy-start.6 = (f32[8192]{0:T(1024)S(1)}, f32[8192]{0:T(1024)}, u32[]{:S(2)}) copy-start(f32[8192]{0:T(1024)} %param.13) | copy-start | bytes 98308
  42.5 10.6 %copy-start.7 = (f32[8192]{0:T(1024)S(1)}, f32[8192]{0:T(1024)}, u32[]{:S(2)}) copy-start(f32[8192]{0:T(1024)} %param.14) | copy-start | bytes 98308
  49.2 3.9 %collective-permute-start.5 = (f32[8,12,8,256]{3,2,1,0:T(8,128)S(1)}, f32[8,12,8,256]{3,2,1,0:T(8,128)S(1)}, u32[]{:S(2)}, u32[]{:S(2)}) collective-permute-start(f32[8,12,8,256]{3,2,1,0:T(8,128)S(1)} %all-to-all-done.1.own_ref), channel_id=1, source_target_pairs={{0,1},{1,0},{2,3},{3,2},{4,5},{5,4},{6,7},{7,6},{8,9},{9,8},{10,11... | collective-permute-start | bytes 2359304 | tf_op jit(solution)/shard_map/ppermute | solution.py:481
  54.9 19.9 %copy-start.12 = (f32[448,128]{1,0:T(8,128)}, f32[448,128]{1,0:T(8,128)S(1)}, u32[]{:S(2)}) copy-start(f32[448,128]{1,0:T(8,128)S(1)} %get-tuple-element.115.image_ref) | copy-start | bytes 688132
  54.9 19.9 %copy-start.11 = (f32[8,1,7,8192]{3,1,2,0:T(1,128)S(1)}, f32[8,1,7,8192]{3,1,2,0:T(1,128)}, u32[]{:S(2)}) copy-start(f32[8,1,7,8192]{3,1,2,0:T(1,128)} %param.10) | copy-start | bytes 5505028
  75.4 0.5 copy-start.14

commit v4 on v3

--- a/solution.py
+++ b/solution.py
@@ -30,11 +30,11 @@
 GUARD = 0.02
 CHUNK = 4
 FLUX_INNER = 10**7
-INNER_MIB = 50
+INNER_MIB = 46
 OUTER_MIB = 16
 MIX = 10**6
 FLUX_OUTER = 10**6
-RECON_INNER = 6 * 10**9
+RECON_INNER = 2 * 10**10
 
 
 def mixing_weights():
@@ -128,51 +128,109 @@
         copy.wait()
 
 
-def tables_kernel(ids_ref, neighbour_ref, orient_ref, table_ref, position):
+PART_OF = (4, 0, 1, 0, 1, 2, 3, 2)
+CORE_OF = (0, 0, 0, 1, 1, 0, 0, 1)
+
+
+def tables_kernel(ids_ref, neighbour_ref, orient_ref, table_ref, later_ref, position):
     core = lax.axis_index("core")
-    rank = (lax.axis_index("xh") * 4 + lax.axis_index("y")) * 2 + core
+    chip = lax.axis_index("xh") * 4 + lax.axis_index("y")
 
     def place(slot, carry):
         position[ids_ref[slot]] = slot
         return carry
 
     lax.fori_loop(0, BLOCKS, place, 0)
+
+    def pick_of(values, index):
+        result = jnp.int32(values[0])
+        for k in range(1, len(values)):
+            result = jnp.where(index == k, jnp.int32(values[k]), result)
+        return result
+
+    for mine in (True, False):
+        for number in range(FACES):
+            rank = chip * 2 + (core if mine else 1 - core)
+            owner = ids_ref[rank * PER + number // 6]
+            partner = neighbour_ref[number % 6, owner]
+            target = jnp.maximum(partner, 0)
+            slot = position[target // 6]
+            device = slot // PER
+            row = (slot % PER) * 6 + target % 6
+            source_core = device % 2
+            offset = (device // 2) ^ chip
+            part = pick_of(PART_OF, offset)
+            among = jnp.where(source_core == core, row, row + FACES)
+            if mine:
+                code = jnp.where(partner < 0, -1, orient_ref[number % 6, owner])
+                same = source_core == core
+                table_ref[number * 4] = device // 2
+                table_ref[number * 4 + 1] = jnp.where(same, 1, 0)
+                table_ref[number * 4 + 2] = row
+                table_ref[number * 4 + 3] = code
+                here = jnp.where(
+                    part == 4, True, jnp.where(part == 3, same, pick_of(CORE_OF, offset) == core)
+                )
+                later_ref[number * 5] = part
+                later_ref[number * 5 + 1] = among
+                later_ref[number * 5 + 2] = row
+                later_ref[number * 5 + 3] = jnp.where(here, 1, 0)
+                later_ref[number * 5 + 4] = code
+            else:
+                later_ref[5 * FACES + number * 3] = part
+                later_ref[5 * FACES + number * 3 + 1] = among
+                later_ref[5 * FACES + number * 3 + 2] = row
+
+
+def choose(parts, part, among, row):
+    value = parts[4][among]
+    for k in range(3):
+        value = jnp.where(part == k, parts[k][among], value)
+    return jnp.where(part == 3, parts[3][row], value)
+
+
+def select_kernel(
+    later_ref, one_ref, two_ref, three_ref, four_ref, chip_ref, token_ref, wanted_ref
+):
+    parts = (one_ref, two_ref, three_ref, four_ref, chip_ref)
     for number in range(FACES):
-        owner = ids_ref[rank * PER + number // 6]
-        partner = neighbour_ref[number % 6, owner]
-        code = orient_ref[number % 6, owner]
-        target = jnp.maximum(partner, 0)
-        slot = position[target // 6]
-        device = slot // PER
-        table_ref[number * 4] = device // 2
-        table_ref[number * 4 + 1] = jnp.where(device % 2 == core, 1, 0)
-        table_ref[number * 4 + 2] = (slot % PER) * 6 + target % 6
-        table_ref[number * 4 + 3] = jnp.where(partner < 0, -1, code)
+        base = 5 * FACES + number * 3
+        wanted_ref[number] = choose(parts, later_ref[base], later_ref[base + 1], later_ref[base + 2])
+
+
+def turn_face(source, code, halos, number):
+    lane = lanes((8, LANES))
+    source = jnp.where(code < 0, 0.0, source)
+    code = jnp.maximum(code, 0)
+    low, high = (source[:, :LANES], source[:, LANES:])
+    transposed = code & 1 == 1
+    flip_a = (code >> 1 & 1) * (EDGE - 1)
+    flip_b = (code >> 2) * (EDGE - 1)
+    for half in range(2):
+        a = ((lane >> 4) + half * 8) ^ flip_a
+        b = (lane & 15) ^ flip_b
+        index = jnp.where(transposed, (b << 4) + a, (a << 4) + b)
+        inside = index & (LANES - 1)
+        halos[number, :, half * LANES : (half + 1) * LANES] = jnp.where(
+            index < LANES, pick(low, inside), pick(high, inside)
+        )
 
 
 def fetch_halos(table_ref, own_ref, swapped_ref, halos):
-    lane = lanes((8, LANES))
     for number in range(FACES):
         chip = table_ref[number * 4]
         here = table_ref[number * 4 + 1] == 1
         row = table_ref[number * 4 + 2]
-        code = table_ref[number * 4 + 3]
-        wall = code < 0
-        code = jnp.maximum(code, 0)
         source = jnp.where(here, own_ref[chip, row], swapped_ref[chip, row])
-        source = jnp.where(wall, 0.0, source)
-        low, high = (source[:, :LANES], source[:, LANES:])
-        transposed = code & 1 == 1
-        flip_a = (code >> 1 & 1) * (EDGE - 1)
-        flip_b = (code >> 2) * (EDGE - 1)
-        for half in range(2):
-            a = ((lane >> 4) + half * 8) ^ flip_a
-            b = (lane & 15) ^ flip_b
-            index = jnp.where(transposed, (b << 4) + a, (a << 4) + b)
-            inside = index & (LANES - 1)
-            halos[number, :, half * LANES : (half + 1) * LANES] = jnp.where(
-                index < LANES, pick(low, inside), pick(high, inside)
-            )
+        turn_face(source, table_ref[number * 4 + 3], halos, number)
+
+
+def fetch_later_halos(later_ref, parts, swapped_ref, halos):
+    for number in range(FACES):
+        base = number * 5
+        source = choose(parts, later_ref[base], later_ref[base + 1], later_ref[base + 2])
+        source = jnp.where(later_ref[base + 3] == 1, source, swapped_ref[number])
+        turn_face(source, later_ref[base + 4], halos, number)
 
 
 def inner_kernel(
@@ -302,24 +360,20 @@
 
 
 def flux_kernel(
-    table_ref, own_ref, swapped_ref, part_ref, across_z_ref, across_y_ref, across_x_ref, token_ref,
-    first_ref, sent_ref, halos, faces, arrived
+    table_ref, own_ref, swapped_ref, part_ref, across_z_ref, across_y_ref, across_x_ref, token_ref, mixed_ref,
+    first_ref, faces_ref, halos
 ):
     fetch_halos(table_ref, own_ref, swapped_ref, halos)
 
     def put(k, slab):
         first_ref[:, k * SQUARE : (k + 1) * SQUARE] = slab
 
-    copies = []
     for block in range(PER):
         outer_block(across_x_ref, part_ref, across_z_ref, across_y_ref, halos, block, put)
-        collect_block(first_ref, faces, block)
-        copies += send_block(faces, sent_ref, arrived, block)
-    for copy in copies:
-        copy.wait()
-
-
-def mix_kernel(own_ref, one_ref, two_ref, three_ref, first_ref, kept_ref, given_ref):
+        collect_block(first_ref, faces_ref, block)
+
+
+def mix_kernel(own_ref, one_ref, two_ref, three_ref, kept_ref, given_ref, token_ref):
     z = lax.axis_index("z")
     xl = lax.axis_index("xl")
     table = mixing_weights()
@@ -344,6 +398,7 @@
         return carry
 
     lax.fori_loop(0, ROWS // 64, step, 0)
+    token_ref[...] = jnp.zeros_like(token_ref)
 
 
 def lane_sums(rows, first_lane):
@@ -352,7 +407,7 @@
     return jnp.sum(jnp.where(spot, totals, 0.0), axis=0, keepdims=True)
 
 
-def gram_kernel(flat_ref, basis_ref, gram_ref, lines, arrived):
+def gram_kernel(flat_ref, gram_ref, basis_ref, lines, arrived):
     copy = pltpu.make_async_copy(flat_ref, basis_ref, arrived)
     copy.start()
     copy.wait()
@@ -380,11 +435,14 @@
 
 
 def image_kernel(
-    table_ref, own_ref, swapped_ref, part_ref, across_z_ref, across_y_ref, across_x_ref,
-    basis_ref, pseudo_ref, omega_ref, kept_ref, returned_ref, gram_ref, token_ref,
-    image_ref, sums_ref, halos, section
+    later_ref, one_ref, two_ref, three_ref, four_ref, chip_ref, swapped_ref,
+    part_ref, across_z_ref, across_y_ref, across_x_ref,
+    flat_ref, pseudo_ref, omega_ref, kept_ref, returned_ref, gram_ref,
+    image_ref, sums_ref, basis_ref, halos, section, arrived
 ):
-    fetch_halos(table_ref, own_ref, swapped_ref, halos)
+    copy = pltpu.make_async_copy(flat_ref, basis_ref, arrived)
+    copy.start()
+    fetch_later_halos(later_ref, (one_ref, two_ref, three_ref, four_ref, chip_ref), swapped_ref, halos)
 
     def put(k, slab):
         section[pl.ds(2 * k, 8, stride=GROUPS), :] = slab[:, :LANES]
@@ -392,6 +450,7 @@
 
     for block in range(PER):
         outer_block(across_x_ref, part_ref, across_z_ref, across_y_ref, halos, block, put)
+    copy.wait()
 
     def step(k, totals):
         start = k * 8
@@ -477,6 +536,26 @@
     return lax.optimization_barrier((value, others))
 
 
+def split_pairs(first, second):
+    pairs = []
+    for chip in range(CHIP_COUNT):
+        pairs.append((chip * 2, (chip ^ first) * 2))
+        pairs.append((chip * 2 + 1, (chip ^ second) * 2 + 1))
+    return pairs
+
+
+def second_exchange(faces):
+    space = ("xh", "y", "core")
+    chip = jnp.concatenate([faces, swap_cores(faces)])
+    return (
+        lax.ppermute(chip, space, split_pairs(1, 3)),
+        lax.ppermute(chip, space, split_pairs(2, 4)),
+        lax.ppermute(chip, space, split_pairs(5, 7)),
+        lax.ppermute(faces, space, split_pairs(6, 6)),
+        chip,
+    )
+
+
 def swap_cores(own):
     return lax.ppermute(own, "core", swap(2, 1))
 
@@ -504,17 +583,16 @@
     )(field, coeff)
 
 
-def mix(parts, first):
-    kept, given = pl.pallas_call(
+def mix(parts):
+    return pl.pallas_call(
         mix_kernel,
-        in_specs=[whole()] * 4 + [whole(pl.ANY)],
-        out_specs=[whole()] * 2,
-        out_shape=[f32(ROWS, LANES), f32(ROWS, LANES)],
+        in_specs=[whole()] * 4,
+        out_specs=[whole()] * 3,
+        out_shape=[f32(ROWS, LANES), f32(ROWS, LANES), f32(8, LANES)],
         compiler_params=params(8),
         cost_estimate=cost(MIX, 6 * 4 * ROWS * LANES),
         name="mix",
-    )(*parts, first)
-    return kept, lax.ppermute(given, "xl", swap(2, 1))
+    )(*parts)
 
 
 def local(basis, flux, recon, pseudo_time, vol_omega, block_ids, neighbour, orient):
@@ -530,58 +608,72 @@
         name="first_faces",
     )(flat)
     own = exchange(sent)
-    table = pl.pallas_call(
+    table, later = pl.pallas_call(
         tables_kernel,
         in_specs=[whole(SMEM)] * 3,
-        out_specs=whole(SMEM),
-        out_shape=jax.ShapeDtypeStruct((4 * FACES,), jnp.int32),
+        out_specs=[whole(SMEM), whole(SMEM)],
+        out_shape=[
+            jax.ShapeDtypeStruct((4 * FACES,), jnp.int32),
+            jax.ShapeDtypeStruct((8 * FACES,), jnp.int32),
+        ],
         scratch_shapes=[SMEM((BLOCKS,), jnp.int32)],
         compiler_params=params(4),
         cost_estimate=cost(10**5, 10**5),
         name="tables",
     )(block_ids, neighbour.T, orient.T)
-    held, gram = pl.pallas_call(
+    *pieces, token = inner_section(padded, flux, "flux_inner", FLUX_INNER)
+    gram = pl.pallas_call(
         gram_kernel,
         in_specs=[whole(pl.ANY)],
-        out_specs=[whole(), whole()],
-        out_shape=[f32(KRYLOV * ROWS, LANES), f32(8, LANES)],
-        scratch_shapes=[VMEM((KRYLOV * KRYLOV, LANES), jnp.float32), pltpu.SemaphoreType.DMA],
+        out_specs=whole(),
+        out_shape=f32(8, LANES),
+        scratch_shapes=[
+            VMEM((KRYLOV * ROWS, LANES), jnp.float32),
+            VMEM((KRYLOV * KRYLOV, LANES), jnp.float32),
+            pltpu.SemaphoreType.DMA,
+        ],
         compiler_params=params(8),
         cost_estimate=cost(2 * 36 * VARS * CELLS, 2 * 2**20),
         name="gram",
     )(flat)
-    *pieces, token = inner_section(padded, flux, "flux_inner", FLUX_INNER)
-    one, two, three = [lax.ppermute(dense, "z", swap(4, k)) for k in (1, 2, 3)]
-    own, (token, table, one, three) = after(own, (token, table, one, three))
-    parts = (dense, one, two, three)
+    kept, given, mixed = mix([dense] + [lax.ppermute(dense, "z", swap(4, k)) for k in (1, 2, 3)])
+    own, (token, table, mixed, gram) = after(own, (token, table, mixed, gram))
     swapped = swap_cores(own)
-    first, sent = pl.pallas_call(
+    first, faces = pl.pallas_call(
         flux_kernel,
-        in_specs=[whole(SMEM)] + [whole()] * 6 + [whole(pl.ANY)],
-        out_specs=[whole(), whole(pl.ANY)],
-        out_shape=[f32(8, CELLS), SENT],
-        scratch_shapes=[FACES_VMEM, FACES_VMEM, pltpu.SemaphoreType.DMA((PER, CHIP_COUNT))],
+        in_specs=[whole(SMEM)] + [whole()] * 6 + [whole(pl.ANY)] * 2,
+        out_specs=[whole(), whole()],
+        out_shape=[f32(8, CELLS), f32(FACES, 8, SQUARE)],
+        scratch_shapes=[FACES_VMEM],
         compiler_params=params(OUTER_MIB),
         cost_estimate=cost(FLUX_OUTER, 4 * 2**20),
         name="flux_outer",
-    )(table, own, swapped, *pieces, token)
-    own = exchange(sent)
-    kept, returned = mix(parts, first)
+    )(table, own, swapped, *pieces, token, mixed)
+    returned = lax.ppermute(given, "xl", swap(2, 1))
     *pieces, token = inner_section(first, recon, "recon_inner", RECON_INNER)
-    own, (token, returned) = after(own, (token, returned))
-    swapped = swap_cores(own)
-    image, sums = pl.pallas_call(
+    parts = second_exchange(faces)
+    wanted = pl.pallas_call(
+        select_kernel,
+        in_specs=[whole(SMEM)] + [whole()] * 5 + [whole(pl.ANY)],
+        out_specs=whole(),
+        out_shape=f32(FACES, 8, SQUARE),
+        compiler_params=params(4),
+        cost_estimate=cost(10**5, 10**6),
+        name="select",
+    )(later, *parts, token)
+    swapped = swap_cores(wanted)
+    image, sums, held = pl.pallas_call(
         image_kernel,
-        in_specs=[whole(SMEM)] + [whole()] * 12 + [whole(pl.ANY)],
-        out_specs=[whole(), whole()],
-        out_shape=[f32(ROWS, LANES), f32(LANES, LANES)],
-        scratch_shapes=[FACES_VMEM, VMEM((8 * GROUPS, LANES), jnp.float32)],
+        in_specs=[whole(SMEM)] + [whole()] * 10 + [whole(pl.ANY)] + [whole()] * 5,
+        out_specs=[whole(), whole(), whole()],
+        out_shape=[f32(ROWS, LANES), f32(LANES, LANES), f32(KRYLOV * ROWS, LANES)],
+        scratch_shapes=[FACES_VMEM, VMEM((8 * GROUPS, LANES), jnp.float32), pltpu.SemaphoreType.DMA],
         compiler_params=params(OUTER_MIB),
         cost_estimate=cost(10**6, 6 * 2**20),
         name="image",
     )(
-        table, own, swapped, *pieces,
-        held, pseudo_time.reshape(GROUPS, LANES), vol_omega.reshape(GROUPS, LANES), kept, returned, gram, token,
+        later, *parts, swapped, *pieces,
+        flat, pseudo_time.reshape(GROUPS, LANES), vol_omega.reshape(GROUPS, LANES), kept, returned, gram,
     )
     received = lax.all_to_all(sums, ALL, 0, 0)
     following, column, flag = pl.pallas_call(

time: 76.4 us -> 72.5 us (0.949)
  local copies, waits for them, and re-layouts: 4.48 us -> 1.23 us
  starting transfers between devices: 22.9 us -> 25.6 us
  blocking collectives: 18.6 us -> 15.9 us
  Pallas kernels: 21.3 us -> 19.5 us
  waiting for transfers between devices: 7.15 us -> 8.41 us
    ppermute x4 -> x8, starting transfers between devices: 7.79 us -> 15.5 us  [the longest x1 5.37 us: second_exchange(): lax.ppermute(faces, space, split_pairs(6, 6))]
    ppermute x2 -> x3, waiting for transfers between devices: 0.01 us -> 3.81 us  [swap_cores(): return lax.ppermute(own, 'core', swap(2, 1))]
    all_to_all x2 -> x1, starting transfers between devices: 11 us -> 7.49 us  [exchange(): return lax.all_to_all(sent, CHIPS, 0, 0)]
    unnamed x28 -> x19, local copies, waits for them, and re-layouts: 4.48 us -> 1.23 us
    all_to_all x1, blocking collectives: 18.6 us -> 15.9 us  [local(): received = lax.all_to_all(sums, ALL, 0, 0)]
    ppermute x4 -> x8, waiting for transfers between devices: 6.63 us -> 4.59 us  [the longest x3 2.23 us: local(): lax.ppermute(dense, 'z', swap(4, k))]
    ppermute x2 -> x3, starting transfers between devices: 4.03 us -> 2.56 us  [swap_cores(): return lax.ppermute(own, 'core', swap(2, 1))]
    pallas_call x4 -> x5, Pallas kernels: 7.47 us -> 6.37 us  [the longest x1 2.23 us: local(): pl.pallas_call(tables_kernel, in_specs=[whole(SMEM)] * 3, out_specs=[whol...]
  transfers between devices with their start and end apart: 8 -> 12, of which waited for: 2 -> 8; matrix products, arithmetic and copies ran while one was open for 0% -> 0% of each run, Pallas kernels for 21% -> 19%
where the time goes in v4:
time: 72.5 us; the launch traced here: 72.3 us
  starting transfers between devices  25.6 us (35%)
  Pallas kernels  19.5 us (27%)
  blocking collectives  15.9 us (22%)
  waiting for transfers between devices  8.41 us (12%)
  local copies, waits for them, and re-layouts  1.23 us (2%)
  loops' own time  0.83 us (1%)
  between operations  0.81 us (1%)
    all_to_all x1, blocking collectives, local(): received = lax.all_to_all(sums, ALL, 0, 0)  15.9 us
    pallas_call x2, Pallas kernels, inner_section(): pl.pallas_call(inner_kernel, in_specs=[whole(), whole(pltpu.HBM)], out_sp...  7.62 us
    all_to_all x1, starting transfers between devices, exchange(): return lax.all_to_all(sent, CHIPS, 0, 0)  7.49 us
    ppermute x1, starting transfers between devices, second_exchange(): lax.ppermute(faces, space, split_pairs(6, 6))  5.37 us
    ppermute x3, starting transfers between devices, local(): lax.ppermute(dense, 'z', swap(4, k))  4.42 us
    ppermute x3, waiting for transfers between devices, swap_cores(): return lax.ppermute(own, 'core', swap(2, 1))  3.81 us
    ppermute x1, starting transfers between devices, second_exchange(): lax.ppermute(chip, space, split_pairs(2, 4))  2.69 us
    pallas_call x1, Pallas kernels, local(): pl.pallas_call(first_faces_kernel, in_specs=[whole(pl.ANY)], out_specs=[w...  2.58 us
  transfers between devices with their start and end apart: 12, of which 8 were waited for; matrix products, arithmetic and copies ran while one was open for 0% of the time, Pallas kernels for 19%

profile of v4, /device:TPU:1, one launch (start us, length us, event | category | flops | bytes accessed | tf_op | source)
XLA Modules:
  0.0 72.3 jit_solution(12212420995491235843)
XLA Ops:
  0.7 2.6 %first_faces.1 = (f32[8,12,8,256]{3,2,1,0:T(8,128)}, f32[8,8192]{1,0:T(8,128)S(1)}, f32[448,128]{1,0:T(8,128)S(1)}) custom-call(f32[3584,128]{1,0:T(8,128)} %bitcast.30), custom_call_target="tpu_custom_call" | custom-call | flops 1000000 | bytes 2097152 | tf_op jit(solution)/shard_map/first_faces/pallas_call | solution.py:600
  3.3 7.5 %all-to-all-start = ((f32[8,12,8,256]{3,2,1,0:T(8,128)}), f32[8,12,8,256]{3,2,1,0:T(8,128)S(1)}, u32[]{:S(2)}, u32[]{:S(2)}) async-start(f32[8,12,8,256]{3,2,1,0:T(8,128)} %get-tuple-element.60), calls=%async_computation | async-start | bytes 1572864 | tf_op jit(solution)/shard_map/all_to_all | solution.py:532
  10.7 3.8 %collective-permute-start.2 = (f32[448,128]{1,0:T(8,128)S(1)}, f32[448,128]{1,0:T(8,128)S(1)}, u32[]{:S(2)}, u32[]{:S(2)}) collective-permute-start(f32[448,128]{1,0:T(8,128)S(1)} %get-tuple-element.64.own_ref), channel_id=1, source_target_pairs={{0,96},{32,64},{64,32},{96,0},{1,97},{33,65},{65,33},{97,1},{2,98}... | collective-permute-start | bytes 688136 | tf_op jit(solution)/shard_map/ppermute | solution.py:639
  14.5 0.7 collective-permute-start
  15.2 2.2 %tables.1 = (s32[48]{0:T(128)S(1)}, s32[96]{0:T(128)S(1)}) custom-call(s32[32]{0:T(128)S(1)} %copy-done.4, s32[6,32]{1,0:T(8,128)S(1)} %bitcast.28, s32[6,32]{1,0:T(8,128)S(1)} %bitcast.29), custom_call_target="tpu_custom_call" | custom-call | flops 100000 | bytes 100000 | tf_op jit(solution)/shard_map/tables/pallas_call | solution.py:611
  17.4 1.4 %gram.1.gram_ref = f32[8,128]{1,0:T(8,128)S(1)} custom-call(f32[3584,128]{1,0:T(8,128)S(1)} %bitcast.31), custom_call_target="tpu_custom_call" | custom-call | flops 4128768 | bytes 2097152 | tf_op jit(solution)/shard_map/gram/pallas_call | solution.py:625
  18.9 3.7 %flux_inner.1 = (f32[8,8192]{1,0:T(8,128)S(1)}, bf16[7,8,8192]{2,1,0:T(8,128)(2,1)S(1)}, bf16[7,8,8192]{2,1,0:T(8,128)(2,1)S(1)}, bf16[4,7,8,256]{3,2,1,0:T(8,128)(2,1)S(1)}, f32[8,128]{1,0:T(8,128)S(1)}) custom-call(f32[8,8192]{1,0:T(8,128)S(1)} %get-tuple-element.61.field_ref, bf16[1,7,7,7,8192]{4,3,2,1,0:T(8,128)(2,1)} %coeff_ref.2), custom_call_target="tpu_custom_call" | custom-call | flops 10000000 | bytes 8388608 | tf_op jit(solution)/shard_map/flux_inner/pallas_call | solution.py:569
  22.6 1.7 %collective-permute-done.2.three_ref = f32[448,128]{1,0:T(8,128)S(1)} collective-permute-done((f32[448,128]{1,0:T(8,128)S(1)}, f32[448,128]{1,0:T(8,128)S(1)}, u32[]{:S(2)}, u32[]{:S(2)}) %collective-permute-start.2) | collective-permute-done | bytes 229408 | tf_op jit(solution)/shard_map/ppermute | solution.py:639
  24.3 0.6 collective-permute-done.one_ref
  24.9 0.1 mix.1
  25.0 0.7 copy-done.5
  25.7 1.8 %collective-permute-start.3 = (f32[8,12,8,256]{3,2,1,0:T(8,128)S(1)}, f32[8,12,8,256]{3,2,1,0:T(8,128)S(1)}, u32[]{:S(2)}, u32[]{:S(2)}) collective-permute-start(f32[8,12,8,256]{3,2,1,0:T(8,128)S(1)} %all-to-all-done.own_ref), channel_id=1, source_target_pairs={{0,1},{1,0},{2,3},{3,2},{4,5},{5,4},{6,7},{7,6},{8,9},{9,8},{10,11... | collective-permute-start | bytes 2359304 | tf_op jit(solution)/shard_map/ppermute | solution.py:560
  27.5 0.3 collective-permute-start.10
  27.8 1.6 %collective-permute-done.3.swapped_ref = f32[8,12,8,256]{3,2,1,0:T(8,128)S(1)} collective-permute-done((f32[8,12,8,256]{3,2,1,0:T(8,128)S(1)}, f32[8,12,8,256]{3,2,1,0:T(8,128)S(1)}, u32[]{:S(2)}, u32[]{:S(2)}) %collective-permute-start.3) | collective-permute-done | bytes 786464 | tf_op jit(solution)/shard_map/ppermute | solution.py:560
  29.4 1.7 %flux_outer.1 = (f32[8,8192]{1,0:T(8,128)S(1)}, f32[12,8,256]{2,1,0:T(8,128)S(1)}) custom-call(s32[48]{0:T(128)S(1)} %get-tuple-element.66.table_ref, f32[8,12,8,256]{3,2,1,0:T(8,128)S(1)} %all-to-all-done.own_ref, f32[8,12,8,256]{3,2,1,0:T(8,128)S(1)} %collective-permute-done.3.swapped_ref, f32[8,8192]{1,0:T(8,128)S(1)} %get-tuple-element.68.part_ref, ...), custom_call_target="tpu_custom_call" | custom-call | flops 1000000 | bytes 4194304 | tf_op jit(solution)/shard_map/flux_outer/pallas_call | solution.py:642
  31.2 5.4 %collective-permute-start.8 = (f32[12,8,256]{2,1,0:T(8,128)S(1)}, f32[12,8,256]{2,1,0:T(8,128)S(1)}, u32[]{:S(2)}, u32[]{:S(2)}) collective-permute-start(f32[12,8,256]{2,1,0:T(8,128)S(1)} %get-tuple-element.74), channel_id=1, source_target_pairs={{0,12},{1,13},{2,14},{3,15},{4,8},{5,9},{6,10},{7,11},{8,4},{9,5},... | collective-permute-start | bytes 294920 | tf_op jit(solution)/shard_map/ppermute | solution.py:554
  36.5 0.7 collective-permute-start.4
  37.2 0.9 %collective-permute-done.4 = f32[12,8,256]{2,1,0:T(8,128)S(1)} collective-permute-done((f32[12,8,256]{2,1,0:T(8,128)S(1)}, f32[12,8,256]{2,1,0:T(8,128)S(1)}, u32[]{:S(2)}, u32[]{:S(2)}) %collective-permute-start.4) | collective-permute-done | bytes 98336 | tf_op jit(solution)/shard_map/ppermute | solution.py:560
  38.1 1.0 %collective-permute-start.7 = (f32[24,8,256]{2,1,0:T(8,128)S(1)}, f32[24,8,256]{2,1,0:T(8,128)S(1)}, u32[]{:S(2)}, u32[]{:S(2)}) collective-permute-start(f32[24,8,256]{2,1,0:T(8,128)S(1)} %constant_dynamic-update-slice_fusion.chip_ref), channel_id=1, source_target_pairs={{0,10},{1,15},{2,8},{3,13},{4,14},{5,11},{6,12},{7,9},{8,2},{9,7},... | collective-permute-start | bytes 589832 | tf_op jit(solution)/shard_map/ppermute | solution.py:553
  39.1 2.7 %collective-permute-start.6 = (f32[24,8,256]{2,1,0:T(8,128)S(1)}, f32[24,8,256]{2,1,0:T(8,128)S(1)}, u32[]{:S(2)}, u32[]{:S(2)}) collective-permute-start(f32[24,8,256]{2,1,0:T(8,128)S(1)} %constant_dynamic-update-slice_fusion.chip_ref), channel_id=1, source_target_pairs={{0,4},{1,9},{2,6},{3,11},{4,0},{5,13},{6,2},{7,15},{8,12},{9,1},{1... | collective-permute-start | bytes 589832 | tf_op jit(solution)/shard_map/ppermute | solution.py:552
  41.8 1.8 %collective-permute-start.5 = (f32[24,8,256]{2,1,0:T(8,128)S(1)}, f32[24,8,256]{2,1,0:T(8,128)S(1)}, u32[]{:S(2)}, u32[]{:S(2)}) collective-permute-start(f32[24,8,256]{2,1,0:T(8,128)S(1)} %constant_dynamic-update-slice_fusion.chip_ref), channel_id=1, source_target_pairs={{0,2},{1,7},{2,0},{3,5},{4,6},{5,3},{6,4},{7,1},{8,10},{9,15},{10,... | collective-permute-start | bytes 589832 | tf_op jit(solution)/shard_map/ppermute | solution.py:551
  43.6 3.9 %recon_inner.1 = (f32[8,8192]{1,0:T(8,128)S(1)}, bf16[7,8,8192]{2,1,0:T(8,128)(2,1)S(1)}, bf16[7,8,8192]{2,1,0:T(8,128)(2,1)S(1)}, bf16[4,7,8,256]{3,2,1,0:T(8,128)(2,1)S(1)}, f32[8,128]{1,0:T(8,128)S(1)}) custom-call(f32[8,8192]{1,0:T(8,128)S(1)} %get-tuple-element.75.field_ref, bf16[1,7,7,7,8192]{4,3,2,1,0:T(8,128)(2,1)} %coeff_ref.3), custom_call_target="tpu_custom_call" | custom-call | flops 20000000000 | bytes 8388608 | tf_op jit(solution)/shard_map/recon_inner/pallas_call | solution.py:569
  47.5 0.4 collective-permute-done.7.three_ref
  47.8 1.2 %collective-permute-done.6.two_ref = f32[24,8,256]{2,1,0:T(8,128)S(1)} collective-permute-done((f32[24,8,256]{2,1,0:T(8,128)S(1)}, f32[24,8,256]{2,1,0:T(8,128)S(1)}, u32[]{:S(2)}, u32[]{:S(2)}) %collective-permute-start.6) | collective-permute-done | bytes 196640 | tf_op jit(solution)/shard_map/ppermute | solution.py:552
  49.1 0.8 %collective-permute-done.5.one_ref = f32[24,8,256]{2,1,0:T(8,128)S(1)} collective-permute-done((f32[24,8,256]{2,1,0:T(8,128)S(1)}, f32[24,8,256]{2,1,0:T(8,128)S(1)}, u32[]{:S(2)}, u32[]{:S(2)}) %collective-permute-start.5) | collective-permute-done | bytes 196640 | tf_op jit(solution)/shard_map/ppermute | solution.py:551
  49.8 0.6 select.1
  50.6 1.3 %collective-permute-done.9.swapped_ref = f32[12,8,256]{2,1,0:T(8,128)S(1)} collective-permute-done((f32[12,8,256]{2,1,0:T(8,128)S(1)}, f32[12,8,256]{2,1,0:T(8,128)S(1)}, u32[]{:S(2)}, u32[]{:S(2)}) %collective-permute-start.9) | collective-permute-done | bytes 98336 | tf_op jit(solution)/shard_map/ppermute | solution.py:560
  51.9 1.9 %image.1 = (f32[448,128]{1,0:T(8,128)S(1)}, f32[128,128]{1,0:T(8,128)S(1)}, f32[3584,128]{1,0:T(8,128)S(1)}) custom-call(s32[96]{0:T(128)S(1)} %get-tuple-element.59.later_ref, f32[24,8,256]{2,1,0:T(8,128)S(1)} %collective-permute-done.5.one_ref, f32[24,8,256]{2,1,0:T(8,128)S(1)} %collective-permute-done.6.two_ref, ...), custom_call_target="tpu_custom_call" | custom-call | flops 1000000 | bytes 6291456 | tf_op jit(solution)/shard_map/image/pallas_call | solution.py:665
  53.8 15.9 %all_to_all.16 = f32[128,1,128]{2,1,0:T(1,128)S(1)} all-to-all(f32[128,1,128]{2,1,0:T(1,128)S(1)} %bitcast.25), channel_id=1, replica_groups=mesh['z'=4,'xl'=2,'xh'=2,'y'=4,'core'=2] {'z','xl','xh','y','core'}, dimensions={0} | all-to-all | bytes 131072 | tf_op jit(solution)/shard_map/all_to_all | solution.py:678
  69.7 1.3 %finish.1 = (f32[448,128]{1,0:T(8,128)}, f32[1,9]{1,0:T(1,128)S(1)}, s32[1]{0:T(128)}) custom-call(f32[128,128]{1,0:T(8,128)S(1)} %bitcast.24, f32[448,128]{1,0:T(8,128)S(1)} %get-tuple-element.113.image_ref, f32[3584,128]{1,0:T(8,128)S(1)} %get-tuple-element.86.basis_ref), custom_call_target="tpu_custom_call" | custom-call | flops 1000000 | bytes 3145728 | tf_op jit(solution)/shard_map/finish/pallas_call | solution.py:679
  71.0 0.8 %while.11 = (f32[448,128]{1,0:T(8,128)}, f32[1,9]{1,0:T(1,128)S(1)}, s32[]{:T(128)}, f32[8,1,7,8192]{3,1,2,0:T(1,128)S(1)}, f32[448,128]{1,0:T(8,128)S(1)}) while((f32[448,128]{1,0:T(8,128)}, f32[1,9]{1,0:T(1,128)S(1)}, s32[]{:T(128)}, f32[8,1,7,8192]{3,1,2,0:T(1,128)S(1)}, f32[448,128]{1,0:T(8,128)S(1)}) %tuple.23), condition=%region_3.0_spmd, body=%region_0.0_spmd | while | flops 5734412 | bytes 3211541 | solution.py:699
  71.8 0.5 copy-done.8
  (24 shorter events, 0.2 us)
Async XLA Ops:
  0.6 16.8 %copy-start.6 = (f32[8,1,7,8192]{3,1,2,0:T(1,128)S(1)}, f32[8,1,7,8192]{3,1,2,0:T(1,128)}, u32[]{:S(2)}) copy-start(f32[8,1,7,8192]{3,1,2,0:T(1,128)} %param.10) | copy-start | bytes 5505028
  0.6 14.5 %copy-start.3 = (s32[32,6]{0,1:T(8,128)S(1)}, s32[32,6]{0,1:T(8,128)}, u32[]{:S(2)}) copy-start(s32[32,6]{0,1:T(8,128)} %param.17) | copy-start | bytes 2308
  0.7 14.5 %copy-start.2 = (s32[32,6]{0,1:T(8,128)S(1)}, s32[32,6]{0,1:T(8,128)}, u32[]{:S(2)}) copy-start(s32[32,6]{0,1:T(8,128)} %param.16) | copy-start | bytes 2308
  0.7 14.5 %copy-start.4 = (s32[32]{0:T(128)S(1)}, s32[32]{0:T(128)}, u32[]{:S(2)}) copy-start(s32[32]{0:T(128)} %ids_ref.1) | copy-start | bytes 388
  3.3 22.4 %all-to-all-start = ((f32[8,12,8,256]{3,2,1,0:T(8,128)}), f32[8,12,8,256]{3,2,1,0:T(8,128)S(1)}, u32[]{:S(2)}, u32[]{:S(2)}) async-start(f32[8,12,8,256]{3,2,1,0:T(8,128)} %get-tuple-element.60), calls=%async_computation | async-start | bytes 1572864 | tf_op jit(solution)/shard_map/all_to_all | solution.py:532
  10.7 13.6 %collective-permute-start.2 = (f32[448,128]{1,0:T(8,128)S(1)}, f32[448,128]{1,0:T(8,128)S(1)}, u32[]{:S(2)}, u32[]{:S(2)}) collective-permute-start(f32[448,128]{1,0:T(8,128)S(1)} %get-tuple-element.64.own_ref), channel_id=1, source_target_pairs={{0,96},{32,64},{64,32},{96,0},{1,97},{33,65},{65,33},{97,1},{2,98}... | collective-permute-start | bytes 688136 | tf_op jit(solution)/shard_map/ppermute | solution.py:639
  14.5 9.8 %collective-permute-start.1 = (f32[448,128]{1,0:T(8,128)S(1)}, f32[448,128]{1,0:T(8,128)S(1)}, u32[]{:S(2)}, u32[]{:S(2)}) collective-permute-start(f32[448,128]{1,0:T(8,128)S(1)} %get-tuple-element.64.own_ref), channel_id=1, source_target_pairs={{0,64},{32,96},{64,0},{96,32},{1,65},{33,97},{65,1},{97,33},{2,66}... | collective-permute-start | bytes 688136 | tf_op jit(solution)/shard_map/ppermute | solution.py:639
  14.5 10.4 %collective-permute-start = (f32[448,128]{1,0:T(8,128)S(1)}, f32[448,128]{1,0:T(8,128)S(1)}, u32[]{:S(2)}, u32[]{:S(2)}) collective-permute-start(f32[448,128]{1,0:T(8,128)S(1)} %get-tuple-element.64.own_ref), channel_id=1, source_target_pairs={{0,32},{32,0},{64,96},{96,64},{1,33},{33,1},{65,97},{97,65},{2,34}... | collective-permute-start | bytes 688136 | tf_op jit(solution)/shard_map/ppermute | solution.py:639
  25.0 0.7 copy-start.5
  25.7 3.7 %collective-permute-start.3 = (f32[8,12,8,256]{3,2,1,0:T(8,128)S(1)}, f32[8,12,8,256]{3,2,1,0:T(8,128)S(1)}, u32[]{:S(2)}, u32[]{:S(2)}) collective-permute-start(f32[8,12,8,256]{3,2,1,0:T(8,128)S(1)} %all-to-all-done.own_ref), channel_id=1, source_target_pairs={{0,1},{1,0},{2,3},{3,2},{4,5},{5,4},{6,7},{7,6},{8,9},{9,8},{10,11... | collective-permute-start | bytes 2359304 | tf_op jit(solution)/shard_map/ppermute | solution.py:560
  27.5 23.0 %collective-permute-start.10 = (f32[448,128]{1,0:T(8,128)}, f32[448,128]{1,0:T(8,128)S(1)}, u32[]{:S(2)}, u32[]{:S(2)}) collective-permute-start(f32[448,128]{1,0:T(8,128)} %copy-done.5), channel_id=1, source_target_pairs={{0,16},{16,0},{1,17},{17,1},{2,18},{18,2},{3,19},{19,3},{4,20},{20... | collective-permute-start | bytes 688136 | tf_op jit(solution)/shard_map/ppermute | solution.py:652
  31.2 16.3 %collective-permute-start.8 = (f32[12,8,256]{2,1,0:T(8,128)S(1)}, f32[12,8,256]{2,1,0:T(8,128)S(1)}, u32[]{:S(2)}, u32[]{:S(2)}) collective-permute-start(f32[12,8,256]{2,1,0:T(8,128)S(1)} %get-tuple-element.74), channel_id=1, source_target_pairs={{0,12},{1,13},{2,14},{3,15},{4,8},{5,9},{6,10},{7,11},{8,4},{9,5},... | collective-permute-start | bytes 294920 | tf_op jit(solution)/shard_map/ppermute | solution.py:554
  36.5 1.6 %collective-permute-start.4 = (f32[12,8,256]{2,1,0:T(8,128)S(1)}, f32[12,8,256]{2,1,0:T(8,128)S(1)}, u32[]{:S(2)}, u32[]{:S(2)}) collective-permute-start(f32[12,8,256]{2,1,0:T(8,128)S(1)} %get-tuple-element.74), channel_id=1, source_target_pairs={{0,1},{1,0},{2,3},{3,2},{4,5},{5,4},{6,7},{7,6},{8,9},{9,8},{10,11... | collective-permute-start | bytes 294920 | tf_op jit(solution)/shard_map/ppermute | solution.py:560
  38.1 9.7 %collective-permute-start.7 = (f32[24,8,256]{2,1,0:T(8,128)S(1)}, f32[24,8,256]{2,1,0:T(8,128)S(1)}, u32[]{:S(2)}, u32[]{:S(2)}) collective-permute-start(f32[24,8,256]{2,1,0:T(8,128)S(1)} %constant_dynamic-update-slice_fusion.chip_ref), channel_id=1, source_target_pairs={{0,10},{1,15},{2,8},{3,13},{4,14},{5,11},{6,12},{7,9},{8,2},{9,7},... | collective-permute-start | bytes 589832 | tf_op jit(solution)/shard_map/ppermute | solution.py:553
  39.1 10.0 %collective-permute-start.6 = (f32[24,8,256]{2,1,0:T(8,128)S(1)}, f32[24,8,256]{2,1,0:T(8,128)S(1)}, u32[]{:S(2)}, u32[]{:S(2)}) collective-permute-start(f32[24,8,256]{2,1,0:T(8,128)S(1)} %constant_dynamic-update-slice_fusion.chip_ref), channel_id=1, source_target_pairs={{0,4},{1,9},{2,6},{3,11},{4,0},{5,13},{6,2},{7,15},{8,12},{9,1},{1... | collective-permute-start | bytes 589832 | tf_op jit(solution)/shard_map/ppermute | solution.py:552
  41.8 8.0 %collective-permute-start.5 = (f32[24,8,256]{2,1,0:T(8,128)S(1)}, f32[24,8,256]{2,1,0:T(8,128)S(1)}, u32[]{:S(2)}, u32[]{:S(2)}) collective-permute-start(f32[24,8,256]{2,1,0:T(8,128)S(1)} %constant_dynamic-update-slice_fusion.chip_ref), channel_id=1, source_target_pairs={{0,2},{1,7},{2,0},{3,5},{4,6},{5,3},{6,4},{7,1},{8,10},{9,15},{10,... | collective-permute-start | bytes 589832 | tf_op jit(solution)/shard_map/ppermute | solution.py:551
  43.6 8.3 %copy-start = (f32[8192]{0:T(1024)S(1)}, f32[8192]{0:T(1024)}, u32[]{:S(2)}) copy-start(f32[8192]{0:T(1024)} %param.13) | copy-start | bytes 98308
  43.6 8.3 %copy-start.1 = (f32[8192]{0:T(1024)S(1)}, f32[8192]{0:T(1024)}, u32[]{:S(2)}) copy-start(f32[8192]{0:T(1024)} %param.14) | copy-start | bytes 98308
  43.6 8.3 %copy-start.7 = (f32[8,1,7,8192]{3,1,2,0:T(1,128)S(1)}, f32[8,1,7,8192]{3,1,2,0:T(1,128)}, u32[]{:S(2)}) copy-start(f32[8,1,7,8192]{3,1,2,0:T(1,128)} %param.10) | copy-start | bytes 5505028
  50.5 1.4 %collective-permute-start.9 = (f32[12,8,256]{2,1,0:T(8,128)S(1)}, f32[12,8,256]{2,1,0:T(8,128)S(1)}, u32[]{:S(2)}, u32[]{:S(2)}) collective-permute-start(f32[12,8,256]{2,1,0:T(8,128)S(1)} %select.1), channel_id=1, source_target_pairs={{0,1},{1,0},{2,3},{3,2},{4,5},{5,4},{6,7},{7,6},{8,9},{9,8},{10,11... | collective-permute-start | bytes 294920 | tf_op jit(solution)/shard_map/ppermute | solution.py:560
  71.8 0.5 copy-start.8

commit v5 on v4

--- a/solution.py
+++ b/solution.py
@@ -29,7 +29,7 @@
 SMEM = pltpu.SMEM
 GUARD = 0.02
 CHUNK = 4
-FLUX_INNER = 10**7
+FLUX_INNER = 10**6
 INNER_MIB = 46
 OUTER_MIB = 16
 MIX = 10**6
@@ -169,7 +169,7 @@
                 table_ref[number * 4 + 2] = row
                 table_ref[number * 4 + 3] = code
                 here = jnp.where(
-                    part == 4, True, jnp.where(part == 3, same, pick_of(CORE_OF, offset) == core)
+                    part == 4, True, jnp.where(part == 3, jnp.logical_not(same), pick_of(CORE_OF, offset) == core)
                 )
                 later_ref[number * 5] = part
                 later_ref[number * 5 + 1] = among
@@ -177,6 +177,8 @@
                 later_ref[number * 5 + 3] = jnp.where(here, 1, 0)
                 later_ref[number * 5 + 4] = code
             else:
+                table_ref[4 * FACES + number * 2] = device // 2
+                table_ref[4 * FACES + number * 2 + 1] = row
                 later_ref[5 * FACES + number * 3] = part
                 later_ref[5 * FACES + number * 3 + 1] = among
                 later_ref[5 * FACES + number * 3 + 2] = row
@@ -196,6 +198,12 @@
     for number in range(FACES):
         base = 5 * FACES + number * 3
         wanted_ref[number] = choose(parts, later_ref[base], later_ref[base + 1], later_ref[base + 2])
+
+
+def select_near_kernel(table_ref, own_ref, token_ref, gram_ref, wanted_ref):
+    for number in range(FACES):
+        base = 4 * FACES + number * 2
+        wanted_ref[number] = own_ref[table_ref[base], table_ref[base + 1]]
 
 
 def turn_face(source, code, halos, number):
@@ -221,7 +229,7 @@
         chip = table_ref[number * 4]
         here = table_ref[number * 4 + 1] == 1
         row = table_ref[number * 4 + 2]
-        source = jnp.where(here, own_ref[chip, row], swapped_ref[chip, row])
+        source = jnp.where(here, own_ref[chip, row], swapped_ref[number])
         turn_face(source, table_ref[number * 4 + 3], halos, number)
 
 
@@ -360,7 +368,7 @@
 
 
 def flux_kernel(
-    table_ref, own_ref, swapped_ref, part_ref, across_z_ref, across_y_ref, across_x_ref, token_ref, mixed_ref,
+    table_ref, own_ref, swapped_ref, part_ref, across_z_ref, across_y_ref, across_x_ref, mixed_ref,
     first_ref, faces_ref, halos
 ):
     fetch_halos(table_ref, own_ref, swapped_ref, halos)
@@ -532,10 +540,6 @@
     return lax.all_to_all(sent, CHIPS, 0, 0)
 
 
-def after(value, others):
-    return lax.optimization_barrier((value, others))
-
-
 def split_pairs(first, second):
     pairs = []
     for chip in range(CHIP_COUNT):
@@ -551,7 +555,7 @@
         lax.ppermute(chip, space, split_pairs(1, 3)),
         lax.ppermute(chip, space, split_pairs(2, 4)),
         lax.ppermute(chip, space, split_pairs(5, 7)),
-        lax.ppermute(faces, space, split_pairs(6, 6)),
+        lax.ppermute(chip[FACES:], space, split_pairs(6, 6)),
         chip,
     )
 
@@ -613,7 +617,7 @@
         in_specs=[whole(SMEM)] * 3,
         out_specs=[whole(SMEM), whole(SMEM)],
         out_shape=[
-            jax.ShapeDtypeStruct((4 * FACES,), jnp.int32),
+            jax.ShapeDtypeStruct((6 * FACES,), jnp.int32),
             jax.ShapeDtypeStruct((8 * FACES,), jnp.int32),
         ],
         scratch_shapes=[SMEM((BLOCKS,), jnp.int32)],
@@ -637,18 +641,26 @@
         name="gram",
     )(flat)
     kept, given, mixed = mix([dense] + [lax.ppermute(dense, "z", swap(4, k)) for k in (1, 2, 3)])
-    own, (token, table, mixed, gram) = after(own, (token, table, mixed, gram))
-    swapped = swap_cores(own)
+    wanted = pl.pallas_call(
+        select_near_kernel,
+        in_specs=[whole(SMEM), whole(), whole(pl.ANY), whole(pl.ANY)],
+        out_specs=whole(),
+        out_shape=f32(FACES, 8, SQUARE),
+        compiler_params=params(4),
+        cost_estimate=cost(10**5, 10**6),
+        name="select_near",
+    )(table, own, token, gram)
+    swapped = swap_cores(wanted)
     first, faces = pl.pallas_call(
         flux_kernel,
-        in_specs=[whole(SMEM)] + [whole()] * 6 + [whole(pl.ANY)] * 2,
+        in_specs=[whole(SMEM)] + [whole()] * 6 + [whole(pl.ANY)],
         out_specs=[whole(), whole()],
         out_shape=[f32(8, CELLS), f32(FACES, 8, SQUARE)],
         scratch_shapes=[FACES_VMEM],
         compiler_params=params(OUTER_MIB),
         cost_estimate=cost(FLUX_OUTER, 4 * 2**20),
         name="flux_outer",
-    )(table, own, swapped, *pieces, token, mixed)
+    )(table, own, swapped, *pieces, mixed)
     returned = lax.ppermute(given, "xl", swap(2, 1))
     *pieces, token = inner_section(first, recon, "recon_inner", RECON_INNER)
     parts = second_exchange(faces)

time: 72.5 us -> 71.6 us (0.988)
  waiting for transfers between devices: 8.41 us -> 4.17 us
  Pallas kernels: 19.5 us -> 21.3 us
  blocking collectives: 15.9 us -> 17 us
  starting transfers between devices: 25.6 us -> 26.7 us
    ppermute x1, starting transfers between devices: 0.96 us -> 5.68 us  [second_exchange(): lax.ppermute(chip, space, split_pairs(5, 7))]
    ppermute x1, starting transfers between devices: 2.69 us -> 0.01 us  [second_exchange(): lax.ppermute(chip, space, split_pairs(2, 4))]
    ppermute x3, waiting for transfers between devices: 2.23 us -> 0.01 us  [local(): lax.ppermute(dense, 'z', swap(4, k))]
    ppermute x3, waiting for transfers between devices: 3.81 us -> 1.88 us  [swap_cores(): return lax.ppermute(own, 'core', swap(2, 1))]
    ppermute x3, starting transfers between devices: 2.56 us -> 4.24 us  [swap_cores(): return lax.ppermute(own, 'core', swap(2, 1))]
    ppermute x1, starting transfers between devices: 1.79 us -> 0.37 us  [second_exchange(): lax.ppermute(chip, space, split_pairs(1, 3))]
    ppermute x1, starting transfers between devices: 5.37 us -> 4.07 us  [second_exchange(): lax.ppermute(chip[FACES:], space, split_pairs(6, 6))]
    ppermute x1, waiting for transfers between devices: 1.22 us -> 0.01 us  [second_exchange(): lax.ppermute(chip, space, split_pairs(2, 4))]
  transfers between devices with their start and end apart: 12 -> 12, of which waited for: 8 -> 4; matrix products, arithmetic and copies ran while one was open for 0% -> 0% of each run, Pallas kernels for 19% -> 22%
where the time goes in v5:
time: 71.6 us; the launch traced here: 71.3 us
  starting transfers between devices  26.7 us (37%)
  Pallas kernels  21.3 us (30%)
  blocking collectives  17 us (24%)
  waiting for transfers between devices  4.17 us (6%)
  loops' own time  0.83 us (1%)
  between operations  0.8 us (1%)
    all_to_all x1, blocking collectives, local(): received = lax.all_to_all(sums, ALL, 0, 0)  17 us
    pallas_call x2, Pallas kernels, inner_section(): pl.pallas_call(inner_kernel, in_specs=[whole(), whole(pltpu.HBM)], out_sp...  7.75 us
    all_to_all x1, starting transfers between devices, exchange(): return lax.all_to_all(sent, CHIPS, 0, 0)  7.49 us
    ppermute x1, starting transfers between devices, second_exchange(): lax.ppermute(chip, space, split_pairs(5, 7))  5.68 us
    ppermute x3, starting transfers between devices, local(): lax.ppermute(dense, 'z', swap(4, k))  4.42 us
    ppermute x3, starting transfers between devices, swap_cores(): return lax.ppermute(own, 'core', swap(2, 1))  4.24 us
    ppermute x1, starting transfers between devices, second_exchange(): lax.ppermute(chip[FACES:], space, split_pairs(6, 6))  4.07 us
    pallas_call x1, Pallas kernels, local(): pl.pallas_call(first_faces_kernel, in_specs=[whole(pl.ANY)], out_specs=[w...  2.48 us
  transfers between devices with their start and end apart: 12, of which 4 were waited for; matrix products, arithmetic and copies ran while one was open for 0% of the time, Pallas kernels for 22%

profile of v5, /device:TPU:1, one launch (start us, length us, event | category | flops | bytes accessed | tf_op | source)
XLA Modules:
  0.0 71.3 jit_solution(12504070365466470953)
XLA Ops:
  0.7 2.5 %first_faces.1 = (f32[8,12,8,256]{3,2,1,0:T(8,128)}, f32[8,8192]{1,0:T(8,128)S(1)}, f32[448,128]{1,0:T(8,128)S(1)}) custom-call(f32[3584,128]{1,0:T(8,128)} %bitcast.30), custom_call_target="tpu_custom_call" | custom-call | flops 1000000 | bytes 2097152 | tf_op jit(solution)/shard_map/first_faces/pallas_call | solution.py:604
  3.1 7.5 %all-to-all-start = ((f32[8,12,8,256]{3,2,1,0:T(8,128)}), f32[8,12,8,256]{3,2,1,0:T(8,128)S(1)}, u32[]{:S(2)}, u32[]{:S(2)}) async-start(f32[8,12,8,256]{3,2,1,0:T(8,128)} %get-tuple-element.56), calls=%async_computation | async-start | bytes 1572864 | tf_op jit(solution)/shard_map/all_to_all | solution.py:540
  10.6 3.8 %collective-permute-start.3 = (f32[448,128]{1,0:T(8,128)S(1)}, f32[448,128]{1,0:T(8,128)}, u32[]{:S(2)}, u32[]{:S(2)}) collective-permute-start(f32[448,128]{1,0:T(8,128)S(1)} %get-tuple-element.63.own_ref), channel_id=1, source_target_pairs={{0,96},{32,64},{64,32},{96,0},{1,97},{33,65},{65,33},{97,1},{2,98}... | collective-permute-start | bytes 688136 | tf_op jit(solution)/shard_map/ppermute | solution.py:643
  14.4 0.0 collective-permute-start.2
  14.4 0.7 collective-permute-start.1
  15.1 2.3 %tables.1 = (s32[72]{0:T(128)S(1)}, s32[96]{0:T(128)S(1)}) custom-call(s32[32]{0:T(128)S(1)} %copy-done.4, s32[6,32]{1,0:T(8,128)S(1)} %bitcast.28, s32[6,32]{1,0:T(8,128)S(1)} %bitcast.29), custom_call_target="tpu_custom_call" | custom-call | flops 100000 | bytes 100000 | tf_op jit(solution)/shard_map/tables/pallas_call | solution.py:615
  17.3 0.0 copy-start.5
  17.3 3.9 %flux_inner.1 = (f32[8,8192]{1,0:T(8,128)S(1)}, bf16[7,8,8192]{2,1,0:T(8,128)(2,1)S(1)}, bf16[7,8,8192]{2,1,0:T(8,128)(2,1)S(1)}, bf16[4,7,8,256]{3,2,1,0:T(8,128)(2,1)S(1)}, f32[8,128]{1,0:T(8,128)S(1)}) custom-call(f32[8,8192]{1,0:T(8,128)S(1)} %get-tuple-element.57.field_ref, bf16[1,7,7,7,8192]{4,3,2,1,0:T(8,128)(2,1)} %coeff_ref.2), custom_call_target="tpu_custom_call" | custom-call | flops 1000000 | bytes 8388608 | tf_op jit(solution)/shard_map/flux_inner/pallas_call | solution.py:573
  21.2 1.4 %gram.1.gram_ref = f32[8,128]{1,0:T(8,128)S(1)} custom-call(f32[3584,128]{1,0:T(8,128)S(1)} %bitcast.31), custom_call_target="tpu_custom_call" | custom-call | flops 4128768 | bytes 2097152 | tf_op jit(solution)/shard_map/gram/pallas_call | solution.py:629
  22.7 0.6 select_near.1
  23.3 2.4 %collective-permute-start = (f32[12,8,256]{2,1,0:T(8,128)S(1)}, f32[12,8,256]{2,1,0:T(8,128)S(1)}, u32[]{:S(2)}, u32[]{:S(2)}) collective-permute-start(f32[12,8,256]{2,1,0:T(8,128)S(1)} %select_near.1), channel_id=1, source_target_pairs={{0,1},{1,0},{2,3},{3,2},{4,5},{5,4},{6,7},{7,6},{8,9},{9,8},{10,11... | collective-permute-start | bytes 294920 | tf_op jit(solution)/shard_map/ppermute | solution.py:564
  25.6 0.0 collective-permute-done.3.three_ref
  25.6 1.3 %mix.1 = (f32[448,128]{1,0:T(8,128)S(1)}, f32[448,128]{1,0:T(8,128)S(1)}, f32[8,128]{1,0:T(8,128)S(1)}) custom-call(f32[448,128]{1,0:T(8,128)S(1)} %get-tuple-element.63.own_ref, f32[448,128]{1,0:T(8,128)} %collective-permute-done.1.one_ref, f32[448,128]{1,0:T(8,128)} %collective-permute-done.2.two_ref, f32[448,128]{1,0:T(8,128)} %collective-permute-done.3.three_ref), custom_call_target="tpu_custom_call" | custom-call | flops 1000000 | bytes 1376256 | tf_op jit(solution)/shard_map/mix/pallas_call | solution.py:591
  26.9 0.4 collective-permute-start.10
  27.3 1.7 %flux_outer.1 = (f32[8,8192]{1,0:T(8,128)S(1)}, f32[12,8,256]{2,1,0:T(8,128)S(1)}) custom-call(s32[72]{0:T(128)S(1)} %get-tuple-element.55.table_ref, f32[8,12,8,256]{3,2,1,0:T(8,128)S(1)} %all-to-all-done.own_ref, f32[12,8,256]{2,1,0:T(8,128)S(1)} %collective-permute-done.swapped_ref, f32[8,8192]{1,0:T(8,128)S(1)} %get-tuple-element.59.part_ref, ...), custom_call_target="tpu_custom_call" | custom-call | flops 1000000 | bytes 4194304 | tf_op jit(solution)/shard_map/flux_outer/pallas_call | solution.py:654
  29.1 1.4 %collective-permute-start.4 = (f32[12,8,256]{2,1,0:T(8,128)S(1)}, f32[12,8,256]{2,1,0:T(8,128)S(1)}, u32[]{:S(2)}, u32[]{:S(2)}) collective-permute-start(f32[12,8,256]{2,1,0:T(8,128)S(1)} %get-tuple-element.65), channel_id=1, source_target_pairs={{0,1},{1,0},{2,3},{3,2},{4,5},{5,4},{6,7},{7,6},{8,9},{9,8},{10,11... | collective-permute-start | bytes 294920 | tf_op jit(solution)/shard_map/ppermute | solution.py:564
  30.5 0.9 %collective-permute-done.4 = f32[12,8,256]{2,1,0:T(8,128)S(1)} collective-permute-done((f32[12,8,256]{2,1,0:T(8,128)S(1)}, f32[12,8,256]{2,1,0:T(8,128)S(1)}, u32[]{:S(2)}, u32[]{:S(2)}) %collective-permute-start.4) | collective-permute-done | bytes 98336 | tf_op jit(solution)/shard_map/ppermute | solution.py:564
  31.4 5.7 %collective-permute-start.7 = (f32[24,8,256]{2,1,0:T(8,128)S(1)}, f32[24,8,256]{2,1,0:T(8,128)S(1)}, u32[]{:S(2)}, u32[]{:S(2)}) collective-permute-start(f32[24,8,256]{2,1,0:T(8,128)S(1)} %constant_dynamic-update-slice_fusion.chip_ref), channel_id=1, source_target_pairs={{0,10},{1,15},{2,8},{3,13},{4,14},{5,11},{6,12},{7,9},{8,2},{9,7},... | collective-permute-start | bytes 589832 | tf_op jit(solution)/shard_map/ppermute | solution.py:557
  37.1 0.4 collective-permute-start.5
  37.5 4.1 %collective-permute-start.8 = (f32[12,8,256]{2,1,0:T(8,128)S(1)}, f32[12,8,256]{2,1,0:T(8,128)S(1)}, u32[]{:S(2)}, u32[]{:S(2)}) collective-permute-start(f32[12,8,256]{2,1,0:T(8,128)S(1)} %collective-permute-done.4), channel_id=1, source_target_pairs={{0,12},{1,13},{2,14},{3,15},{4,8},{5,9},{6,10},{7,11},{8,4},{9,5},... | collective-permute-start | bytes 294920 | tf_op jit(solution)/shard_map/ppermute | solution.py:558
  41.5 3.9 %recon_inner.1 = (f32[8,8192]{1,0:T(8,128)S(1)}, bf16[7,8,8192]{2,1,0:T(8,128)(2,1)S(1)}, bf16[7,8,8192]{2,1,0:T(8,128)(2,1)S(1)}, bf16[4,7,8,256]{3,2,1,0:T(8,128)(2,1)S(1)}, f32[8,128]{1,0:T(8,128)S(1)}) custom-call(f32[8,8192]{1,0:T(8,128)S(1)} %get-tuple-element.66.field_ref, bf16[1,7,7,7,8192]{4,3,2,1,0:T(8,128)(2,1)} %coeff_ref.3), custom_call_target="tpu_custom_call" | custom-call | flops 20000000000 | bytes 8388608 | tf_op jit(solution)/shard_map/recon_inner/pallas_call | solution.py:573
  45.4 0.7 %collective-permute-done.8.four_ref = f32[12,8,256]{2,1,0:T(8,128)S(1)} collective-permute-done((f32[12,8,256]{2,1,0:T(8,128)S(1)}, f32[12,8,256]{2,1,0:T(8,128)S(1)}, u32[]{:S(2)}, u32[]{:S(2)}) %collective-permute-start.8) | collective-permute-done | bytes 98336 | tf_op jit(solution)/shard_map/ppermute | solution.py:558
  46.2 1.6 %collective-permute-done.5.one_ref = f32[24,8,256]{2,1,0:T(8,128)S(1)} collective-permute-done((f32[24,8,256]{2,1,0:T(8,128)S(1)}, f32[24,8,256]{2,1,0:T(8,128)S(1)}, u32[]{:S(2)}, u32[]{:S(2)}) %collective-permute-start.5) | collective-permute-done | bytes 196640 | tf_op jit(solution)/shard_map/ppermute | solution.py:555
  47.7 0.6 select.1
  48.3 0.5 collective-permute-start.9
  48.8 0.9 %collective-permute-done.9.swapped_ref = f32[12,8,256]{2,1,0:T(8,128)S(1)} collective-permute-done((f32[12,8,256]{2,1,0:T(8,128)S(1)}, f32[12,8,256]{2,1,0:T(8,128)S(1)}, u32[]{:S(2)}, u32[]{:S(2)}) %collective-permute-start.9) | collective-permute-done | bytes 98336 | tf_op jit(solution)/shard_map/ppermute | solution.py:564
  49.8 1.9 %image.1 = (f32[448,128]{1,0:T(8,128)S(1)}, f32[128,128]{1,0:T(8,128)S(1)}, f32[3584,128]{1,0:T(8,128)S(1)}) custom-call(s32[96]{0:T(128)S(1)} %get-tuple-element.54.later_ref, f32[24,8,256]{2,1,0:T(8,128)S(1)} %collective-permute-done.5.one_ref, f32[24,8,256]{2,1,0:T(8,128)S(1)} %collective-permute-done.6.two_ref, ...), custom_call_target="tpu_custom_call" | custom-call | flops 1000000 | bytes 6291456 | tf_op jit(solution)/shard_map/image/pallas_call | solution.py:677
  51.7 17.0 %all_to_all.16 = f32[128,1,128]{2,1,0:T(1,128)S(1)} all-to-all(f32[128,1,128]{2,1,0:T(1,128)S(1)} %bitcast.25), channel_id=1, replica_groups=mesh['z'=4,'xl'=2,'xh'=2,'y'=4,'core'=2] {'z','xl','xh','y','core'}, dimensions={0} | all-to-all | bytes 131072 | tf_op jit(solution)/shard_map/all_to_all | solution.py:690
  68.7 1.3 %finish.1 = (f32[448,128]{1,0:T(8,128)}, f32[1,9]{1,0:T(1,128)S(1)}, s32[1]{0:T(128)}) custom-call(f32[128,128]{1,0:T(8,128)S(1)} %bitcast.24, f32[448,128]{1,0:T(8,128)S(1)} %get-tuple-element.103.image_ref, f32[3584,128]{1,0:T(8,128)S(1)} %get-tuple-element.76.basis_ref), custom_call_target="tpu_custom_call" | custom-call | flops 1000000 | bytes 3145728 | tf_op jit(solution)/shard_map/finish/pallas_call | solution.py:691
  70.0 0.8 %while.11 = (f32[448,128]{1,0:T(8,128)}, f32[1,9]{1,0:T(1,128)S(1)}, s32[]{:T(128)}, f32[8,1,7,8192]{3,1,2,0:T(1,128)S(1)}, f32[448,128]{1,0:T(8,128)S(1)}) while((f32[448,128]{1,0:T(8,128)}, f32[1,9]{1,0:T(1,128)S(1)}, s32[]{:T(128)}, f32[8,1,7,8192]{3,1,2,0:T(1,128)S(1)}, f32[448,128]{1,0:T(8,128)S(1)}) %tuple.21), condition=%region_3.0_spmd, body=%region_0.0_spmd | while | flops 5734412 | bytes 3211541 | solution.py:711
  70.8 0.0 copy-start.7
  70.8 0.5 copy-done.7
  (23 shorter events, 0.1 us)
Async XLA Ops:
  0.6 14.4 %copy-start.3 = (s32[32,6]{0,1:T(8,128)S(1)}, s32[32,6]{0,1:T(8,128)}, u32[]{:S(2)}) copy-start(s32[32,6]{0,1:T(8,128)} %param.17) | copy-start | bytes 2308
  0.6 14.4 %copy-start.2 = (s32[32,6]{0,1:T(8,128)S(1)}, s32[32,6]{0,1:T(8,128)}, u32[]{:S(2)}) copy-start(s32[32,6]{0,1:T(8,128)} %param.16) | copy-start | bytes 2308
  0.7 14.4 %copy-start.4 = (s32[32]{0:T(128)S(1)}, s32[32]{0:T(128)}, u32[]{:S(2)}) copy-start(s32[32]{0:T(128)} %ids_ref.1) | copy-start | bytes 388
  3.1 19.5 %all-to-all-start = ((f32[8,12,8,256]{3,2,1,0:T(8,128)}), f32[8,12,8,256]{3,2,1,0:T(8,128)S(1)}, u32[]{:S(2)}, u32[]{:S(2)}) async-start(f32[8,12,8,256]{3,2,1,0:T(8,128)} %get-tuple-element.56), calls=%async_computation | async-start | bytes 1572864 | tf_op jit(solution)/shard_map/all_to_all | solution.py:540
  10.6 15.0 %collective-permute-start.3 = (f32[448,128]{1,0:T(8,128)S(1)}, f32[448,128]{1,0:T(8,128)}, u32[]{:S(2)}, u32[]{:S(2)}) collective-permute-start(f32[448,128]{1,0:T(8,128)S(1)} %get-tuple-element.63.own_ref), channel_id=1, source_target_pairs={{0,96},{32,64},{64,32},{96,0},{1,97},{33,65},{65,33},{97,1},{2,98}... | collective-permute-start | bytes 688136 | tf_op jit(solution)/shard_map/ppermute | solution.py:643
  14.4 11.2 %collective-permute-start.2 = (f32[448,128]{1,0:T(8,128)S(1)}, f32[448,128]{1,0:T(8,128)}, u32[]{:S(2)}, u32[]{:S(2)}) collective-permute-start(f32[448,128]{1,0:T(8,128)S(1)} %get-tuple-element.63.own_ref), channel_id=1, source_target_pairs={{0,64},{32,96},{64,0},{96,32},{1,65},{33,97},{65,1},{97,33},{2,66}... | collective-permute-start | bytes 688136 | tf_op jit(solution)/shard_map/ppermute | solution.py:643
  14.4 11.2 %collective-permute-start.1 = (f32[448,128]{1,0:T(8,128)S(1)}, f32[448,128]{1,0:T(8,128)}, u32[]{:S(2)}, u32[]{:S(2)}) collective-permute-start(f32[448,128]{1,0:T(8,128)S(1)} %get-tuple-element.63.own_ref), channel_id=1, source_target_pairs={{0,32},{32,0},{64,96},{96,64},{1,33},{33,1},{65,97},{97,65},{2,34}... | collective-permute-start | bytes 688136 | tf_op jit(solution)/shard_map/ppermute | solution.py:643
  17.3 3.9 %copy-start.5 = (f32[8,1,7,8192]{3,1,2,0:T(1,128)S(1)}, f32[8,1,7,8192]{3,1,2,0:T(1,128)}, u32[]{:S(2)}) copy-start(f32[8,1,7,8192]{3,1,2,0:T(1,128)} %param.10) | copy-start | bytes 5505028
  23.3 4.1 %collective-permute-start = (f32[12,8,256]{2,1,0:T(8,128)S(1)}, f32[12,8,256]{2,1,0:T(8,128)S(1)}, u32[]{:S(2)}, u32[]{:S(2)}) collective-permute-start(f32[12,8,256]{2,1,0:T(8,128)S(1)} %select_near.1), channel_id=1, source_target_pairs={{0,1},{1,0},{2,3},{3,2},{4,5},{5,4},{6,7},{7,6},{8,9},{9,8},{10,11... | collective-permute-start | bytes 294920 | tf_op jit(solution)/shard_map/ppermute | solution.py:564
  26.9 21.9 %collective-permute-start.10 = (f32[448,128]{1,0:T(8,128)S(1)}, f32[448,128]{1,0:T(8,128)S(1)}, u32[]{:S(2)}, u32[]{:S(2)}) collective-permute-start(f32[448,128]{1,0:T(8,128)S(1)} %get-tuple-element.73), channel_id=1, source_target_pairs={{0,16},{16,0},{1,17},{17,1},{2,18},{18,2},{3,19},{19,3},{4,20},{20... | collective-permute-start | bytes 688136 | tf_op jit(solution)/shard_map/ppermute | solution.py:664
  29.1 2.3 %collective-permute-start.4 = (f32[12,8,256]{2,1,0:T(8,128)S(1)}, f32[12,8,256]{2,1,0:T(8,128)S(1)}, u32[]{:S(2)}, u32[]{:S(2)}) collective-permute-start(f32[12,8,256]{2,1,0:T(8,128)S(1)} %get-tuple-element.65), channel_id=1, source_target_pairs={{0,1},{1,0},{2,3},{3,2},{4,5},{5,4},{6,7},{7,6},{8,9},{9,8},{10,11... | collective-permute-start | bytes 294920 | tf_op jit(solution)/shard_map/ppermute | solution.py:564
  31.4 14.7 %collective-permute-start.7 = (f32[24,8,256]{2,1,0:T(8,128)S(1)}, f32[24,8,256]{2,1,0:T(8,128)S(1)}, u32[]{:S(2)}, u32[]{:S(2)}) collective-permute-start(f32[24,8,256]{2,1,0:T(8,128)S(1)} %constant_dynamic-update-slice_fusion.chip_ref), channel_id=1, source_target_pairs={{0,10},{1,15},{2,8},{3,13},{4,14},{5,11},{6,12},{7,9},{8,2},{9,7},... | collective-permute-start | bytes 589832 | tf_op jit(solution)/shard_map/ppermute | solution.py:557
  37.1 9.1 %collective-permute-start.6 = (f32[24,8,256]{2,1,0:T(8,128)S(1)}, f32[24,8,256]{2,1,0:T(8,128)S(1)}, u32[]{:S(2)}, u32[]{:S(2)}) collective-permute-start(f32[24,8,256]{2,1,0:T(8,128)S(1)} %constant_dynamic-update-slice_fusion.chip_ref), channel_id=1, source_target_pairs={{0,4},{1,9},{2,6},{3,11},{4,0},{5,13},{6,2},{7,15},{8,12},{9,1},{1... | collective-permute-start | bytes 589832 | tf_op jit(solution)/shard_map/ppermute | solution.py:556
  37.1 10.6 %collective-permute-start.5 = (f32[24,8,256]{2,1,0:T(8,128)S(1)}, f32[24,8,256]{2,1,0:T(8,128)S(1)}, u32[]{:S(2)}, u32[]{:S(2)}) collective-permute-start(f32[24,8,256]{2,1,0:T(8,128)S(1)} %constant_dynamic-update-slice_fusion.chip_ref), channel_id=1, source_target_pairs={{0,2},{1,7},{2,0},{3,5},{4,6},{5,3},{6,4},{7,1},{8,10},{9,15},{10,... | collective-permute-start | bytes 589832 | tf_op jit(solution)/shard_map/ppermute | solution.py:555
  37.5 8.7 %collective-permute-start.8 = (f32[12,8,256]{2,1,0:T(8,128)S(1)}, f32[12,8,256]{2,1,0:T(8,128)S(1)}, u32[]{:S(2)}, u32[]{:S(2)}) collective-permute-start(f32[12,8,256]{2,1,0:T(8,128)S(1)} %collective-permute-done.4), channel_id=1, source_target_pairs={{0,12},{1,13},{2,14},{3,15},{4,8},{5,9},{6,10},{7,11},{8,4},{9,5},... | collective-permute-start | bytes 294920 | tf_op jit(solution)/shard_map/ppermute | solution.py:558
  41.5 8.2 %copy-start = (f32[8192]{0:T(1024)S(1)}, f32[8192]{0:T(1024)}, u32[]{:S(2)}) copy-start(f32[8192]{0:T(1024)} %param.13) | copy-start | bytes 98308
  41.5 8.2 %copy-start.1 = (f32[8192]{0:T(1024)S(1)}, f32[8192]{0:T(1024)}, u32[]{:S(2)}) copy-start(f32[8192]{0:T(1024)} %param.14) | copy-start | bytes 98308
  41.5 8.2 %copy-start.6 = (f32[8,1,7,8192]{3,1,2,0:T(1,128)S(1)}, f32[8,1,7,8192]{3,1,2,0:T(1,128)}, u32[]{:S(2)}) copy-start(f32[8,1,7,8192]{3,1,2,0:T(1,128)} %param.10) | copy-start | bytes 5505028
  48.3 1.4 %collective-permute-start.9 = (f32[12,8,256]{2,1,0:T(8,128)S(1)}, f32[12,8,256]{2,1,0:T(8,128)S(1)}, u32[]{:S(2)}, u32[]{:S(2)}) collective-permute-start(f32[12,8,256]{2,1,0:T(8,128)S(1)} %select.1), channel_id=1, source_target_pairs={{0,1},{1,0},{2,3},{3,2},{4,5},{5,4},{6,7},{7,6},{8,9},{9,8},{10,11... | collective-permute-start | bytes 294920 | tf_op jit(solution)/shard_map/ppermute | solution.py:564
  70.8 0.5 copy-start.7

commit v6 on v5

--- a/solution.py
+++ b/solution.py
@@ -30,11 +30,12 @@
 GUARD = 0.02
 CHUNK = 4
 FLUX_INNER = 10**6
-INNER_MIB = 46
+INNER_MIB = 50
 OUTER_MIB = 16
-MIX = 10**6
+MIX = 5 * 10**9
+GRAM = 10**9
 FLUX_OUTER = 10**6
-RECON_INNER = 2 * 10**10
+RECON_INNER = 10**6
 
 
 def mixing_weights():
@@ -117,19 +118,15 @@
     fetch.start()
     field[ROWS:] = jnp.zeros((GROUPS, LANES), jnp.float32)
     fetch.wait()
-    copies = []
+    copies = [pltpu.make_async_copy(field.at[pl.ds(0, ROWS)], dense_ref, arrived.at[PER, 0])]
+    copies[0].start()
     for block in range(PER):
         for group in range(block * 32, block * 32 + 32):
             padded_ref[:, group * LANES : (group + 1) * LANES] = field[pl.ds(group, 8, stride=GROUPS), :]
         collect_block(padded_ref, faces, block)
         copies += send_block(faces, sent_ref, arrived, block)
-    dense_ref[...] = field[:ROWS]
     for copy in copies:
         copy.wait()
-
-
-PART_OF = (4, 0, 1, 0, 1, 2, 3, 2)
-CORE_OF = (0, 0, 0, 1, 1, 0, 0, 1)
 
 
 def tables_kernel(ids_ref, neighbour_ref, orient_ref, table_ref, later_ref, position):
@@ -141,12 +138,6 @@
         return carry
 
     lax.fori_loop(0, BLOCKS, place, 0)
-
-    def pick_of(values, index):
-        result = jnp.int32(values[0])
-        for k in range(1, len(values)):
-            result = jnp.where(index == k, jnp.int32(values[k]), result)
-        return result
 
     for mine in (True, False):
         for number in range(FACES):
@@ -159,8 +150,8 @@
             row = (slot % PER) * 6 + target % 6
             source_core = device % 2
             offset = (device // 2) ^ chip
-            part = pick_of(PART_OF, offset)
-            among = jnp.where(source_core == core, row, row + FACES)
+            part = offset & 3
+            among = (offset >> 2) * FACES + row
             if mine:
                 code = jnp.where(partner < 0, -1, orient_ref[number % 6, owner])
                 same = source_core == core
@@ -168,39 +159,34 @@
                 table_ref[number * 4 + 1] = jnp.where(same, 1, 0)
                 table_ref[number * 4 + 2] = row
                 table_ref[number * 4 + 3] = code
-                here = jnp.where(
-                    part == 4, True, jnp.where(part == 3, jnp.logical_not(same), pick_of(CORE_OF, offset) == core)
-                )
-                later_ref[number * 5] = part
-                later_ref[number * 5 + 1] = among
-                later_ref[number * 5 + 2] = row
-                later_ref[number * 5 + 3] = jnp.where(here, 1, 0)
-                later_ref[number * 5 + 4] = code
+                later_ref[number * 4] = part
+                later_ref[number * 4 + 1] = among
+                later_ref[number * 4 + 2] = jnp.where(same, 1, 0)
+                later_ref[number * 4 + 3] = code
             else:
                 table_ref[4 * FACES + number * 2] = device // 2
                 table_ref[4 * FACES + number * 2 + 1] = row
-                later_ref[5 * FACES + number * 3] = part
-                later_ref[5 * FACES + number * 3 + 1] = among
-                later_ref[5 * FACES + number * 3 + 2] = row
-
-
-def choose(parts, part, among, row):
-    value = parts[4][among]
-    for k in range(3):
+                later_ref[4 * FACES + number * 2] = part
+                later_ref[4 * FACES + number * 2 + 1] = among
+
+
+def choose(parts, part, among):
+    value = parts[0][among]
+    for k in range(1, 4):
         value = jnp.where(part == k, parts[k][among], value)
-    return jnp.where(part == 3, parts[3][row], value)
+    return value
 
 
 def select_kernel(
-    later_ref, one_ref, two_ref, three_ref, four_ref, chip_ref, token_ref, wanted_ref
+    later_ref, pair_ref, one_ref, two_ref, three_ref, token_ref, mixed_ref, gram_ref, wanted_ref
 ):
-    parts = (one_ref, two_ref, three_ref, four_ref, chip_ref)
+    parts = (pair_ref, one_ref, two_ref, three_ref)
     for number in range(FACES):
-        base = 5 * FACES + number * 3
-        wanted_ref[number] = choose(parts, later_ref[base], later_ref[base + 1], later_ref[base + 2])
-
-
-def select_near_kernel(table_ref, own_ref, token_ref, gram_ref, wanted_ref):
+        base = 4 * FACES + number * 2
+        wanted_ref[number] = choose(parts, later_ref[base], later_ref[base + 1])
+
+
+def select_near_kernel(table_ref, own_ref, token_ref, wanted_ref):
     for number in range(FACES):
         base = 4 * FACES + number * 2
         wanted_ref[number] = own_ref[table_ref[base], table_ref[base + 1]]
@@ -235,10 +221,10 @@
 
 def fetch_later_halos(later_ref, parts, swapped_ref, halos):
     for number in range(FACES):
-        base = number * 5
-        source = choose(parts, later_ref[base], later_ref[base + 1], later_ref[base + 2])
-        source = jnp.where(later_ref[base + 3] == 1, source, swapped_ref[number])
-        turn_face(source, later_ref[base + 4], halos, number)
+        base = number * 4
+        source = choose(parts, later_ref[base], later_ref[base + 1])
+        source = jnp.where(later_ref[base + 2] == 1, source, swapped_ref[number])
+        turn_face(source, later_ref[base + 3], halos, number)
 
 
 def inner_kernel(
@@ -368,8 +354,8 @@
 
 
 def flux_kernel(
-    table_ref, own_ref, swapped_ref, part_ref, across_z_ref, across_y_ref, across_x_ref, mixed_ref,
-    first_ref, faces_ref, halos
+    table_ref, own_ref, swapped_ref, part_ref, across_z_ref, across_y_ref, across_x_ref,
+    z_one_ref, z_two_ref, z_three_ref, first_ref, faces_ref, halos
 ):
     fetch_halos(table_ref, own_ref, swapped_ref, halos)
 
@@ -381,7 +367,7 @@
         collect_block(first_ref, faces_ref, block)
 
 
-def mix_kernel(own_ref, one_ref, two_ref, three_ref, kept_ref, given_ref, token_ref):
+def mix_kernel(own_ref, one_ref, two_ref, three_ref, pair_ref, kept_ref, given_ref, token_ref):
     z = lax.axis_index("z")
     xl = lax.axis_index("xl")
     table = mixing_weights()
@@ -415,7 +401,7 @@
     return jnp.sum(jnp.where(spot, totals, 0.0), axis=0, keepdims=True)
 
 
-def gram_kernel(flat_ref, gram_ref, basis_ref, lines, arrived):
+def gram_kernel(flat_ref, pair_ref, gram_ref, basis_ref, lines, arrived):
     copy = pltpu.make_async_copy(flat_ref, basis_ref, arrived)
     copy.start()
     copy.wait()
@@ -443,14 +429,14 @@
 
 
 def image_kernel(
-    later_ref, one_ref, two_ref, three_ref, four_ref, chip_ref, swapped_ref,
+    later_ref, pair_ref, one_ref, two_ref, three_ref, swapped_ref,
     part_ref, across_z_ref, across_y_ref, across_x_ref,
     flat_ref, pseudo_ref, omega_ref, kept_ref, returned_ref, gram_ref,
     image_ref, sums_ref, basis_ref, halos, section, arrived
 ):
     copy = pltpu.make_async_copy(flat_ref, basis_ref, arrived)
     copy.start()
-    fetch_later_halos(later_ref, (one_ref, two_ref, three_ref, four_ref, chip_ref), swapped_ref, halos)
+    fetch_later_halos(later_ref, (pair_ref, one_ref, two_ref, three_ref), swapped_ref, halos)
 
     def put(k, slab):
         section[pl.ds(2 * k, 8, stride=GROUPS), :] = slab[:, :LANES]
@@ -540,24 +526,15 @@
     return lax.all_to_all(sent, CHIPS, 0, 0)
 
 
-def split_pairs(first, second):
-    pairs = []
-    for chip in range(CHIP_COUNT):
-        pairs.append((chip * 2, (chip ^ first) * 2))
-        pairs.append((chip * 2 + 1, (chip ^ second) * 2 + 1))
-    return pairs
-
-
-def second_exchange(faces):
+def chip_pairs(offset):
+    return [(rank, rank ^ (2 * offset)) for rank in range(SPACE)]
+
+
+def second_exchange(faces, token):
     space = ("xh", "y", "core")
-    chip = jnp.concatenate([faces, swap_cores(faces)])
-    return (
-        lax.ppermute(chip, space, split_pairs(1, 3)),
-        lax.ppermute(chip, space, split_pairs(2, 4)),
-        lax.ppermute(chip, space, split_pairs(5, 7)),
-        lax.ppermute(chip[FACES:], space, split_pairs(6, 6)),
-        chip,
-    )
+    other, token = lax.optimization_barrier((lax.ppermute(faces, space, chip_pairs(4)), token))
+    pair = jnp.concatenate([faces, other])
+    return token, [pair] + [lax.ppermute(pair, space, chip_pairs(offset)) for offset in (1, 2, 3)]
 
 
 def swap_cores(own):
@@ -582,21 +559,21 @@
             pltpu.SemaphoreType.DMA((chunks,)),
         ],
         compiler_params=params(INNER_MIB),
-        cost_estimate=cost(flops, 8 * 2**20),
+        cost_estimate=cost(flops, 2**10),
         name=name,
     )(field, coeff)
 
 
-def mix(parts):
+def mix(parts, pair):
     return pl.pallas_call(
         mix_kernel,
-        in_specs=[whole()] * 4,
+        in_specs=[whole()] * 4 + [whole(pl.ANY)],
         out_specs=[whole()] * 3,
         out_shape=[f32(ROWS, LANES), f32(ROWS, LANES), f32(8, LANES)],
         compiler_params=params(8),
         cost_estimate=cost(MIX, 6 * 4 * ROWS * LANES),
         name="mix",
-    )(*parts)
+    )(*parts, pair)
 
 
 def local(basis, flux, recon, pseudo_time, vol_omega, block_ids, neighbour, orient):
@@ -604,9 +581,9 @@
     sent, padded, dense = pl.pallas_call(
         first_faces_kernel,
         in_specs=[whole(pl.ANY)],
-        out_specs=[whole(pl.ANY), whole(), whole()],
+        out_specs=[whole(pl.ANY), whole(), whole(pl.ANY)],
         out_shape=[SENT, f32(8, CELLS), f32(ROWS, LANES)],
-        scratch_shapes=[VMEM((8 * GROUPS, LANES), jnp.float32), FACES_VMEM, pltpu.SemaphoreType.DMA((PER, CHIP_COUNT))],
+        scratch_shapes=[VMEM((8 * GROUPS, LANES), jnp.float32), FACES_VMEM, pltpu.SemaphoreType.DMA((PER + 1, CHIP_COUNT))],
         compiler_params=params(8),
         cost_estimate=cost(10**6, 2 * 2**20),
         name="first_faces",
@@ -618,7 +595,7 @@
         out_specs=[whole(SMEM), whole(SMEM)],
         out_shape=[
             jax.ShapeDtypeStruct((6 * FACES,), jnp.int32),
-            jax.ShapeDtypeStruct((8 * FACES,), jnp.int32),
+            jax.ShapeDtypeStruct((6 * FACES,), jnp.int32),
         ],
         scratch_shapes=[SMEM((BLOCKS,), jnp.int32)],
         compiler_params=params(4),
@@ -626,9 +603,34 @@
         name="tables",
     )(block_ids, neighbour.T, orient.T)
     *pieces, token = inner_section(padded, flux, "flux_inner", FLUX_INNER)
+    others = [lax.ppermute(dense, "z", swap(4, k)) for k in (1, 2, 3)]
+    wanted = pl.pallas_call(
+        select_near_kernel,
+        in_specs=[whole(SMEM), whole(), whole(pl.ANY)],
+        out_specs=whole(),
+        out_shape=f32(FACES, 8, SQUARE),
+        compiler_params=params(4),
+        cost_estimate=cost(10**5, 10**6),
+        name="select_near",
+    )(table, own, token)
+    swapped = swap_cores(wanted)
+    first, faces = pl.pallas_call(
+        flux_kernel,
+        in_specs=[whole(SMEM)] + [whole()] * 6 + [whole(pl.ANY)] * 3,
+        out_specs=[whole(), whole()],
+        out_shape=[f32(8, CELLS), f32(FACES, 8, SQUARE)],
+        scratch_shapes=[FACES_VMEM],
+        compiler_params=params(OUTER_MIB),
+        cost_estimate=cost(1, 1),
+        name="flux_outer",
+    )(table, own, swapped, *pieces, *others)
+    *pieces, token = inner_section(first, recon, "recon_inner", RECON_INNER)
+    token, parts = second_exchange(faces, token)
+    kept, given, mixed = mix([dense] + others, parts[0])
+    returned = lax.ppermute(given, "xl", swap(2, 1))
     gram = pl.pallas_call(
         gram_kernel,
-        in_specs=[whole(pl.ANY)],
+        in_specs=[whole(pl.ANY)] * 2,
         out_specs=whole(),
         out_shape=f32(8, LANES),
         scratch_shapes=[
@@ -637,46 +639,22 @@
             pltpu.SemaphoreType.DMA,
         ],
         compiler_params=params(8),
-        cost_estimate=cost(2 * 36 * VARS * CELLS, 2 * 2**20),
+        cost_estimate=cost(GRAM, 2 * 2**20),
         name="gram",
-    )(flat)
-    kept, given, mixed = mix([dense] + [lax.ppermute(dense, "z", swap(4, k)) for k in (1, 2, 3)])
-    wanted = pl.pallas_call(
-        select_near_kernel,
-        in_specs=[whole(SMEM), whole(), whole(pl.ANY), whole(pl.ANY)],
-        out_specs=whole(),
-        out_shape=f32(FACES, 8, SQUARE),
-        compiler_params=params(4),
-        cost_estimate=cost(10**5, 10**6),
-        name="select_near",
-    )(table, own, token, gram)
-    swapped = swap_cores(wanted)
-    first, faces = pl.pallas_call(
-        flux_kernel,
-        in_specs=[whole(SMEM)] + [whole()] * 6 + [whole(pl.ANY)],
-        out_specs=[whole(), whole()],
-        out_shape=[f32(8, CELLS), f32(FACES, 8, SQUARE)],
-        scratch_shapes=[FACES_VMEM],
-        compiler_params=params(OUTER_MIB),
-        cost_estimate=cost(FLUX_OUTER, 4 * 2**20),
-        name="flux_outer",
-    )(table, own, swapped, *pieces, mixed)
-    returned = lax.ppermute(given, "xl", swap(2, 1))
-    *pieces, token = inner_section(first, recon, "recon_inner", RECON_INNER)
-    parts = second_exchange(faces)
+    )(flat, parts[0])
     wanted = pl.pallas_call(
         select_kernel,
-        in_specs=[whole(SMEM)] + [whole()] * 5 + [whole(pl.ANY)],
+        in_specs=[whole(SMEM)] + [whole()] * 4 + [whole(pl.ANY)] * 3,
         out_specs=whole(),
         out_shape=f32(FACES, 8, SQUARE),
         compiler_params=params(4),
         cost_estimate=cost(10**5, 10**6),
         name="select",
-    )(later, *parts, token)
+    )(later, *parts, token, mixed, gram)
     swapped = swap_cores(wanted)
     image, sums, held = pl.pallas_call(
         image_kernel,
-        in_specs=[whole(SMEM)] + [whole()] * 10 + [whole(pl.ANY)] + [whole()] * 5,
+        in_specs=[whole(SMEM)] + [whole()] * 9 + [whole(pl.ANY)] + [whole()] * 5,
         out_specs=[whole(), whole(), whole()],
         out_shape=[f32(ROWS, LANES), f32(LANES, LANES), f32(KRYLOV * ROWS, LANES)],
         scratch_shapes=[FACES_VMEM, VMEM((8 * GROUPS, LANES), jnp.float32), pltpu.SemaphoreType.DMA],

time: 71.6 us -> 70.7 us (0.987)
  starting transfers between devices: 26.7 us -> 22.9 us
  waiting for transfers between devices: 4.17 us -> 7.57 us
    ppermute x7, starting transfers between devices: 14.5 us -> 9.13 us  [the longest x3 4.42 us: local(): others = [lax.ppermute(dense, 'z', swap(4, k)) for k in (1, 2, 3)]]
    ppermute x7, waiting for transfers between devices: 2.29 us -> 4.51 us  [the longest x3 4.03 us: second_exchange(): lax.ppermute(pair, space, chip_pairs(offset))]
    ppermute x3 -> x2, starting transfers between devices: 4.24 us -> 5.92 us  [swap_cores(): return lax.ppermute(own, 'core', swap(2, 1))]
    all_to_all x1, waiting for transfers between devices: 0.01 us -> 1.19 us  [exchange(): return lax.all_to_all(sent, CHIPS, 0, 0)]
    ppermute x3 -> x2, waiting for transfers between devices: 1.88 us -> 1.87 us  [swap_cores(): return lax.ppermute(own, 'core', swap(2, 1))]
  transfers between devices with their start and end apart: 12 -> 11, of which waited for: 4 -> 6; matrix products, arithmetic and copies ran while one was open for 0% -> 0% of each run, Pallas kernels for 22% -> 19%
where the time goes in v6:
time: 70.7 us; the launch traced here: 70.5 us
  starting transfers between devices  22.9 us (32%)
  Pallas kernels  20.9 us (30%)
  blocking collectives  17.1 us (24%)
  waiting for transfers between devices  7.57 us (11%)
  between operations  0.8 us (1%)
    all_to_all x1, blocking collectives, local(): received = lax.all_to_all(sums, ALL, 0, 0)  17.1 us
    all_to_all x1, starting transfers between devices, exchange(): return lax.all_to_all(sent, CHIPS, 0, 0)  7.49 us
    pallas_call x2, Pallas kernels, inner_section(): pl.pallas_call(inner_kernel, in_specs=[whole(), whole(pltpu.HBM)], out_sp...  7.48 us
    ppermute x2, starting transfers between devices, swap_cores(): return lax.ppermute(own, 'core', swap(2, 1))  5.92 us
    ppermute x3, starting transfers between devices, local(): others = [lax.ppermute(dense, 'z', swap(4, k)) for k in (1, 2, 3)]  4.42 us
    ppermute x3, waiting for transfers between devices, second_exchange(): lax.ppermute(pair, space, chip_pairs(offset))  4.03 us
    ppermute x3, starting transfers between devices, second_exchange(): lax.ppermute(pair, space, chip_pairs(offset))  3.33 us
    pallas_call x1, Pallas kernels, local(): pl.pallas_call(first_faces_kernel, in_specs=[whole(pl.ANY)], out_specs=[w...  2.49 us
  transfers between devices with their start and end apart: 11, of which 6 were waited for; matrix products, arithmetic and copies ran while one was open for 0% of the time, Pallas kernels for 19%

profile of v6, /device:TPU:1, one launch (start us, length us, event | category | flops | bytes accessed | tf_op | source)
XLA Modules:
  0.0 70.5 jit_solution(14401374636709596023)
XLA Ops:
  0.7 2.5 %first_faces.1 = (f32[8,12,8,256]{3,2,1,0:T(8,128)}, f32[8,8192]{1,0:T(8,128)S(1)}, f32[448,128]{1,0:T(8,128)}) custom-call(f32[3584,128]{1,0:T(8,128)} %bitcast.30), custom_call_target="tpu_custom_call" | custom-call | flops 1000000 | bytes 2097152 | tf_op jit(solution)/shard_map/first_faces/pallas_call | solution.py:581
  3.2 7.5 %all-to-all-start = ((f32[8,12,8,256]{3,2,1,0:T(8,128)}), f32[8,12,8,256]{3,2,1,0:T(8,128)S(1)}, u32[]{:S(2)}, u32[]{:S(2)}) async-start(f32[8,12,8,256]{3,2,1,0:T(8,128)} %get-tuple-element.58), calls=%async_computation | async-start | bytes 1572864 | tf_op jit(solution)/shard_map/all_to_all | solution.py:526
  10.7 3.8 %collective-permute-start.3 = (f32[448,128]{1,0:T(8,128)}, f32[448,128]{1,0:T(8,128)S(1)}, u32[]{:S(2)}, u32[]{:S(2)}) collective-permute-start(f32[448,128]{1,0:T(8,128)} %get-tuple-element.65.own_ref), channel_id=1, source_target_pairs={{0,96},{32,64},{64,32},{96,0},{1,97},{33,65},{65,33},{97,1},{2,98}... | collective-permute-start | bytes 688136 | tf_op jit(solution)/shard_map/ppermute | solution.py:606
  14.4 0.7 collective-permute-start.1
  15.1 2.1 %tables.1 = (s32[72]{0:T(128)S(1)}, s32[72]{0:T(128)S(1)}) custom-call(s32[32]{0:T(128)S(1)} %copy-done.4, s32[6,32]{1,0:T(8,128)S(1)} %bitcast.28, s32[6,32]{1,0:T(8,128)S(1)} %bitcast.29), custom_call_target="tpu_custom_call" | custom-call | flops 100000 | bytes 100000 | tf_op jit(solution)/shard_map/tables/pallas_call | solution.py:592
  17.2 3.7 %flux_inner.1 = (f32[8,8192]{1,0:T(8,128)S(1)}, bf16[7,8,8192]{2,1,0:T(8,128)(2,1)S(1)}, bf16[7,8,8192]{2,1,0:T(8,128)(2,1)S(1)}, bf16[4,7,8,256]{3,2,1,0:T(8,128)(2,1)S(1)}, f32[8,128]{1,0:T(8,128)S(1)}) custom-call(f32[8,8192]{1,0:T(8,128)S(1)} %get-tuple-element.59.field_ref, bf16[1,7,7,7,8192]{4,3,2,1,0:T(8,128)(2,1)} %coeff_ref.2), custom_call_target="tpu_custom_call" | custom-call | flops 1000000 | bytes 1024 | tf_op jit(solution)/shard_map/flux_inner/pallas_call | solution.py:550
  20.9 1.2 %all-to-all-done.own_ref = f32[8,12,8,256]{3,2,1,0:T(8,128)S(1)} async-done(((f32[8,12,8,256]{3,2,1,0:T(8,128)}), f32[8,12,8,256]{3,2,1,0:T(8,128)S(1)}, u32[]{:S(2)}, u32[]{:S(2)}) %all-to-all-start) | async-done | bytes 786464 | tf_op jit(solution)/shard_map/all_to_all | solution.py:526
  22.1 0.6 select_near.1
  22.7 2.9 %collective-permute-start = (f32[12,8,256]{2,1,0:T(8,128)S(1)}, f32[12,8,256]{2,1,0:T(8,128)S(1)}, u32[]{:S(2)}, u32[]{:S(2)}) collective-permute-start(f32[12,8,256]{2,1,0:T(8,128)S(1)} %select_near.1), channel_id=1, source_target_pairs={{0,1},{1,0},{2,3},{3,2},{4,5},{5,4},{6,7},{7,6},{8,9},{9,8},{10,11... | collective-permute-start | bytes 294920 | tf_op jit(solution)/shard_map/ppermute | solution.py:541
  25.7 0.9 %collective-permute-done.swapped_ref = f32[12,8,256]{2,1,0:T(8,128)S(1)} collective-permute-done((f32[12,8,256]{2,1,0:T(8,128)S(1)}, f32[12,8,256]{2,1,0:T(8,128)S(1)}, u32[]{:S(2)}, u32[]{:S(2)}) %collective-permute-start) | collective-permute-done | bytes 98336 | tf_op jit(solution)/shard_map/ppermute | solution.py:541
  26.6 1.7 %flux_outer.1 = (f32[8,8192]{1,0:T(8,128)S(1)}, f32[12,8,256]{2,1,0:T(8,128)S(1)}) custom-call(s32[72]{0:T(128)S(1)} %get-tuple-element.57.table_ref, f32[8,12,8,256]{3,2,1,0:T(8,128)S(1)} %all-to-all-done.own_ref, f32[12,8,256]{2,1,0:T(8,128)S(1)} %collective-permute-done.swapped_ref, f32[8,8192]{1,0:T(8,128)S(1)} %get-tuple-element.61.part_ref, ...), custom_call_target="tpu_custom_call" | custom-call | flops 1 | bytes 1 | tf_op jit(solution)/shard_map/flux_outer/pallas_call | solution.py:617
  28.3 1.4 %collective-permute-start.4 = (f32[12,8,256]{2,1,0:T(8,128)S(1)}, f32[12,8,256]{2,1,0:T(8,128)S(1)}, u32[]{:S(2)}, u32[]{:S(2)}) collective-permute-start(f32[12,8,256]{2,1,0:T(8,128)S(1)} %get-tuple-element.66), channel_id=1, source_target_pairs={{0,8},{1,9},{2,10},{3,11},{4,12},{5,13},{6,14},{7,15},{8,0},{9,1},... | collective-permute-start | bytes 294920 | tf_op jit(solution)/shard_map/ppermute | solution.py:535
  29.7 3.7 %recon_inner.1 = (f32[8,8192]{1,0:T(8,128)S(1)}, bf16[7,8,8192]{2,1,0:T(8,128)(2,1)S(1)}, bf16[7,8,8192]{2,1,0:T(8,128)(2,1)S(1)}, bf16[4,7,8,256]{3,2,1,0:T(8,128)(2,1)S(1)}, f32[8,128]{1,0:T(8,128)S(1)}) custom-call(f32[8,8192]{1,0:T(8,128)S(1)} %get-tuple-element.67.field_ref, bf16[1,7,7,7,8192]{4,3,2,1,0:T(8,128)(2,1)} %coeff_ref.3), custom_call_target="tpu_custom_call" | custom-call | flops 1000000 | bytes 1024 | tf_op jit(solution)/shard_map/recon_inner/pallas_call | solution.py:550
  33.5 0.5 collective-permute-done.4
  33.9 1.8 %collective-permute-start.7 = (f32[24,8,256]{2,1,0:T(8,128)S(1)}, f32[24,8,256]{2,1,0:T(8,128)S(1)}, u32[]{:S(2)}, u32[]{:S(2)}) collective-permute-start(f32[24,8,256]{2,1,0:T(8,128)S(1)} %constant_dynamic-update-slice_fusion.pair_ref), channel_id=1, source_target_pairs={{0,6},{1,7},{2,4},{3,5},{4,2},{5,3},{6,0},{7,1},{8,14},{9,15},{10,... | collective-permute-start | bytes 589832 | tf_op jit(solution)/shard_map/ppermute | solution.py:537
  35.8 0.6 collective-permute-start.6
  36.3 0.9 %collective-permute-start.5 = (f32[24,8,256]{2,1,0:T(8,128)S(1)}, f32[24,8,256]{2,1,0:T(8,128)S(1)}, u32[]{:S(2)}, u32[]{:S(2)}) collective-permute-start(f32[24,8,256]{2,1,0:T(8,128)S(1)} %constant_dynamic-update-slice_fusion.pair_ref), channel_id=1, source_target_pairs={{0,2},{1,3},{2,0},{3,1},{4,6},{5,7},{6,4},{7,5},{8,10},{9,11},{10,... | collective-permute-start | bytes 589832 | tf_op jit(solution)/shard_map/ppermute | solution.py:537
  37.3 1.3 %mix.1 = (f32[448,128]{1,0:T(8,128)S(1)}, f32[448,128]{1,0:T(8,128)S(1)}, f32[8,128]{1,0:T(8,128)S(1)}) custom-call(f32[448,128]{1,0:T(8,128)} %get-tuple-element.65.own_ref, f32[448,128]{1,0:T(8,128)} %collective-permute-done.1.z_one_ref.one_ref, f32[448,128]{1,0:T(8,128)} %collective-permute-done.2.z_two_ref.two_ref, ...), custom_call_target="tpu_custom_call" | custom-call | flops 5000000000 | bytes 1376256 | tf_op jit(solution)/shard_map/mix/pallas_call | solution.py:568
  38.6 0.0 copy-start
  38.6 0.4 collective-permute-start.9
  39.0 1.4 %gram.1.gram_ref = f32[8,128]{1,0:T(8,128)S(1)} custom-call(f32[3584,128]{1,0:T(8,128)S(1)} %bitcast.31, f32[24,8,256]{2,1,0:T(8,128)S(1)} %constant_dynamic-update-slice_fusion.pair_ref), custom_call_target="tpu_custom_call" | custom-call | flops 1000000000 | bytes 2097152 | tf_op jit(solution)/shard_map/gram/pallas_call | solution.py:631
  40.4 1.4 %collective-permute-done.7.three_ref = f32[24,8,256]{2,1,0:T(8,128)S(1)} collective-permute-done((f32[24,8,256]{2,1,0:T(8,128)S(1)}, f32[24,8,256]{2,1,0:T(8,128)S(1)}, u32[]{:S(2)}, u32[]{:S(2)}) %collective-permute-start.7) | collective-permute-done | bytes 196640 | tf_op jit(solution)/shard_map/ppermute | solution.py:537
  41.9 0.0 collective-permute-done.6.two_ref
  41.9 2.6 %collective-permute-done.5.one_ref = f32[24,8,256]{2,1,0:T(8,128)S(1)} collective-permute-done((f32[24,8,256]{2,1,0:T(8,128)S(1)}, f32[24,8,256]{2,1,0:T(8,128)S(1)}, u32[]{:S(2)}, u32[]{:S(2)}) %collective-permute-start.5) | collective-permute-done | bytes 196640 | tf_op jit(solution)/shard_map/ppermute | solution.py:537
  44.5 0.6 select.1
  45.1 3.0 %collective-permute-start.8 = (f32[12,8,256]{2,1,0:T(8,128)S(1)}, f32[12,8,256]{2,1,0:T(8,128)S(1)}, u32[]{:S(2)}, u32[]{:S(2)}) collective-permute-start(f32[12,8,256]{2,1,0:T(8,128)S(1)} %select.1), channel_id=1, source_target_pairs={{0,1},{1,0},{2,3},{3,2},{4,5},{5,4},{6,7},{7,6},{8,9},{9,8},{10,11... | collective-permute-start | bytes 294920 | tf_op jit(solution)/shard_map/ppermute | solution.py:541
  48.1 0.9 %collective-permute-done.8.swapped_ref = f32[12,8,256]{2,1,0:T(8,128)S(1)} collective-permute-done((f32[12,8,256]{2,1,0:T(8,128)S(1)}, f32[12,8,256]{2,1,0:T(8,128)S(1)}, u32[]{:S(2)}, u32[]{:S(2)}) %collective-permute-start.8) | collective-permute-done | bytes 98336 | tf_op jit(solution)/shard_map/ppermute | solution.py:541
  49.0 1.9 %image.1 = (f32[448,128]{1,0:T(8,128)S(1)}, f32[128,128]{1,0:T(8,128)S(1)}, f32[3584,128]{1,0:T(8,128)S(1)}) custom-call(s32[72]{0:T(128)S(1)} %get-tuple-element.56.later_ref, f32[24,8,256]{2,1,0:T(8,128)S(1)} %constant_dynamic-update-slice_fusion.pair_ref, f32[24,8,256]{2,1,0:T(8,128)S(1)} %collective-permute-done.5.one_ref, ...), custom_call_target="tpu_custom_call" | custom-call | flops 1000000 | bytes 6291456 | tf_op jit(solution)/shard_map/image/pallas_call | solution.py:655
  51.0 17.1 %all_to_all.16 = f32[128,1,128]{2,1,0:T(1,128)S(1)} all-to-all(f32[128,1,128]{2,1,0:T(1,128)S(1)} %bitcast.25), channel_id=1, replica_groups=mesh['z'=4,'xl'=2,'xh'=2,'y'=4,'core'=2] {'z','xl','xh','y','core'}, dimensions={0} | all-to-all | bytes 131072 | tf_op jit(solution)/shard_map/all_to_all | solution.py:668
  68.0 1.3 %finish.1 = (f32[448,128]{1,0:T(8,128)}, f32[1,9]{1,0:T(1,128)S(1)}, s32[1]{0:T(128)}) custom-call(f32[128,128]{1,0:T(8,128)S(1)} %bitcast.24, f32[448,128]{1,0:T(8,128)S(1)} %get-tuple-element.107.image_ref, f32[3584,128]{1,0:T(8,128)S(1)} %get-tuple-element.80.basis_ref), custom_call_target="tpu_custom_call" | custom-call | flops 1000000 | bytes 3145728 | tf_op jit(solution)/shard_map/finish/pallas_call | solution.py:669
  69.3 0.7 while.11
  70.0 0.5 copy-done.6
  (19 shorter events, 0.1 us)
Async XLA Ops:
  0.6 14.4 %copy-start.3 = (s32[32,6]{0,1:T(8,128)S(1)}, s32[32,6]{0,1:T(8,128)}, u32[]{:S(2)}) copy-start(s32[32,6]{0,1:T(8,128)} %param.17) | copy-start | bytes 2308
  0.6 14.4 %copy-start.2 = (s32[32,6]{0,1:T(8,128)S(1)}, s32[32,6]{0,1:T(8,128)}, u32[]{:S(2)}) copy-start(s32[32,6]{0,1:T(8,128)} %param.16) | copy-start | bytes 2308
  0.7 14.4 %copy-start.4 = (s32[32]{0:T(128)S(1)}, s32[32]{0:T(128)}, u32[]{:S(2)}) copy-start(s32[32]{0:T(128)} %ids_ref.1) | copy-start | bytes 388
  3.2 19.0 %all-to-all-start = ((f32[8,12,8,256]{3,2,1,0:T(8,128)}), f32[8,12,8,256]{3,2,1,0:T(8,128)S(1)}, u32[]{:S(2)}, u32[]{:S(2)}) async-start(f32[8,12,8,256]{3,2,1,0:T(8,128)} %get-tuple-element.58), calls=%async_computation | async-start | bytes 1572864 | tf_op jit(solution)/shard_map/all_to_all | solution.py:526
  10.7 15.0 %collective-permute-start.3 = (f32[448,128]{1,0:T(8,128)}, f32[448,128]{1,0:T(8,128)S(1)}, u32[]{:S(2)}, u32[]{:S(2)}) collective-permute-start(f32[448,128]{1,0:T(8,128)} %get-tuple-element.65.own_ref), channel_id=1, source_target_pairs={{0,96},{32,64},{64,32},{96,0},{1,97},{33,65},{65,33},{97,1},{2,98}... | collective-permute-start | bytes 688136 | tf_op jit(solution)/shard_map/ppermute | solution.py:606
  14.4 11.2 %collective-permute-start.2 = (f32[448,128]{1,0:T(8,128)}, f32[448,128]{1,0:T(8,128)}, u32[]{:S(2)}, u32[]{:S(2)}) collective-permute-start(f32[448,128]{1,0:T(8,128)} %get-tuple-element.65.own_ref), channel_id=1, source_target_pairs={{0,64},{32,96},{64,0},{96,32},{1,65},{33,97},{65,1},{97,33},{2,66}... | collective-permute-start | bytes 688136 | tf_op jit(solution)/shard_map/ppermute | solution.py:606
  14.4 11.2 %collective-permute-start.1 = (f32[448,128]{1,0:T(8,128)}, f32[448,128]{1,0:T(8,128)}, u32[]{:S(2)}, u32[]{:S(2)}) collective-permute-start(f32[448,128]{1,0:T(8,128)} %get-tuple-element.65.own_ref), channel_id=1, source_target_pairs={{0,32},{32,0},{64,96},{96,64},{1,33},{33,1},{65,97},{97,65},{2,34}... | collective-permute-start | bytes 688136 | tf_op jit(solution)/shard_map/ppermute | solution.py:606
  22.7 3.9 %collective-permute-start = (f32[12,8,256]{2,1,0:T(8,128)S(1)}, f32[12,8,256]{2,1,0:T(8,128)S(1)}, u32[]{:S(2)}, u32[]{:S(2)}) collective-permute-start(f32[12,8,256]{2,1,0:T(8,128)S(1)} %select_near.1), channel_id=1, source_target_pairs={{0,1},{1,0},{2,3},{3,2},{4,5},{5,4},{6,7},{7,6},{8,9},{9,8},{10,11... | collective-permute-start | bytes 294920 | tf_op jit(solution)/shard_map/ppermute | solution.py:541
  28.3 5.6 %collective-permute-start.4 = (f32[12,8,256]{2,1,0:T(8,128)S(1)}, f32[12,8,256]{2,1,0:T(8,128)S(1)}, u32[]{:S(2)}, u32[]{:S(2)}) collective-permute-start(f32[12,8,256]{2,1,0:T(8,128)S(1)} %get-tuple-element.66), channel_id=1, source_target_pairs={{0,8},{1,9},{2,10},{3,11},{4,12},{5,13},{6,14},{7,15},{8,0},{9,1},... | collective-permute-start | bytes 294920 | tf_op jit(solution)/shard_map/ppermute | solution.py:535
  33.9 5.1 %copy-start.5 = (f32[8,1,7,8192]{3,1,2,0:T(1,128)S(1)}, f32[8,1,7,8192]{3,1,2,0:T(1,128)}, u32[]{:S(2)}) copy-start(f32[8,1,7,8192]{3,1,2,0:T(1,128)} %param.10) | copy-start | bytes 5505028
  33.9 7.9 %collective-permute-start.7 = (f32[24,8,256]{2,1,0:T(8,128)S(1)}, f32[24,8,256]{2,1,0:T(8,128)S(1)}, u32[]{:S(2)}, u32[]{:S(2)}) collective-permute-start(f32[24,8,256]{2,1,0:T(8,128)S(1)} %constant_dynamic-update-slice_fusion.pair_ref), channel_id=1, source_target_pairs={{0,6},{1,7},{2,4},{3,5},{4,2},{5,3},{6,0},{7,1},{8,14},{9,15},{10,... | collective-permute-start | bytes 589832 | tf_op jit(solution)/shard_map/ppermute | solution.py:537
  35.8 6.1 %collective-permute-start.6 = (f32[24,8,256]{2,1,0:T(8,128)S(1)}, f32[24,8,256]{2,1,0:T(8,128)S(1)}, u32[]{:S(2)}, u32[]{:S(2)}) collective-permute-start(f32[24,8,256]{2,1,0:T(8,128)S(1)} %constant_dynamic-update-slice_fusion.pair_ref), channel_id=1, source_target_pairs={{0,4},{1,5},{2,6},{3,7},{4,0},{5,1},{6,2},{7,3},{8,12},{9,13},{10,... | collective-permute-start | bytes 589832 | tf_op jit(solution)/shard_map/ppermute | solution.py:537
  36.3 8.1 %collective-permute-start.5 = (f32[24,8,256]{2,1,0:T(8,128)S(1)}, f32[24,8,256]{2,1,0:T(8,128)S(1)}, u32[]{:S(2)}, u32[]{:S(2)}) collective-permute-start(f32[24,8,256]{2,1,0:T(8,128)S(1)} %constant_dynamic-update-slice_fusion.pair_ref), channel_id=1, source_target_pairs={{0,2},{1,3},{2,0},{3,1},{4,6},{5,7},{6,4},{7,5},{8,10},{9,11},{10,... | collective-permute-start | bytes 589832 | tf_op jit(solution)/shard_map/ppermute | solution.py:537
  38.6 10.4 %copy-start = (f32[8192]{0:T(1024)S(1)}, f32[8192]{0:T(1024)}, u32[]{:S(2)}) copy-start(f32[8192]{0:T(1024)} %param.13) | copy-start | bytes 98308
  38.6 10.4 %copy-start.1 = (f32[8192]{0:T(1024)S(1)}, f32[8192]{0:T(1024)}, u32[]{:S(2)}) copy-start(f32[8192]{0:T(1024)} %param.14) | copy-start | bytes 98308
  38.6 9.5 %collective-permute-start.9 = (f32[448,128]{1,0:T(8,128)S(1)}, f32[448,128]{1,0:T(8,128)S(1)}, u32[]{:S(2)}, u32[]{:S(2)}) collective-permute-start(f32[448,128]{1,0:T(8,128)S(1)} %get-tuple-element.77), channel_id=1, source_target_pairs={{0,16},{16,0},{1,17},{17,1},{2,18},{18,2},{3,19},{19,3},{4,20},{20... | collective-permute-start | bytes 688136 | tf_op jit(solution)/shard_map/ppermute | solution.py:630
  45.1 3.9 %collective-permute-start.8 = (f32[12,8,256]{2,1,0:T(8,128)S(1)}, f32[12,8,256]{2,1,0:T(8,128)S(1)}, u32[]{:S(2)}, u32[]{:S(2)}) collective-permute-start(f32[12,8,256]{2,1,0:T(8,128)S(1)} %select.1), channel_id=1, source_target_pairs={{0,1},{1,0},{2,3},{3,2},{4,5},{5,4},{6,7},{7,6},{8,9},{9,8},{10,11... | collective-permute-start | bytes 294920 | tf_op jit(solution)/shard_map/ppermute | solution.py:541
  70.0 0.5 copy-start.6

commit v7 on v6

--- a/solution.py
+++ b/solution.py
@@ -534,7 +534,8 @@
     space = ("xh", "y", "core")
     other, token = lax.optimization_barrier((lax.ppermute(faces, space, chip_pairs(4)), token))
     pair = jnp.concatenate([faces, other])
-    return token, [pair] + [lax.ppermute(pair, space, chip_pairs(offset)) for offset in (1, 2, 3)]
+    one, three, two = [lax.ppermute(pair, space, chip_pairs(offset)) for offset in (1, 3, 2)]
+    return token, [pair, one, two, three]
 
 
 def swap_cores(own):

time: 70.7 us -> 70.7 us (level)
  transfers between devices with their start and end apart: 11 -> 11, of which waited for: 6 -> 7; matrix products, arithmetic and copies ran while one was open for 0% -> 0% of each run, Pallas kernels for 19% -> 19%
where the time goes in v7:
time: 70.7 us; the launch traced here: 70.5 us
  starting transfers between devices  22.9 us (32%)
  Pallas kernels  20.9 us (30%)
  blocking collectives  17.1 us (24%)
  waiting for transfers between devices  7.58 us (11%)
  between operations  0.8 us (1%)
    all_to_all x1, blocking collectives, local(): received = lax.all_to_all(sums, ALL, 0, 0)  17.1 us
    all_to_all x1, starting transfers between devices, exchange(): return lax.all_to_all(sent, CHIPS, 0, 0)  7.49 us
    pallas_call x2, Pallas kernels, inner_section(): pl.pallas_call(inner_kernel, in_specs=[whole(), whole(pltpu.HBM)], out_sp...  7.48 us
    ppermute x2, starting transfers between devices, swap_cores(): return lax.ppermute(own, 'core', swap(2, 1))  5.92 us
    ppermute x3, starting transfers between devices, local(): others = [lax.ppermute(dense, 'z', swap(4, k)) for k in (1, 2, 3)]  4.42 us
    ppermute x3, waiting for transfers between devices, second_exchange(): lax.ppermute(pair, space, chip_pairs(offset))  4.04 us
    ppermute x3, starting transfers between devices, second_exchange(): lax.ppermute(pair, space, chip_pairs(offset))  3.33 us
    pallas_call x1, Pallas kernels, local(): pl.pallas_call(first_faces_kernel, in_specs=[whole(pl.ANY)], out_specs=[w...  2.49 us
  transfers between devices with their start and end apart: 11, of which 7 were waited for; matrix products, arithmetic and copies ran while one was open for 0% of the time, Pallas kernels for 19%

profile of v7, /device:TPU:1, one launch (start us, length us, event | category | flops | bytes accessed | tf_op | source)
XLA Modules:
  0.0 70.5 jit_solution(14401374636709596023)
XLA Ops:
  0.7 2.5 %first_faces.1 = (f32[8,12,8,256]{3,2,1,0:T(8,128)}, f32[8,8192]{1,0:T(8,128)S(1)}, f32[448,128]{1,0:T(8,128)}) custom-call(f32[3584,128]{1,0:T(8,128)} %bitcast.30), custom_call_target="tpu_custom_call" | custom-call | flops 1000000 | bytes 2097152 | tf_op jit(solution)/shard_map/first_faces/pallas_call | solution.py:582
  3.2 7.5 %all-to-all-start = ((f32[8,12,8,256]{3,2,1,0:T(8,128)}), f32[8,12,8,256]{3,2,1,0:T(8,128)S(1)}, u32[]{:S(2)}, u32[]{:S(2)}) async-start(f32[8,12,8,256]{3,2,1,0:T(8,128)} %get-tuple-element.58), calls=%async_computation | async-start | bytes 1572864 | tf_op jit(solution)/shard_map/all_to_all | solution.py:526
  10.7 3.8 %collective-permute-start.3 = (f32[448,128]{1,0:T(8,128)}, f32[448,128]{1,0:T(8,128)S(1)}, u32[]{:S(2)}, u32[]{:S(2)}) collective-permute-start(f32[448,128]{1,0:T(8,128)} %get-tuple-element.65.own_ref), channel_id=1, source_target_pairs={{0,96},{32,64},{64,32},{96,0},{1,97},{33,65},{65,33},{97,1},{2,98}... | collective-permute-start | bytes 688136 | tf_op jit(solution)/shard_map/ppermute | solution.py:607
  14.4 0.7 collective-permute-start.1
  15.1 2.1 %tables.1 = (s32[72]{0:T(128)S(1)}, s32[72]{0:T(128)S(1)}) custom-call(s32[32]{0:T(128)S(1)} %copy-done.4, s32[6,32]{1,0:T(8,128)S(1)} %bitcast.28, s32[6,32]{1,0:T(8,128)S(1)} %bitcast.29), custom_call_target="tpu_custom_call" | custom-call | flops 100000 | bytes 100000 | tf_op jit(solution)/shard_map/tables/pallas_call | solution.py:593
  17.2 3.7 %flux_inner.1 = (f32[8,8192]{1,0:T(8,128)S(1)}, bf16[7,8,8192]{2,1,0:T(8,128)(2,1)S(1)}, bf16[7,8,8192]{2,1,0:T(8,128)(2,1)S(1)}, bf16[4,7,8,256]{3,2,1,0:T(8,128)(2,1)S(1)}, f32[8,128]{1,0:T(8,128)S(1)}) custom-call(f32[8,8192]{1,0:T(8,128)S(1)} %get-tuple-element.59.field_ref, bf16[1,7,7,7,8192]{4,3,2,1,0:T(8,128)(2,1)} %coeff_ref.2), custom_call_target="tpu_custom_call" | custom-call | flops 1000000 | bytes 1024 | tf_op jit(solution)/shard_map/flux_inner/pallas_call | solution.py:551
  20.9 1.2 %all-to-all-done.own_ref = f32[8,12,8,256]{3,2,1,0:T(8,128)S(1)} async-done(((f32[8,12,8,256]{3,2,1,0:T(8,128)}), f32[8,12,8,256]{3,2,1,0:T(8,128)S(1)}, u32[]{:S(2)}, u32[]{:S(2)}) %all-to-all-start) | async-done | bytes 786464 | tf_op jit(solution)/shard_map/all_to_all | solution.py:526
  22.1 0.6 select_near.1
  22.7 2.9 %collective-permute-start = (f32[12,8,256]{2,1,0:T(8,128)S(1)}, f32[12,8,256]{2,1,0:T(8,128)S(1)}, u32[]{:S(2)}, u32[]{:S(2)}) collective-permute-start(f32[12,8,256]{2,1,0:T(8,128)S(1)} %select_near.1), channel_id=1, source_target_pairs={{0,1},{1,0},{2,3},{3,2},{4,5},{5,4},{6,7},{7,6},{8,9},{9,8},{10,11... | collective-permute-start | bytes 294920 | tf_op jit(solution)/shard_map/ppermute | solution.py:542
  25.7 0.9 %collective-permute-done.swapped_ref = f32[12,8,256]{2,1,0:T(8,128)S(1)} collective-permute-done((f32[12,8,256]{2,1,0:T(8,128)S(1)}, f32[12,8,256]{2,1,0:T(8,128)S(1)}, u32[]{:S(2)}, u32[]{:S(2)}) %collective-permute-start) | collective-permute-done | bytes 98336 | tf_op jit(solution)/shard_map/ppermute | solution.py:542
  26.6 1.7 %flux_outer.1 = (f32[8,8192]{1,0:T(8,128)S(1)}, f32[12,8,256]{2,1,0:T(8,128)S(1)}) custom-call(s32[72]{0:T(128)S(1)} %get-tuple-element.57.table_ref, f32[8,12,8,256]{3,2,1,0:T(8,128)S(1)} %all-to-all-done.own_ref, f32[12,8,256]{2,1,0:T(8,128)S(1)} %collective-permute-done.swapped_ref, f32[8,8192]{1,0:T(8,128)S(1)} %get-tuple-element.61.part_ref, ...), custom_call_target="tpu_custom_call" | custom-call | flops 1 | bytes 1 | tf_op jit(solution)/shard_map/flux_outer/pallas_call | solution.py:618
  28.3 1.4 %collective-permute-start.4 = (f32[12,8,256]{2,1,0:T(8,128)S(1)}, f32[12,8,256]{2,1,0:T(8,128)S(1)}, u32[]{:S(2)}, u32[]{:S(2)}) collective-permute-start(f32[12,8,256]{2,1,0:T(8,128)S(1)} %get-tuple-element.66), channel_id=1, source_target_pairs={{0,8},{1,9},{2,10},{3,11},{4,12},{5,13},{6,14},{7,15},{8,0},{9,1},... | collective-permute-start | bytes 294920 | tf_op jit(solution)/shard_map/ppermute | solution.py:535
  29.7 3.7 %recon_inner.1 = (f32[8,8192]{1,0:T(8,128)S(1)}, bf16[7,8,8192]{2,1,0:T(8,128)(2,1)S(1)}, bf16[7,8,8192]{2,1,0:T(8,128)(2,1)S(1)}, bf16[4,7,8,256]{3,2,1,0:T(8,128)(2,1)S(1)}, f32[8,128]{1,0:T(8,128)S(1)}) custom-call(f32[8,8192]{1,0:T(8,128)S(1)} %get-tuple-element.67.field_ref, bf16[1,7,7,7,8192]{4,3,2,1,0:T(8,128)(2,1)} %coeff_ref.3), custom_call_target="tpu_custom_call" | custom-call | flops 1000000 | bytes 1024 | tf_op jit(solution)/shard_map/recon_inner/pallas_call | solution.py:551
  33.5 0.5 collective-permute-done.4
  33.9 1.8 %collective-permute-start.7 = (f32[24,8,256]{2,1,0:T(8,128)S(1)}, f32[24,8,256]{2,1,0:T(8,128)S(1)}, u32[]{:S(2)}, u32[]{:S(2)}) collective-permute-start(f32[24,8,256]{2,1,0:T(8,128)S(1)} %constant_dynamic-update-slice_fusion.pair_ref), channel_id=1, source_target_pairs={{0,6},{1,7},{2,4},{3,5},{4,2},{5,3},{6,0},{7,1},{8,14},{9,15},{10,... | collective-permute-start | bytes 589832 | tf_op jit(solution)/shard_map/ppermute | solution.py:537
  35.8 0.6 collective-permute-start.6
  36.3 0.9 %collective-permute-start.5 = (f32[24,8,256]{2,1,0:T(8,128)S(1)}, f32[24,8,256]{2,1,0:T(8,128)S(1)}, u32[]{:S(2)}, u32[]{:S(2)}) collective-permute-start(f32[24,8,256]{2,1,0:T(8,128)S(1)} %constant_dynamic-update-slice_fusion.pair_ref), channel_id=1, source_target_pairs={{0,2},{1,3},{2,0},{3,1},{4,6},{5,7},{6,4},{7,5},{8,10},{9,11},{10,... | collective-permute-start | bytes 589832 | tf_op jit(solution)/shard_map/ppermute | solution.py:537
  37.3 1.3 %mix.1 = (f32[448,128]{1,0:T(8,128)S(1)}, f32[448,128]{1,0:T(8,128)S(1)}, f32[8,128]{1,0:T(8,128)S(1)}) custom-call(f32[448,128]{1,0:T(8,128)} %get-tuple-element.65.own_ref, f32[448,128]{1,0:T(8,128)} %collective-permute-done.1.z_one_ref.one_ref, f32[448,128]{1,0:T(8,128)} %collective-permute-done.2.z_two_ref.two_ref, ...), custom_call_target="tpu_custom_call" | custom-call | flops 5000000000 | bytes 1376256 | tf_op jit(solution)/shard_map/mix/pallas_call | solution.py:569
  38.6 0.4 collective-permute-start.9
  39.0 1.4 %gram.1.gram_ref = f32[8,128]{1,0:T(8,128)S(1)} custom-call(f32[3584,128]{1,0:T(8,128)S(1)} %bitcast.31, f32[24,8,256]{2,1,0:T(8,128)S(1)} %constant_dynamic-update-slice_fusion.pair_ref), custom_call_target="tpu_custom_call" | custom-call | flops 1000000000 | bytes 2097152 | tf_op jit(solution)/shard_map/gram/pallas_call | solution.py:632
  40.5 1.4 %collective-permute-done.7.three_ref = f32[24,8,256]{2,1,0:T(8,128)S(1)} collective-permute-done((f32[24,8,256]{2,1,0:T(8,128)S(1)}, f32[24,8,256]{2,1,0:T(8,128)S(1)}, u32[]{:S(2)}, u32[]{:S(2)}) %collective-permute-start.7) | collective-permute-done | bytes 196640 | tf_op jit(solution)/shard_map/ppermute | solution.py:537
  41.8 0.1 collective-permute-done.6.two_ref
  41.9 2.6 %collective-permute-done.5.one_ref = f32[24,8,256]{2,1,0:T(8,128)S(1)} collective-permute-done((f32[24,8,256]{2,1,0:T(8,128)S(1)}, f32[24,8,256]{2,1,0:T(8,128)S(1)}, u32[]{:S(2)}, u32[]{:S(2)}) %collective-permute-start.5) | collective-permute-done | bytes 196640 | tf_op jit(solution)/shard_map/ppermute | solution.py:537
  44.5 0.6 select.1
  45.1 3.0 %collective-permute-start.8 = (f32[12,8,256]{2,1,0:T(8,128)S(1)}, f32[12,8,256]{2,1,0:T(8,128)S(1)}, u32[]{:S(2)}, u32[]{:S(2)}) collective-permute-start(f32[12,8,256]{2,1,0:T(8,128)S(1)} %select.1), channel_id=1, source_target_pairs={{0,1},{1,0},{2,3},{3,2},{4,5},{5,4},{6,7},{7,6},{8,9},{9,8},{10,11... | collective-permute-start | bytes 294920 | tf_op jit(solution)/shard_map/ppermute | solution.py:542
  48.1 0.9 %collective-permute-done.8.swapped_ref = f32[12,8,256]{2,1,0:T(8,128)S(1)} collective-permute-done((f32[12,8,256]{2,1,0:T(8,128)S(1)}, f32[12,8,256]{2,1,0:T(8,128)S(1)}, u32[]{:S(2)}, u32[]{:S(2)}) %collective-permute-start.8) | collective-permute-done | bytes 98336 | tf_op jit(solution)/shard_map/ppermute | solution.py:542
  49.0 1.9 %image.1 = (f32[448,128]{1,0:T(8,128)S(1)}, f32[128,128]{1,0:T(8,128)S(1)}, f32[3584,128]{1,0:T(8,128)S(1)}) custom-call(s32[72]{0:T(128)S(1)} %get-tuple-element.56.later_ref, f32[24,8,256]{2,1,0:T(8,128)S(1)} %constant_dynamic-update-slice_fusion.pair_ref, f32[24,8,256]{2,1,0:T(8,128)S(1)} %collective-permute-done.5.one_ref, ...), custom_call_target="tpu_custom_call" | custom-call | flops 1000000 | bytes 6291456 | tf_op jit(solution)/shard_map/image/pallas_call | solution.py:656
  51.0 17.1 %all_to_all.16 = f32[128,1,128]{2,1,0:T(1,128)S(1)} all-to-all(f32[128,1,128]{2,1,0:T(1,128)S(1)} %bitcast.25), channel_id=1, replica_groups=mesh['z'=4,'xl'=2,'xh'=2,'y'=4,'core'=2] {'z','xl','xh','y','core'}, dimensions={0} | all-to-all | bytes 131072 | tf_op jit(solution)/shard_map/all_to_all | solution.py:669
  68.0 1.3 %finish.1 = (f32[448,128]{1,0:T(8,128)}, f32[1,9]{1,0:T(1,128)S(1)}, s32[1]{0:T(128)}) custom-call(f32[128,128]{1,0:T(8,128)S(1)} %bitcast.24, f32[448,128]{1,0:T(8,128)S(1)} %get-tuple-element.107.image_ref, f32[3584,128]{1,0:T(8,128)S(1)} %get-tuple-element.80.basis_ref), custom_call_target="tpu_custom_call" | custom-call | flops 1000000 | bytes 3145728 | tf_op jit(solution)/shard_map/finish/pallas_call | solution.py:670
  69.3 0.7 while.11
  70.0 0.0 copy-start.6
  70.0 0.5 copy-done.6
  (19 shorter events, 0.1 us)
Async XLA Ops:
  0.6 14.4 %copy-start.3 = (s32[32,6]{0,1:T(8,128)S(1)}, s32[32,6]{0,1:T(8,128)}, u32[]{:S(2)}) copy-start(s32[32,6]{0,1:T(8,128)} %param.17) | copy-start | bytes 2308
  0.6 14.4 %copy-start.2 = (s32[32,6]{0,1:T(8,128)S(1)}, s32[32,6]{0,1:T(8,128)}, u32[]{:S(2)}) copy-start(s32[32,6]{0,1:T(8,128)} %param.16) | copy-start | bytes 2308
  0.7 14.4 %copy-start.4 = (s32[32]{0:T(128)S(1)}, s32[32]{0:T(128)}, u32[]{:S(2)}) copy-start(s32[32]{0:T(128)} %ids_ref.1) | copy-start | bytes 388
  3.2 19.0 %all-to-all-start = ((f32[8,12,8,256]{3,2,1,0:T(8,128)}), f32[8,12,8,256]{3,2,1,0:T(8,128)S(1)}, u32[]{:S(2)}, u32[]{:S(2)}) async-start(f32[8,12,8,256]{3,2,1,0:T(8,128)} %get-tuple-element.58), calls=%async_computation | async-start | bytes 1572864 | tf_op jit(solution)/shard_map/all_to_all | solution.py:526
  10.7 15.0 %collective-permute-start.3 = (f32[448,128]{1,0:T(8,128)}, f32[448,128]{1,0:T(8,128)S(1)}, u32[]{:S(2)}, u32[]{:S(2)}) collective-permute-start(f32[448,128]{1,0:T(8,128)} %get-tuple-element.65.own_ref), channel_id=1, source_target_pairs={{0,96},{32,64},{64,32},{96,0},{1,97},{33,65},{65,33},{97,1},{2,98}... | collective-permute-start | bytes 688136 | tf_op jit(solution)/shard_map/ppermute | solution.py:607
  14.4 11.2 %collective-permute-start.2 = (f32[448,128]{1,0:T(8,128)}, f32[448,128]{1,0:T(8,128)}, u32[]{:S(2)}, u32[]{:S(2)}) collective-permute-start(f32[448,128]{1,0:T(8,128)} %get-tuple-element.65.own_ref), channel_id=1, source_target_pairs={{0,64},{32,96},{64,0},{96,32},{1,65},{33,97},{65,1},{97,33},{2,66}... | collective-permute-start | bytes 688136 | tf_op jit(solution)/shard_map/ppermute | solution.py:607
  14.4 11.2 %collective-permute-start.1 = (f32[448,128]{1,0:T(8,128)}, f32[448,128]{1,0:T(8,128)}, u32[]{:S(2)}, u32[]{:S(2)}) collective-permute-start(f32[448,128]{1,0:T(8,128)} %get-tuple-element.65.own_ref), channel_id=1, source_target_pairs={{0,32},{32,0},{64,96},{96,64},{1,33},{33,1},{65,97},{97,65},{2,34}... | collective-permute-start | bytes 688136 | tf_op jit(solution)/shard_map/ppermute | solution.py:607
  22.7 3.9 %collective-permute-start = (f32[12,8,256]{2,1,0:T(8,128)S(1)}, f32[12,8,256]{2,1,0:T(8,128)S(1)}, u32[]{:S(2)}, u32[]{:S(2)}) collective-permute-start(f32[12,8,256]{2,1,0:T(8,128)S(1)} %select_near.1), channel_id=1, source_target_pairs={{0,1},{1,0},{2,3},{3,2},{4,5},{5,4},{6,7},{7,6},{8,9},{9,8},{10,11... | collective-permute-start | bytes 294920 | tf_op jit(solution)/shard_map/ppermute | solution.py:542
  28.3 5.6 %collective-permute-start.4 = (f32[12,8,256]{2,1,0:T(8,128)S(1)}, f32[12,8,256]{2,1,0:T(8,128)S(1)}, u32[]{:S(2)}, u32[]{:S(2)}) collective-permute-start(f32[12,8,256]{2,1,0:T(8,128)S(1)} %get-tuple-element.66), channel_id=1, source_target_pairs={{0,8},{1,9},{2,10},{3,11},{4,12},{5,13},{6,14},{7,15},{8,0},{9,1},... | collective-permute-start | bytes 294920 | tf_op jit(solution)/shard_map/ppermute | solution.py:535
  33.9 5.1 %copy-start.5 = (f32[8,1,7,8192]{3,1,2,0:T(1,128)S(1)}, f32[8,1,7,8192]{3,1,2,0:T(1,128)}, u32[]{:S(2)}) copy-start(f32[8,1,7,8192]{3,1,2,0:T(1,128)} %param.10) | copy-start | bytes 5505028
  33.9 7.9 %collective-permute-start.7 = (f32[24,8,256]{2,1,0:T(8,128)S(1)}, f32[24,8,256]{2,1,0:T(8,128)S(1)}, u32[]{:S(2)}, u32[]{:S(2)}) collective-permute-start(f32[24,8,256]{2,1,0:T(8,128)S(1)} %constant_dynamic-update-slice_fusion.pair_ref), channel_id=1, source_target_pairs={{0,6},{1,7},{2,4},{3,5},{4,2},{5,3},{6,0},{7,1},{8,14},{9,15},{10,... | collective-permute-start | bytes 589832 | tf_op jit(solution)/shard_map/ppermute | solution.py:537
  35.8 6.1 %collective-permute-start.6 = (f32[24,8,256]{2,1,0:T(8,128)S(1)}, f32[24,8,256]{2,1,0:T(8,128)S(1)}, u32[]{:S(2)}, u32[]{:S(2)}) collective-permute-start(f32[24,8,256]{2,1,0:T(8,128)S(1)} %constant_dynamic-update-slice_fusion.pair_ref), channel_id=1, source_target_pairs={{0,4},{1,5},{2,6},{3,7},{4,0},{5,1},{6,2},{7,3},{8,12},{9,13},{10,... | collective-permute-start | bytes 589832 | tf_op jit(solution)/shard_map/ppermute | solution.py:537
  36.3 8.2 %collective-permute-start.5 = (f32[24,8,256]{2,1,0:T(8,128)S(1)}, f32[24,8,256]{2,1,0:T(8,128)S(1)}, u32[]{:S(2)}, u32[]{:S(2)}) collective-permute-start(f32[24,8,256]{2,1,0:T(8,128)S(1)} %constant_dynamic-update-slice_fusion.pair_ref), channel_id=1, source_target_pairs={{0,2},{1,3},{2,0},{3,1},{4,6},{5,7},{6,4},{7,5},{8,10},{9,11},{10,... | collective-permute-start | bytes 589832 | tf_op jit(solution)/shard_map/ppermute | solution.py:537
  38.6 10.4 %copy-start = (f32[8192]{0:T(1024)S(1)}, f32[8192]{0:T(1024)}, u32[]{:S(2)}) copy-start(f32[8192]{0:T(1024)} %param.13) | copy-start | bytes 98308
  38.6 10.4 %copy-start.1 = (f32[8192]{0:T(1024)S(1)}, f32[8192]{0:T(1024)}, u32[]{:S(2)}) copy-start(f32[8192]{0:T(1024)} %param.14) | copy-start | bytes 98308
  38.6 9.5 %collective-permute-start.9 = (f32[448,128]{1,0:T(8,128)S(1)}, f32[448,128]{1,0:T(8,128)S(1)}, u32[]{:S(2)}, u32[]{:S(2)}) collective-permute-start(f32[448,128]{1,0:T(8,128)S(1)} %get-tuple-element.77), channel_id=1, source_target_pairs={{0,16},{16,0},{1,17},{17,1},{2,18},{18,2},{3,19},{19,3},{4,20},{20... | collective-permute-start | bytes 688136 | tf_op jit(solution)/shard_map/ppermute | solution.py:631
  45.1 3.9 %collective-permute-start.8 = (f32[12,8,256]{2,1,0:T(8,128)S(1)}, f32[12,8,256]{2,1,0:T(8,128)S(1)}, u32[]{:S(2)}, u32[]{:S(2)}) collective-permute-start(f32[12,8,256]{2,1,0:T(8,128)S(1)} %select.1), channel_id=1, source_target_pairs={{0,1},{1,0},{2,3},{3,2},{4,5},{5,4},{6,7},{7,6},{8,9},{9,8},{10,11... | collective-permute-start | bytes 294920 | tf_op jit(solution)/shard_map/ppermute | solution.py:542
  70.0 0.5 copy-start.6
